TPU v7x, 32 devices: a whole 2x2x4 slice. The times are simulated.
32 devices in a mesh: row: 8 (over y, x, core), col: 4 (over z).
Axes of the slice: x: 2, y: 2, z: 4, core: 2. Of those that a mesh axis runs over, the one named last changes fastest.
Arguments:
- kernel_tiles: float32 [8, 4, 9, 256, 512], P('row', 'col'), may hold values from -0.09375 to 0.09375
- footprints: int32 [8, 4, 9], P('row', 'col'), may hold values from 0 to 8, as said below
- counts: int32 [8, 4], P('row', 'col'), may hold values from 64 to 256, as said below
- readings: float32 [8, 4, 256], P('row', 'col'), may hold values from -6 to 6
- damping: float32 [1], replicated, may hold values from 0.1 to 0.5
- layer_depth: float32 [2], replicated, may hold values from 1 to 6
- inclinations: float32 [2], replicated, may hold values from 0.6 to 1.3
- declinations: float32 [2], replicated, may hold values from -3.140625 to 3.140625
- resid_grid: float32 [2048, 1024], P('col', 'row'), may hold values from -3 to 3
Outputs:
- coefficients: float32 [8, 4, 512], P('row', 'col')
- rtp_map: float32 [2048, 1024], P(('row', 'col'))
Inputs may be any that keep to these rules, and one draw needn't show every extreme that they name: `footprints`: each tile's list holds each of the 9 codes once; code 3 (a + 1) + (b + 1) names the source block a tiles north and b tiles east of the tile; blocks outside the survey are empty. `counts`: reading slots from this count on are ignored.
All inputs are finite; a program needn't handle non-finite values.
Results may differ from a plain program's by a relative error of at most 0.0003.
Values sent between devices are 32-bit elements; how exact they have to be, the bound alone decides.
No kernel may reach another device: no remote copies, remote signals or barrier semaphores. Data moves between devices by JAX's collectives and lax.ppermute only.
A program may use at most 128 MiB of HBM per device.

v0:
```python
import math

import jax
import jax.numpy as jnp
from jax import lax
from jax.sharding import PartitionSpec as P

SRC_ROWS = 8
SRC_COLS = 32
LAYERS = 2
REFINE = 16
INNER_LEN = 128
FOOTPRINT = 9
CG_STEPS = 2


HIGHEST_PRECISION = lax.Precision.HIGHEST
NEIGHBOUR_OFFSETS = tuple(
    ((north_step, east_step) for north_step in (-1, 0, 1) for east_step in (-1, 0, 1))
)


def shifted(x, axis, by):
    peers = lax.axis_size(axis)
    pairs = [(i, i + by) for i in range(peers) if 0 <= i + by < peers]
    return lax.ppermute(x, axis, pairs)


def hat_table(fine_start, fine_count, coarse_start, coarse_count):
    fine_pos = jnp.arange(fine_count, dtype=jnp.float32) + fine_start
    coarse_pos = jnp.arange(coarse_count, dtype=jnp.float32) + coarse_start
    offset = (fine_pos[:, None] + 0.5) / REFINE - 0.5 - coarse_pos[None, :]
    return jnp.maximum(0.0, 1.0 - jnp.abs(offset))


def frequency_of(positions, full_len):
    signed = jnp.where(positions < full_len // 2, positions, positions - full_len)
    return signed.astype(jnp.float32) / full_len


def pole_filter(north_freq, east_freq, inclinations, declinations):
    radius = jnp.sqrt(north_freq * north_freq + east_freq * east_freq)
    safe_radius = jnp.where(radius > 0.0, radius, 1.0)
    unit_north = jnp.where(radius > 0.0, north_freq / safe_radius, 0.0)
    unit_east = jnp.where(radius > 0.0, east_freq / safe_radius, 0.0)
    real_part = jnp.ones_like(radius)
    imag_part = jnp.zeros_like(radius)
    for member in range(2):
        vertical = jnp.sin(inclinations[member])
        horizontal = jnp.cos(inclinations[member])
        along_axis = horizontal * (
            jnp.cos(declinations[member]) * unit_north + jnp.sin(declinations[member]) * unit_east
        )
        denominator = vertical * vertical + along_axis * along_axis
        inv_real = vertical / denominator
        inv_imag = -along_axis / denominator
        real_part, imag_part = (
            real_part * inv_real - imag_part * inv_imag,
            real_part * inv_imag + imag_part * inv_real,
        )
    return (real_part, imag_part)


def phase_table(row_len, col_len, period, direction_sign):
    product = (
        jnp.arange(row_len, dtype=jnp.int32)[:, None]
        * jnp.arange(col_len, dtype=jnp.int32)[None, :]
        % period
    )
    angle = 2.0 * math.pi / period * product.astype(jnp.float32)
    return (jnp.cos(angle), direction_sign * jnp.sin(angle))


def transform_last(real_in, imag_in, direction_sign):
    dims_in = real_in.shape
    length = dims_in[-1]
    outer_len = length // INNER_LEN
    real_blocks = real_in.reshape(-1, outer_len, INNER_LEN)
    cos_outer, sin_outer = phase_table(outer_len, outer_len, outer_len, direction_sign)
    first_real = jnp.einsum("man,ak->mkn", real_blocks, cos_outer, precision=HIGHEST_PRECISION)
    first_imag = jnp.einsum("man,ak->mkn", real_blocks, sin_outer, precision=HIGHEST_PRECISION)
    if imag_in is not None:
        imag_blocks = imag_in.reshape(-1, outer_len, INNER_LEN)
        first_real = first_real - jnp.einsum(
            "man,ak->mkn", imag_blocks, sin_outer, precision=HIGHEST_PRECISION
        )
        first_imag = first_imag + jnp.einsum(
            "man,ak->mkn", imag_blocks, cos_outer, precision=HIGHEST_PRECISION
        )
    twist_cos, twist_sin = phase_table(outer_len, INNER_LEN, length, direction_sign)
    turned_real = first_real * twist_cos - first_imag * twist_sin
    turned_imag = first_real * twist_sin + first_imag * twist_cos
    cos_inner, sin_inner = phase_table(INNER_LEN, INNER_LEN, INNER_LEN, direction_sign)
    final_real = jnp.einsum(
        "mkn,nj->mjk", turned_real, cos_inner, precision=HIGHEST_PRECISION
    ) - jnp.einsum("mkn,nj->mjk", turned_imag, sin_inner, precision=HIGHEST_PRECISION)
    final_imag = jnp.einsum(
        "mkn,nj->mjk", turned_real, sin_inner, precision=HIGHEST_PRECISION
    ) + jnp.einsum("mkn,nj->mjk", turned_imag, cos_inner, precision=HIGHEST_PRECISION)
    return (final_real.reshape(dims_in), final_imag.reshape(dims_in))


def neighbour_block(values, step_by, keep_mask):
    arrived = shifted(values, ("row", "col"), step_by)
    return jnp.where(keep_mask, arrived, 0.0)


def collect_blocks(own_block, col_count, col_index):
    pieces = []
    for north_step, east_step in NEIGHBOUR_OFFSETS:
        if north_step == 0 and east_step == 0:
            pieces.append(own_block)
        else:
            source_col = col_index + east_step
            keep_mask = (source_col >= 0) & (source_col < col_count)
            pieces.append(
                neighbour_block(own_block, -(north_step * col_count + east_step), keep_mask)
            )
    return jnp.stack(pieces)


def return_blocks(spread, col_count, col_index):
    summed = spread[4]
    for position, (north_step, east_step) in enumerate(NEIGHBOUR_OFFSETS):
        if north_step != 0 or east_step != 0:
            source_col = col_index - east_step
            keep_mask = (source_col >= 0) & (source_col < col_count)
            summed = summed + neighbour_block(
                spread[position], north_step * col_count + east_step, keep_mask
            )
    return summed


def local_coarse(solution, col_count, col_index):
    final_blocks = collect_blocks(solution, col_count, col_index)
    coarse = final_blocks.reshape(3, 3, LAYERS, SRC_ROWS, SRC_COLS).transpose(2, 0, 3, 1, 4)
    return coarse.reshape(LAYERS, 3 * SRC_ROWS, 3 * SRC_COLS)


def two_products(residual, applied):
    return lax.psum((jnp.sum(residual * residual), jnp.sum(residual * applied)), ("row", "col"))


def on_device(
    kernel_tiles,
    footprints,
    counts,
    readings,
    damping,
    layer_depth,
    inclinations,
    declinations,
    resid_grid,
):
    col_count = lax.axis_size("col")
    row_count = lax.axis_size("row")
    col_index = lax.axis_index("col")
    row_index = lax.axis_index("row")
    kernels = kernel_tiles[0, 0]
    selector = (
        footprints[0, 0][:, None] == jnp.arange(FOOTPRINT, dtype=jnp.int32)[None, :]
    ).astype(jnp.float32)
    live_mask = (jnp.arange(kernels.shape[1], dtype=jnp.int32) < counts[0, 0]).astype(jnp.float32)
    ridge_weight = damping[0]

    def forward(vector):
        blocks = collect_blocks(vector, col_count, col_index)
        chosen = jnp.dot(selector, blocks, precision=HIGHEST_PRECISION)
        return live_mask * jnp.einsum("krs,ks->r", kernels, chosen, precision=HIGHEST_PRECISION)

    def adjoint(values):
        partial_sums = jnp.einsum(
            "krs,r->ks", kernels, live_mask * values, precision=HIGHEST_PRECISION
        )
        spread = jnp.dot(selector.T, partial_sums, precision=HIGHEST_PRECISION)
        return return_blocks(spread, col_count, col_index)

    def operate(vector):
        return adjoint(forward(vector)) + ridge_weight * vector

    right_side = adjoint(readings[0, 0])
    solution = jnp.zeros_like(right_side)
    residual = right_side
    applied = operate(residual)
    norm_now, product = two_products(residual, applied)
    step_size = norm_now / product
    direction, along_dir = (residual, applied)
    for iteration in range(CG_STEPS):
        solution = solution + step_size * direction
        residual = residual - step_size * along_dir
        if iteration + 1 < CG_STEPS:
            applied = operate(residual)
            norm_next, product = two_products(residual, applied)
            beta_ratio = norm_next / norm_now
            step_size = norm_next / (product - beta_ratio * norm_next / step_size)
            direction = residual + beta_ratio * direction
            along_dir = applied + beta_ratio * along_dir
            norm_now = norm_next
    tile_east, tile_north = resid_grid.shape
    slab_rows = tile_north // col_count
    model_spectra = None
    coarse = local_coarse(solution, col_count, col_index)
    up_north = hat_table(0.0, tile_north, -float(SRC_ROWS), 3 * SRC_ROWS)
    up_east = hat_table(0.0, tile_east, -float(SRC_COLS), 3 * SRC_COLS)
    eastward = jnp.einsum("lgh,vh->lgv", coarse, up_east, precision=HIGHEST_PRECISION)
    model_planes = jnp.einsum("lgv,ug->lvu", eastward, up_north, precision=HIGHEST_PRECISION)
    tile_planes = jnp.concatenate([model_planes, resid_grid[None]], axis=0)
    planes = lax.all_to_all(tile_planes, "row", split_axis=1, concat_axis=2, tiled=True)
    full_north = planes.shape[-1]
    north_real, north_imag = transform_last(planes, None, -1.0)
    spectra = jnp.stack([north_real, north_imag])
    slab = lax.all_to_all(
        lax.all_to_all(spectra, "row", split_axis=3, concat_axis=2, tiled=True),
        "col",
        split_axis=3,
        concat_axis=2,
        tiled=True,
    )
    slab = jnp.swapaxes(slab, 2, 3)
    full_east = slab.shape[3]
    east_real, east_imag = transform_last(slab[0], slab[1], -1.0)
    north_index = (
        row_index * tile_north + col_index * slab_rows + jnp.arange(slab_rows, dtype=jnp.int32)
    )
    north_freq = frequency_of(north_index, full_north)[:, None]
    east_freq = frequency_of(jnp.arange(full_east, dtype=jnp.int32), full_east)[None, :]
    wavenumber = 2.0 * math.pi * jnp.sqrt(north_freq * north_freq + east_freq * east_freq)
    combined_real = east_real[-1]
    combined_imag = east_imag[-1]
    for layer in range(LAYERS):
        layer_real, layer_imag = (east_real[layer], east_imag[layer])
        damped = jnp.exp(-wavenumber * layer_depth[layer])
        combined_real = combined_real + damped * layer_real
        combined_imag = combined_imag + damped * layer_imag
    filt_real, filt_imag = pole_filter(north_freq, east_freq, inclinations, declinations)
    shaped_real = filt_real * combined_real - filt_imag * combined_imag
    shaped_imag = filt_real * combined_imag + filt_imag * combined_real
    back_real, back_imag = transform_last(shaped_real, shaped_imag, 1.0)
    stacked = jnp.stack([back_real, back_imag]) / full_east
    returned = lax.all_to_all(
        lax.all_to_all(stacked, "row", split_axis=2, concat_axis=1, tiled=True),
        "col",
        split_axis=2,
        concat_axis=1,
        tiled=True,
    )
    returned = jnp.swapaxes(returned, 1, 2)
    out_cols = returned.shape[1]
    ordered = returned.reshape(2, out_cols, col_count, row_count, slab_rows).transpose(
        0, 1, 3, 2, 4
    )
    ordered = ordered.reshape(2, out_cols, full_north)
    final_real, final_imag = transform_last(ordered[0], ordered[1], 1.0)
    rtp_map = final_real / full_north
    return (solution.reshape(1, 1, -1), rtp_map)


def solution(mesh):
    in_specs = (
        P("row", "col", None, None, None),
        P("row", "col", None),
        P("row", "col"),
        P("row", "col", None),
        P(),
        P(),
        P(),
        P(),
        P("col", "row"),
    )
    out_specs = (P("row", "col", None), P(("row", "col"), None))
    return jax.shard_map(
        on_device, mesh=mesh, in_specs=in_specs, out_specs=out_specs, check_vma=False
    )
```

profile of v0, /device:TPU:0, one launch (start us, length us, event | category | flops | bytes accessed | tf_op | source)
XLA Modules:
  0.0 516.0 jit_solution(8219741678844305294)
XLA Ops:
  1.3 4.7 fusion.8
  11.5 5.6 %collective-permute-start.4 = (f32[512]{0:T(512)S(1)}, f32[512]{0:T(512)S(1)}, u32[]{:S(2)}, u32[]{:S(2)}) collective-permute-start(f32[512]{0:T(512)S(1)} %bitcast.370), channel_id=1, source_target_pairs={{0,1},{1,2},{2,3},{3,4},{4,5},{5,6},{6,7},{7,8},{8,9},{9,10},{10,1... | collective-permute-start | bytes 6152 | tf_op jit(solution)/shard_map/ppermute | solution.py:26
  17.0 8.1 %collective-permute-start.5 = (f32[512]{0:T(512)S(1)}, f32[512]{0:T(512)S(1)}, u32[]{:S(2)}, u32[]{:S(2)}) collective-permute-start(f32[512]{0:T(512)S(1)} %bitcast.369), channel_id=1, source_target_pairs={{0,3},{1,4},{2,5},{3,6},{4,7},{5,8},{6,9},{7,10},{8,11},{9,12},{10... | collective-permute-start | bytes 6152 | tf_op jit(solution)/shard_map/ppermute | solution.py:26
  25.2 4.3 collective-permute-start.6
  29.5 3.9 collective-permute-start.7
  34.8 9.0 %collective-permute-start.10 = (f32[512]{0:T(512)S(1)}, f32[512]{0:T(512)S(1)}, u32[]{:S(2)}, u32[]{:S(2)}) collective-permute-start(f32[512]{0:T(512)S(1)} %select_add_fusion.1), channel_id=1, source_target_pairs={{0,3},{1,4},{2,5},{3,6},{4,7},{5,8},{6,9},{7,10},{8,11},{9,12},{10... | collective-permute-start | bytes 6152 | tf_op jit(solution)/shard_map/ppermute | solution.py:26
  48.9 8.8 %collective-permute-start.8 = (f32[512]{0:T(512)S(1)}, f32[512]{0:T(512)S(1)}, u32[]{:S(2)}, u32[]{:S(2)}) collective-permute-start(f32[512]{0:T(512)S(1)} %select_add_fusion.1), channel_id=1, source_target_pairs={{0,5},{1,6},{2,7},{3,8},{4,9},{5,10},{6,11},{7,12},{8,13},{9,14},{... | collective-permute-start | bytes 6152 | tf_op jit(solution)/shard_map/ppermute | solution.py:26
  57.7 3.4 collective-permute-start.9
  62.5 3.4 collective-permute-done.14
  66.1 6.2 %fusion.6 = f32[1,256,1]{1,0,2:T(1,128)S(1)} fusion(f32[1,1,9,256,512]{4,3,2,1,0:T(8,128)} %param.9, f32[9,512,1]{1,0,2:T(8,128)S(1)} %convolution_bitcast_fusion.1), kind=kOutput, calls=%fused_computation.6 | convolution fusion | flops 14155776 | bytes 4738048 | tf_op jit(solution)/shard_map/krs,ks->r/dot_general | solution.py:169
  72.4 2.3 fusion.4
  80.2 4.5 collective-permute-start.20
  84.8 11.7 %collective-permute-start.21 = (f32[512]{0:T(512)S(1)}, f32[512]{0:T(512)S(1)}, u32[]{:S(2)}, u32[]{:S(2)}) collective-permute-start(f32[512]{0:T(512)S(1)} %bitcast.377), channel_id=1, source_target_pairs={{0,3},{1,4},{2,5},{3,6},{4,7},{5,8},{6,9},{7,10},{8,11},{9,12},{10... | collective-permute-start | bytes 6152 | tf_op jit(solution)/shard_map/ppermute | solution.py:26
  96.6 6.1 %collective-permute-start.22 = (f32[512]{0:T(512)S(1)}, f32[512]{0:T(512)S(1)}, u32[]{:S(2)}, u32[]{:S(2)}) collective-permute-start(f32[512]{0:T(512)S(1)} %bitcast.375), channel_id=1, source_target_pairs={{0,4},{1,5},{2,6},{3,7},{4,8},{5,9},{6,10},{7,11},{8,12},{9,13},{1... | collective-permute-start | bytes 6152 | tf_op jit(solution)/shard_map/ppermute | solution.py:26
  102.7 2.1 collective-permute-start.23
  106.8 48.6 %all-reduce.1 = (f32[]{:T(128)}, f32[]{:T(128)}) all-reduce(f32[]{:T(128)} %get-tuple-element.19, f32[]{:T(128)} %get-tuple-element.18), channel_id=1, replica_groups=mesh['row'=8,'col'=4] {'row','col'}, use_global_device_ids=true, to_apply=%region_1.2 | all-reduce | flops 2 | bytes 16 | tf_op jit(solution)/shard_map/psum | solution.py:141
  156.6 4.2 collective-permute-start.26
  166.6 5.8 %collective-permute-start.25 = (f32[512]{0:T(512)S(1)}, f32[512]{0:T(512)S(1)}, u32[]{:S(2)}, u32[]{:S(2)}) collective-permute-start(f32[512]{0:T(512)S(1)} %multiply_subtract_fusion.3), channel_id=1, source_target_pairs={{0,4},{1,5},{2,6},{3,7},{4,8},{5,9},{6,10},{7,11},{8,12},{9,13},{1... | collective-permute-start | bytes 6152 | tf_op jit(solution)/shard_map/ppermute | solution.py:26
  173.7 7.4 %collective-permute-start.24 = (f32[512]{0:T(512)S(1)}, f32[512]{0:T(512)S(1)}, u32[]{:S(2)}, u32[]{:S(2)}) collective-permute-start(f32[512]{0:T(512)S(1)} %multiply_subtract_fusion.3), channel_id=1, source_target_pairs={{0,5},{1,6},{2,7},{3,8},{4,9},{5,10},{6,11},{7,12},{8,13},{9,14},{... | collective-permute-start | bytes 6152 | tf_op jit(solution)/shard_map/ppermute | solution.py:26
  182.5 6.1 %fusion.2 = f32[1,256,1]{1,0,2:T(1,128)S(1)} fusion(f32[1,1,9,256,512]{4,3,2,1,0:T(8,128)} %param.9, f32[9,512,1]{1,0,2:T(8,128)S(1)} %convolution_bitcast_fusion), kind=kOutput, calls=%fused_computation.2 | convolution fusion | flops 14155776 | bytes 4738048 | tf_op jit(solution)/shard_map/krs,ks->r/dot_general | solution.py:169
  188.6 4.7 fusion
  198.8 4.5 collective-permute-start.36
  203.4 9.2 %collective-permute-start.37 = (f32[512]{0:T(512)S(1)}, f32[512]{0:T(512)S(1)}, u32[]{:S(2)}, u32[]{:S(2)}) collective-permute-start(f32[512]{0:T(512)S(1)} %bitcast.376), channel_id=1, source_target_pairs={{0,3},{1,4},{2,5},{3,6},{4,7},{5,8},{6,9},{7,10},{8,11},{9,12},{10... | collective-permute-start | bytes 6152 | tf_op jit(solution)/shard_map/ppermute | solution.py:26
  212.6 7.5 %collective-permute-start.38 = (f32[512]{0:T(512)S(1)}, f32[512]{0:T(512)S(1)}, u32[]{:S(2)}, u32[]{:S(2)}) collective-permute-start(f32[512]{0:T(512)S(1)} %bitcast.374), channel_id=1, source_target_pairs={{0,4},{1,5},{2,6},{3,7},{4,8},{5,9},{6,10},{7,11},{8,12},{9,13},{1... | collective-permute-start | bytes 6152 | tf_op jit(solution)/shard_map/ppermute | solution.py:26
  220.1 2.6 collective-permute-start.39
  224.7 48.9 %all-reduce = (f32[]{:T(128)}, f32[]{:T(128)}) all-reduce(f32[]{:T(128)} %get-tuple-element.17, f32[]{:T(128)} %get-tuple-element.16), channel_id=1, replica_groups=mesh['row'=8,'col'=4] {'row','col'}, use_global_device_ids=true, to_apply=%region_5.6 | all-reduce | flops 2 | bytes 16 | tf_op jit(solution)/shard_map/psum | solution.py:141
  277.9 4.2 collective-permute-start.42
  287.9 5.8 %collective-permute-start.41 = (f32[512]{0:T(512)S(1)}, f32[512]{0:T(512)S(1)}, u32[]{:S(2)}, u32[]{:S(2)}) collective-permute-start(f32[512]{0:T(512)S(1)} %multiply_add_fusion.8), channel_id=1, source_target_pairs={{0,4},{1,5},{2,6},{3,7},{4,8},{5,9},{6,10},{7,11},{8,12},{9,13},{1... | collective-permute-start | bytes 6152 | tf_op jit(solution)/shard_map/ppermute | solution.py:26
  295.0 7.3 %collective-permute-start.40 = (f32[512]{0:T(512)S(1)}, f32[512]{0:T(512)S(1)}, u32[]{:S(2)}, u32[]{:S(2)}) collective-permute-start(f32[512]{0:T(512)S(1)} %multiply_add_fusion.8), channel_id=1, source_target_pairs={{0,5},{1,6},{2,7},{3,8},{4,9},{5,10},{6,11},{7,12},{8,13},{9,14},{... | collective-permute-start | bytes 6152 | tf_op jit(solution)/shard_map/ppermute | solution.py:26
  306.9 14.8 %all-to-all-start = ((f32[3,512,128]{2,0,1:T(4,128)}), f32[3,512,128]{2,0,1:T(4,128)S(1)}, u32[]{:S(2)}, u32[]{:S(2)}) async-start(f32[3,512,128]{2,0,1:T(4,128)} %copy.337), calls=%async_computation | async-start | bytes 2097152 | tf_op jit(solution)/shard_map/all_to_all | solution.py:208
  321.7 15.3 %all-to-all-done = f32[3,512,128]{2,0,1:T(4,128)S(1)} async-done(((f32[3,512,128]{2,0,1:T(4,128)}), f32[3,512,128]{2,0,1:T(4,128)S(1)}, u32[]{:S(2)}, u32[]{:S(2)}) %all-to-all-start) | async-done | bytes 786464 | tf_op jit(solution)/shard_map/all_to_all | solution.py:208
  344.7 2.5 stack_reshape.12
  347.2 3.1 fusion.12
  350.3 2.5 copy.344
  352.8 3.5 stack_reshape.13
  356.2 2.7 pad_maximum_fusion
  358.9 2.4 copy.450
  361.3 4.5 reshape.288
  365.9 24.5 %all_to_all.87 = f32[8,1,49152]{2,1,0:T(1,128)S(1)} all-to-all(f32[8,1,49152]{2,1,0:T(1,128)} %reshape.288), channel_id=1, replica_groups=mesh['row'=8,'col'=4] {'row'}, dimensions={0} | all-to-all | bytes 3145728 | tf_op jit(solution)/shard_map/all_to_all | solution.py:213
  390.8 6.2 %reduce = f32[8,49152]{1,0:T(8,128)} reduce(f32[8,1,49152]{2,1,0:T(1,128)S(1)} %all_to_all.87, f32[]{:T(128)} %broadcast.789), dimensions={1}, to_apply=%all_to_all.66.reduce_sub_computation | reduce | bytes 3145732 | tf_op jit(solution)/shard_map/all_to_all | solution.py:213
  397.0 3.7 reshape.289
  400.7 3.6 copy.398
  404.4 3.8 copy.348
  408.2 3.7 all-to-all-start.2
  420.2 28.1 %all-to-all-done.2 = f32[2,3,512,128]{2,0,1,3:T(2,128)S(1)} async-done(((f32[2,3,512,128]{2,0,1,3:T(2,128)}), f32[2,3,512,128]{2,0,1,3:T(2,128)S(1)}, u32[]{:S(2)}, u32[]{:S(2)}) %all-to-all-start.2) | async-done | bytes 1572896 | tf_op jit(solution)/shard_map/all_to_all | solution.py:212
  474.9 12.4 %all_to_all.88 = f32[8,1,16384]{2,1,0:T(1,128)S(1)} all-to-all(f32[8,1,16384]{2,1,0:T(1,128)S(1)} %reshape.290), channel_id=1, replica_groups=mesh['row'=8,'col'=4] {'row'}, dimensions={0} | all-to-all | bytes 1048576 | tf_op jit(solution)/shard_map/all_to_all | solution.py:241
  492.9 3.5 all-to-all-start.4
  496.4 14.0 %all-to-all-done.4 = f32[2,256,256]{1,0,2:T(2,128)S(1)} async-done(((f32[2,256,256]{1,0,2:T(2,128)}), f32[2,256,256]{1,0,2:T(2,128)S(1)}, u32[]{:S(2)}, u32[]{:S(2)}) %all-to-all-start.4) | async-done | bytes 524320 | tf_op jit(solution)/shard_map/all_to_all | solution.py:240
  (221 shorter events, 94.8 us)
Async XLA Ops:
  6.3 10.8 %collective-permute-start = (f32[512]{0:T(512)S(1)}, f32[512]{0:T(512)S(1)}, u32[]{:S(2)}, u32[]{:S(2)}) collective-permute-start(f32[512]{0:T(512)S(1)} %bitcast.389), channel_id=1, source_target_pairs={{5,0},{6,1},{7,2},{8,3},{9,4},{10,5},{11,6},{12,7},{13,8},{14,9},{... | collective-permute-start | bytes 6152 | tf_op jit(solution)/shard_map/ppermute | solution.py:26
  7.6 17.6 %collective-permute-start.1 = (f32[512]{0:T(512)S(1)}, f32[512]{0:T(512)S(1)}, u32[]{:S(2)}, u32[]{:S(2)}) collective-permute-start(f32[512]{0:T(512)S(1)} %bitcast.386), channel_id=1, source_target_pairs={{4,0},{5,1},{6,2},{7,3},{8,4},{9,5},{10,6},{11,7},{12,8},{13,9},{1... | collective-permute-start | bytes 6152 | tf_op jit(solution)/shard_map/ppermute | solution.py:26
  8.9 20.6 %collective-permute-start.2 = (f32[512]{0:T(512)S(1)}, f32[512]{0:T(512)S(1)}, u32[]{:S(2)}, u32[]{:S(2)}) collective-permute-start(f32[512]{0:T(512)S(1)} %bitcast.383), channel_id=1, source_target_pairs={{3,0},{4,1},{5,2},{6,3},{7,4},{8,5},{9,6},{10,7},{11,8},{12,9},{13... | collective-permute-start | bytes 6152 | tf_op jit(solution)/shard_map/ppermute | solution.py:26
  10.2 23.3 %collective-permute-start.3 = (f32[512]{0:T(512)S(1)}, f32[512]{0:T(512)S(1)}, u32[]{:S(2)}, u32[]{:S(2)}) collective-permute-start(f32[512]{0:T(512)S(1)} %bitcast.371), channel_id=1, source_target_pairs={{1,0},{2,1},{3,2},{4,3},{5,4},{6,5},{7,6},{8,7},{9,8},{10,9},{11,1... | collective-permute-start | bytes 6152 | tf_op jit(solution)/shard_map/ppermute | solution.py:26
  11.5 22.0 %collective-permute-start.4 = (f32[512]{0:T(512)S(1)}, f32[512]{0:T(512)S(1)}, u32[]{:S(2)}, u32[]{:S(2)}) collective-permute-start(f32[512]{0:T(512)S(1)} %bitcast.370), channel_id=1, source_target_pairs={{0,1},{1,2},{2,3},{3,4},{4,5},{5,6},{6,7},{7,8},{8,9},{9,10},{10,1... | collective-permute-start | bytes 6152 | tf_op jit(solution)/shard_map/ppermute | solution.py:26
  17.0 16.4 %collective-permute-start.5 = (f32[512]{0:T(512)S(1)}, f32[512]{0:T(512)S(1)}, u32[]{:S(2)}, u32[]{:S(2)}) collective-permute-start(f32[512]{0:T(512)S(1)} %bitcast.369), channel_id=1, source_target_pairs={{0,3},{1,4},{2,5},{3,6},{4,7},{5,8},{6,9},{7,10},{8,11},{9,12},{10... | collective-permute-start | bytes 6152 | tf_op jit(solution)/shard_map/ppermute | solution.py:26
  25.2 8.3 %collective-permute-start.6 = (f32[512]{0:T(512)S(1)}, f32[512]{0:T(512)S(1)}, u32[]{:S(2)}, u32[]{:S(2)}) collective-permute-start(f32[512]{0:T(512)S(1)} %bitcast.368), channel_id=1, source_target_pairs={{0,4},{1,5},{2,6},{3,7},{4,8},{5,9},{6,10},{7,11},{8,12},{9,13},{1... | collective-permute-start | bytes 6152 | tf_op jit(solution)/shard_map/ppermute | solution.py:26
  29.5 5.2 %collective-permute-start.7 = (f32[512]{0:T(512)S(1)}, f32[512]{0:T(512)S(1)}, u32[]{:S(2)}, u32[]{:S(2)}) collective-permute-start(f32[512]{0:T(512)S(1)} %bitcast.367), channel_id=1, source_target_pairs={{0,5},{1,6},{2,7},{3,8},{4,9},{5,10},{6,11},{7,12},{8,13},{9,14},{... | collective-permute-start | bytes 6152 | tf_op jit(solution)/shard_map/ppermute | solution.py:26
  34.8 14.2 %collective-permute-start.10 = (f32[512]{0:T(512)S(1)}, f32[512]{0:T(512)S(1)}, u32[]{:S(2)}, u32[]{:S(2)}) collective-permute-start(f32[512]{0:T(512)S(1)} %select_add_fusion.1), channel_id=1, source_target_pairs={{0,3},{1,4},{2,5},{3,6},{4,7},{5,8},{6,9},{7,10},{8,11},{9,12},{10... | collective-permute-start | bytes 6152 | tf_op jit(solution)/shard_map/ppermute | solution.py:26
  43.7 14.0 %collective-permute-start.11 = (f32[512]{0:T(512)S(1)}, f32[512]{0:T(512)S(1)}, u32[]{:S(2)}, u32[]{:S(2)}) collective-permute-start(f32[512]{0:T(512)S(1)} %select_add_fusion.1), channel_id=1, source_target_pairs={{0,1},{1,2},{2,3},{3,4},{4,5},{5,6},{6,7},{7,8},{8,9},{9,10},{10,1... | collective-permute-start | bytes 6152 | tf_op jit(solution)/shard_map/ppermute | solution.py:26
  45.0 16.1 %collective-permute-start.12 = (f32[512]{0:T(512)S(1)}, f32[512]{0:T(512)S(1)}, u32[]{:S(2)}, u32[]{:S(2)}) collective-permute-start(f32[512]{0:T(512)S(1)} %select_add_fusion.1), channel_id=1, source_target_pairs={{1,0},{2,1},{3,2},{4,3},{5,4},{6,5},{7,6},{8,7},{9,8},{10,9},{11,1... | collective-permute-start | bytes 6152 | tf_op jit(solution)/shard_map/ppermute | solution.py:26
  46.3 16.1 %collective-permute-start.13 = (f32[512]{0:T(512)S(1)}, f32[512]{0:T(512)S(1)}, u32[]{:S(2)}, u32[]{:S(2)}) collective-permute-start(f32[512]{0:T(512)S(1)} %select_add_fusion.1), channel_id=1, source_target_pairs={{3,0},{4,1},{5,2},{6,3},{7,4},{8,5},{9,6},{10,7},{11,8},{12,9},{13... | collective-permute-start | bytes 6152 | tf_op jit(solution)/shard_map/ppermute | solution.py:26
  47.6 14.8 %collective-permute-start.15 = (f32[512]{0:T(512)S(1)}, f32[512]{0:T(512)S(1)}, u32[]{:S(2)}, u32[]{:S(2)}) collective-permute-start(f32[512]{0:T(512)S(1)} %select_add_fusion.1), channel_id=1, source_target_pairs={{5,0},{6,1},{7,2},{8,3},{9,4},{10,5},{11,6},{12,7},{13,8},{14,9},{... | collective-permute-start | bytes 6152 | tf_op jit(solution)/shard_map/ppermute | solution.py:26
  48.9 13.5 %collective-permute-start.8 = (f32[512]{0:T(512)S(1)}, f32[512]{0:T(512)S(1)}, u32[]{:S(2)}, u32[]{:S(2)}) collective-permute-start(f32[512]{0:T(512)S(1)} %select_add_fusion.1), channel_id=1, source_target_pairs={{0,5},{1,6},{2,7},{3,8},{4,9},{5,10},{6,11},{7,12},{8,13},{9,14},{... | collective-permute-start | bytes 6152 | tf_op jit(solution)/shard_map/ppermute | solution.py:26
  57.7 4.8 collective-permute-start.9
  75.0 9.8 %collective-permute-start.16 = (f32[512]{0:T(512)S(1)}, f32[512]{0:T(512)S(1)}, u32[]{:S(2)}, u32[]{:S(2)}) collective-permute-start(f32[512]{0:T(512)S(1)} %bitcast.390), channel_id=1, source_target_pairs={{5,0},{6,1},{7,2},{8,3},{9,4},{10,5},{11,6},{12,7},{13,8},{14,9},{... | collective-permute-start | bytes 6152 | tf_op jit(solution)/shard_map/ppermute | solution.py:26
  76.3 20.2 %collective-permute-start.17 = (f32[512]{0:T(512)S(1)}, f32[512]{0:T(512)S(1)}, u32[]{:S(2)}, u32[]{:S(2)}) collective-permute-start(f32[512]{0:T(512)S(1)} %bitcast.387), channel_id=1, source_target_pairs={{4,0},{5,1},{6,2},{7,3},{8,4},{9,5},{10,6},{11,7},{12,8},{13,9},{1... | collective-permute-start | bytes 6152 | tf_op jit(solution)/shard_map/ppermute | solution.py:26
  77.6 25.1 %collective-permute-start.18 = (f32[512]{0:T(512)S(1)}, f32[512]{0:T(512)S(1)}, u32[]{:S(2)}, u32[]{:S(2)}) collective-permute-start(f32[512]{0:T(512)S(1)} %bitcast.384), channel_id=1, source_target_pairs={{3,0},{4,1},{5,2},{6,3},{7,4},{8,5},{9,6},{10,7},{11,8},{12,9},{13... | collective-permute-start | bytes 6152 | tf_op jit(solution)/shard_map/ppermute | solution.py:26
  78.9 26.6 %collective-permute-start.19 = (f32[512]{0:T(512)S(1)}, f32[512]{0:T(512)S(1)}, u32[]{:S(2)}, u32[]{:S(2)}) collective-permute-start(f32[512]{0:T(512)S(1)} %bitcast.381), channel_id=1, source_target_pairs={{1,0},{2,1},{3,2},{4,3},{5,4},{6,5},{7,6},{8,7},{9,8},{10,9},{11,1... | collective-permute-start | bytes 6152 | tf_op jit(solution)/shard_map/ppermute | solution.py:26
  80.2 25.3 %collective-permute-start.20 = (f32[512]{0:T(512)S(1)}, f32[512]{0:T(512)S(1)}, u32[]{:S(2)}, u32[]{:S(2)}) collective-permute-start(f32[512]{0:T(512)S(1)} %bitcast.379), channel_id=1, source_target_pairs={{0,1},{1,2},{2,3},{3,4},{4,5},{5,6},{6,7},{7,8},{8,9},{9,10},{10,1... | collective-permute-start | bytes 6152 | tf_op jit(solution)/shard_map/ppermute | solution.py:26
  84.8 20.7 %collective-permute-start.21 = (f32[512]{0:T(512)S(1)}, f32[512]{0:T(512)S(1)}, u32[]{:S(2)}, u32[]{:S(2)}) collective-permute-start(f32[512]{0:T(512)S(1)} %bitcast.377), channel_id=1, source_target_pairs={{0,3},{1,4},{2,5},{3,6},{4,7},{5,8},{6,9},{7,10},{8,11},{9,12},{10... | collective-permute-start | bytes 6152 | tf_op jit(solution)/shard_map/ppermute | solution.py:26
  96.6 9.0 %collective-permute-start.22 = (f32[512]{0:T(512)S(1)}, f32[512]{0:T(512)S(1)}, u32[]{:S(2)}, u32[]{:S(2)}) collective-permute-start(f32[512]{0:T(512)S(1)} %bitcast.375), channel_id=1, source_target_pairs={{0,4},{1,5},{2,6},{3,7},{4,8},{5,9},{6,10},{7,11},{8,12},{9,13},{1... | collective-permute-start | bytes 6152 | tf_op jit(solution)/shard_map/ppermute | solution.py:26
  156.6 9.9 %collective-permute-start.26 = (f32[512]{0:T(512)S(1)}, f32[512]{0:T(512)S(1)}, u32[]{:S(2)}, u32[]{:S(2)}) collective-permute-start(f32[512]{0:T(512)S(1)} %multiply_subtract_fusion.3), channel_id=1, source_target_pairs={{0,3},{1,4},{2,5},{3,6},{4,7},{5,8},{6,9},{7,10},{8,11},{9,12},{10... | collective-permute-start | bytes 6152 | tf_op jit(solution)/shard_map/ppermute | solution.py:26
  160.9 11.5 %collective-permute-start.27 = (f32[512]{0:T(512)S(1)}, f32[512]{0:T(512)S(1)}, u32[]{:S(2)}, u32[]{:S(2)}) collective-permute-start(f32[512]{0:T(512)S(1)} %multiply_subtract_fusion.3), channel_id=1, source_target_pairs={{0,1},{1,2},{2,3},{3,4},{4,5},{5,6},{6,7},{7,8},{8,9},{9,10},{10,1... | collective-permute-start | bytes 6152 | tf_op jit(solution)/shard_map/ppermute | solution.py:26
  162.6 11.0 %collective-permute-start.28 = (f32[512]{0:T(512)S(1)}, f32[512]{0:T(512)S(1)}, u32[]{:S(2)}, u32[]{:S(2)}) collective-permute-start(f32[512]{0:T(512)S(1)} %multiply_subtract_fusion.3), channel_id=1, source_target_pairs={{1,0},{2,1},{3,2},{4,3},{5,4},{6,5},{7,6},{8,7},{9,8},{10,9},{11,1... | collective-permute-start | bytes 6152 | tf_op jit(solution)/shard_map/ppermute | solution.py:26
  163.9 17.2 %collective-permute-start.29 = (f32[512]{0:T(512)S(1)}, f32[512]{0:T(512)S(1)}, u32[]{:S(2)}, u32[]{:S(2)}) collective-permute-start(f32[512]{0:T(512)S(1)} %multiply_subtract_fusion.3), channel_id=1, source_target_pairs={{3,0},{4,1},{5,2},{6,3},{7,4},{8,5},{9,6},{10,7},{11,8},{12,9},{13... | collective-permute-start | bytes 6152 | tf_op jit(solution)/shard_map/ppermute | solution.py:26
  165.2 15.9 %collective-permute-start.31 = (f32[512]{0:T(512)S(1)}, f32[512]{0:T(512)S(1)}, u32[]{:S(2)}, u32[]{:S(2)}) collective-permute-start(f32[512]{0:T(512)S(1)} %multiply_subtract_fusion.3), channel_id=1, source_target_pairs={{5,0},{6,1},{7,2},{8,3},{9,4},{10,5},{11,6},{12,7},{13,8},{14,9},{... | collective-permute-start | bytes 6152 | tf_op jit(solution)/shard_map/ppermute | solution.py:26
  166.6 14.6 %collective-permute-start.25 = (f32[512]{0:T(512)S(1)}, f32[512]{0:T(512)S(1)}, u32[]{:S(2)}, u32[]{:S(2)}) collective-permute-start(f32[512]{0:T(512)S(1)} %multiply_subtract_fusion.3), channel_id=1, source_target_pairs={{0,4},{1,5},{2,6},{3,7},{4,8},{5,9},{6,10},{7,11},{8,12},{9,13},{1... | collective-permute-start | bytes 6152 | tf_op jit(solution)/shard_map/ppermute | solution.py:26
  172.4 8.9 %collective-permute-start.30 = (f32[512]{0:T(512)S(1)}, f32[512]{0:T(512)S(1)}, u32[]{:S(2)}, u32[]{:S(2)}) collective-permute-start(f32[512]{0:T(512)S(1)} %multiply_subtract_fusion.3), channel_id=1, source_target_pairs={{4,0},{5,1},{6,2},{7,3},{8,4},{9,5},{10,6},{11,7},{12,8},{13,9},{1... | collective-permute-start | bytes 6152 | tf_op jit(solution)/shard_map/ppermute | solution.py:26
  173.7 8.6 %collective-permute-start.24 = (f32[512]{0:T(512)S(1)}, f32[512]{0:T(512)S(1)}, u32[]{:S(2)}, u32[]{:S(2)}) collective-permute-start(f32[512]{0:T(512)S(1)} %multiply_subtract_fusion.3), channel_id=1, source_target_pairs={{0,5},{1,6},{2,7},{3,8},{4,9},{5,10},{6,11},{7,12},{8,13},{9,14},{... | collective-permute-start | bytes 6152 | tf_op jit(solution)/shard_map/ppermute | solution.py:26
  193.6 9.8 %collective-permute-start.32 = (f32[512]{0:T(512)S(1)}, f32[512]{0:T(512)S(1)}, u32[]{:S(2)}, u32[]{:S(2)}) collective-permute-start(f32[512]{0:T(512)S(1)} %bitcast.388), channel_id=1, source_target_pairs={{5,0},{6,1},{7,2},{8,3},{9,4},{10,5},{11,6},{12,7},{13,8},{14,9},{... | collective-permute-start | bytes 6152 | tf_op jit(solution)/shard_map/ppermute | solution.py:26
  194.9 17.7 %collective-permute-start.33 = (f32[512]{0:T(512)S(1)}, f32[512]{0:T(512)S(1)}, u32[]{:S(2)}, u32[]{:S(2)}) collective-permute-start(f32[512]{0:T(512)S(1)} %bitcast.385), channel_id=1, source_target_pairs={{4,0},{5,1},{6,2},{7,3},{8,4},{9,5},{10,6},{11,7},{12,8},{13,9},{1... | collective-permute-start | bytes 6152 | tf_op jit(solution)/shard_map/ppermute | solution.py:26
  196.2 23.9 %collective-permute-start.34 = (f32[512]{0:T(512)S(1)}, f32[512]{0:T(512)S(1)}, u32[]{:S(2)}, u32[]{:S(2)}) collective-permute-start(f32[512]{0:T(512)S(1)} %bitcast.382), channel_id=1, source_target_pairs={{3,0},{4,1},{5,2},{6,3},{7,4},{8,5},{9,6},{10,7},{11,8},{12,9},{13... | collective-permute-start | bytes 6152 | tf_op jit(solution)/shard_map/ppermute | solution.py:26
  197.5 25.2 %collective-permute-start.35 = (f32[512]{0:T(512)S(1)}, f32[512]{0:T(512)S(1)}, u32[]{:S(2)}, u32[]{:S(2)}) collective-permute-start(f32[512]{0:T(512)S(1)} %bitcast.380), channel_id=1, source_target_pairs={{1,0},{2,1},{3,2},{4,3},{5,4},{6,5},{7,6},{8,7},{9,8},{10,9},{11,1... | collective-permute-start | bytes 6152 | tf_op jit(solution)/shard_map/ppermute | solution.py:26
  198.8 23.9 %collective-permute-start.36 = (f32[512]{0:T(512)S(1)}, f32[512]{0:T(512)S(1)}, u32[]{:S(2)}, u32[]{:S(2)}) collective-permute-start(f32[512]{0:T(512)S(1)} %bitcast.378), channel_id=1, source_target_pairs={{0,1},{1,2},{2,3},{3,4},{4,5},{5,6},{6,7},{7,8},{8,9},{9,10},{10,1... | collective-permute-start | bytes 6152 | tf_op jit(solution)/shard_map/ppermute | solution.py:26
  203.4 19.3 %collective-permute-start.37 = (f32[512]{0:T(512)S(1)}, f32[512]{0:T(512)S(1)}, u32[]{:S(2)}, u32[]{:S(2)}) collective-permute-start(f32[512]{0:T(512)S(1)} %bitcast.376), channel_id=1, source_target_pairs={{0,3},{1,4},{2,5},{3,6},{4,7},{5,8},{6,9},{7,10},{8,11},{9,12},{10... | collective-permute-start | bytes 6152 | tf_op jit(solution)/shard_map/ppermute | solution.py:26
  212.6 10.1 %collective-permute-start.38 = (f32[512]{0:T(512)S(1)}, f32[512]{0:T(512)S(1)}, u32[]{:S(2)}, u32[]{:S(2)}) collective-permute-start(f32[512]{0:T(512)S(1)} %bitcast.374), channel_id=1, source_target_pairs={{0,4},{1,5},{2,6},{3,7},{4,8},{5,9},{6,10},{7,11},{8,12},{9,13},{1... | collective-permute-start | bytes 6152 | tf_op jit(solution)/shard_map/ppermute | solution.py:26
  277.9 10.0 %collective-permute-start.42 = (f32[512]{0:T(512)S(1)}, f32[512]{0:T(512)S(1)}, u32[]{:S(2)}, u32[]{:S(2)}) collective-permute-start(f32[512]{0:T(512)S(1)} %multiply_add_fusion.8), channel_id=1, source_target_pairs={{0,3},{1,4},{2,5},{3,6},{4,7},{5,8},{6,9},{7,10},{8,11},{9,12},{10... | collective-permute-start | bytes 6152 | tf_op jit(solution)/shard_map/ppermute | solution.py:26
  282.1 11.6 %collective-permute-start.43 = (f32[512]{0:T(512)S(1)}, f32[512]{0:T(512)S(1)}, u32[]{:S(2)}, u32[]{:S(2)}) collective-permute-start(f32[512]{0:T(512)S(1)} %multiply_add_fusion.8), channel_id=1, source_target_pairs={{0,1},{1,2},{2,3},{3,4},{4,5},{5,6},{6,7},{7,8},{8,9},{9,10},{10,1... | collective-permute-start | bytes 6152 | tf_op jit(solution)/shard_map/ppermute | solution.py:26
  284.0 11.0 %collective-permute-start.44 = (f32[512]{0:T(512)S(1)}, f32[512]{0:T(512)S(1)}, u32[]{:S(2)}, u32[]{:S(2)}) collective-permute-start(f32[512]{0:T(512)S(1)} %multiply_add_fusion.8), channel_id=1, source_target_pairs={{1,0},{2,1},{3,2},{4,3},{5,4},{6,5},{7,6},{8,7},{9,8},{10,9},{11,1... | collective-permute-start | bytes 6152 | tf_op jit(solution)/shard_map/ppermute | solution.py:26
  285.3 17.0 %collective-permute-start.45 = (f32[512]{0:T(512)S(1)}, f32[512]{0:T(512)S(1)}, u32[]{:S(2)}, u32[]{:S(2)}) collective-permute-start(f32[512]{0:T(512)S(1)} %multiply_add_fusion.8), channel_id=1, source_target_pairs={{3,0},{4,1},{5,2},{6,3},{7,4},{8,5},{9,6},{10,7},{11,8},{12,9},{13... | collective-permute-start | bytes 6152 | tf_op jit(solution)/shard_map/ppermute | solution.py:26
  286.6 15.7 %collective-permute-start.47 = (f32[512]{0:T(512)S(1)}, f32[512]{0:T(512)S(1)}, u32[]{:S(2)}, u32[]{:S(2)}) collective-permute-start(f32[512]{0:T(512)S(1)} %multiply_add_fusion.8), channel_id=1, source_target_pairs={{5,0},{6,1},{7,2},{8,3},{9,4},{10,5},{11,6},{12,7},{13,8},{14,9},{... | collective-permute-start | bytes 6152 | tf_op jit(solution)/shard_map/ppermute | solution.py:26
  287.9 14.5 %collective-permute-start.41 = (f32[512]{0:T(512)S(1)}, f32[512]{0:T(512)S(1)}, u32[]{:S(2)}, u32[]{:S(2)}) collective-permute-start(f32[512]{0:T(512)S(1)} %multiply_add_fusion.8), channel_id=1, source_target_pairs={{0,4},{1,5},{2,6},{3,7},{4,8},{5,9},{6,10},{7,11},{8,12},{9,13},{1... | collective-permute-start | bytes 6152 | tf_op jit(solution)/shard_map/ppermute | solution.py:26
  293.7 8.7 %collective-permute-start.46 = (f32[512]{0:T(512)S(1)}, f32[512]{0:T(512)S(1)}, u32[]{:S(2)}, u32[]{:S(2)}) collective-permute-start(f32[512]{0:T(512)S(1)} %multiply_add_fusion.8), channel_id=1, source_target_pairs={{4,0},{5,1},{6,2},{7,3},{8,4},{9,5},{10,6},{11,7},{12,8},{13,9},{1... | collective-permute-start | bytes 6152 | tf_op jit(solution)/shard_map/ppermute | solution.py:26
  295.0 8.6 %collective-permute-start.40 = (f32[512]{0:T(512)S(1)}, f32[512]{0:T(512)S(1)}, u32[]{:S(2)}, u32[]{:S(2)}) collective-permute-start(f32[512]{0:T(512)S(1)} %multiply_add_fusion.8), channel_id=1, source_target_pairs={{0,5},{1,6},{2,7},{3,8},{4,9},{5,10},{6,11},{7,12},{8,13},{9,14},{... | collective-permute-start | bytes 6152 | tf_op jit(solution)/shard_map/ppermute | solution.py:26
  306.9 30.1 %all-to-all-start = ((f32[3,512,128]{2,0,1:T(4,128)}), f32[3,512,128]{2,0,1:T(4,128)S(1)}, u32[]{:S(2)}, u32[]{:S(2)}) async-start(f32[3,512,128]{2,0,1:T(4,128)} %copy.337), calls=%async_computation | async-start | bytes 2097152 | tf_op jit(solution)/shard_map/all_to_all | solution.py:208
  408.2 40.1 %all-to-all-start.2 = ((f32[2,3,512,128]{2,0,1,3:T(2,128)}), f32[2,3,512,128]{2,0,1,3:T(2,128)S(1)}, u32[]{:S(2)}, u32[]{:S(2)}) async-start(f32[2,3,512,128]{2,0,1,3:T(2,128)} %copy.348), calls=%async_computation.2 | async-start | bytes 3145728 | tf_op jit(solution)/shard_map/all_to_all | solution.py:212
  492.9 17.5 %all-to-all-start.4 = ((f32[2,256,256]{1,0,2:T(2,128)}), f32[2,256,256]{1,0,2:T(2,128)S(1)}, u32[]{:S(2)}, u32[]{:S(2)}) async-start(f32[2,256,256]{1,0,2:T(2,128)} %copy.378), calls=%async_computation.4 | async-start | bytes 1048576 | tf_op jit(solution)/shard_map/all_to_all | solution.py:240
  (10 other events, 232.4 us)
where the time goes:
time: 526 us; the launch traced here: 516 us
  starting transfers between devices  184 us (35%)
  blocking collectives  134 us (25%)
  waiting for transfers between devices  66.2 us (13%)
  matrix products  52.2 us (10%)
  local copies, waits for them, and re-layouts  49.4 us (9%)
  between operations  15.6 us (3%)
  other arithmetic  14.3 us (3%)
    ppermute x48, starting transfers between devices, shifted(): return lax.ppermute(x, axis, pairs)  162 us
    psum x2, blocking collectives, two_products(): lax.psum((jnp.sum(residual * residual), jnp.sum(residual * applied)), ('r...  97.5 us
    all_to_all x1, waiting for transfers between devices, on_device(): lax.all_to_all(lax.all_to_all(spectra, 'row', split_axis=3, concat_axis=2...  28.1 us
    all_to_all x1, blocking collectives, on_device(): lax.all_to_all(spectra, 'row', split_axis=3, concat_axis=2, tiled=True)  24.5 us
    all_to_all x1, waiting for transfers between devices, on_device(): lax.all_to_all(tile_planes, 'row', split_axis=1, concat_axis=2, tiled=True)  15.3 us
    all_to_all x1, starting transfers between devices, on_device(): lax.all_to_all(tile_planes, 'row', split_axis=1, concat_axis=2, tiled=True)  14.8 us
    all_to_all x1, waiting for transfers between devices, on_device(): lax.all_to_all(lax.all_to_all(stacked, 'row', split_axis=2, concat_axis=1...  14 us
    unnamed x21, local copies, waits for them, and re-layouts  13.2 us
  transfers between devices with their start and end apart: 51, of which 9 were waited for; matrix products, arithmetic and copies ran while one was open for 0% of the time, Pallas kernels for 0%

commit v1 on v0

v1 whole, which is shorter than its diff:
```python
import functools

import jax
import jax.numpy as jnp
import ml_dtypes
import numpy as np
from jax import lax
from jax.experimental import pallas as pl
from jax.experimental.pallas import tpu as pltpu
from jax.sharding import PartitionSpec as P

SRC_ROWS = 8
SRC_COLS = 32
LAYERS = 2
REFINE = 16
FOOTPRINT = 9
LANES = 128
SUB = 8
HALF = 64
BOTH = ("row", "col")
VMEM_BYTES = 40 * 1024 * 1024
F32 = jnp.float32
BF16 = jnp.bfloat16

VMEM = pl.BlockSpec(memory_space=pltpu.VMEM)
SMEM = pl.BlockSpec(memory_space=pltpu.SMEM)
NN = (((1,), (0,)), ((), ()))
NT = (((1,), (1,)), ((), ()))
TN = (((0,), (0,)), ((), ()))


def split_table(table):
    high = table.astype(ml_dtypes.bfloat16)
    low = (table - high.astype(np.float64)).astype(ml_dtypes.bfloat16)
    return np.stack([high, low])


def group_start(group, rows):
    if group == 0:
        return 0
    if group == 1:
        return rows // 2
    return group // 2 + HALF * rows * (group % 2)


def unit_turn(product, period):
    angle = 2.0 * np.pi * (product % period) / period
    return np.cos(angle), np.sin(angle)


def north_turns(rows):
    north = rows * LANES
    starts = np.array([group_start(g, rows) for g in range(rows)])
    cos, sin = unit_turn(starts[:, None] * np.arange(north)[None, :], north)
    turns = np.stack([cos, -sin]).reshape(2, rows, rows, LANES)
    return turns.astype(np.float32)


def north_forward_table():
    cos, sin = unit_turn(np.outer(np.arange(HALF), np.arange(LANES)), LANES)
    plain = np.concatenate(
        [np.concatenate([cos, sin], 1), np.concatenate([-sin, cos], 1)], 0
    )
    packed = plain.copy()
    packed[HALF, :LANES] = 1.0 - 2.0 * (np.arange(LANES) % 2)
    return np.stack([split_table(packed), split_table(plain)])


def north_inverse_table():
    cos, sin = unit_turn(np.outer(np.arange(HALF), np.arange(LANES)), LANES)
    plain = 2.0 * np.concatenate([cos, sin], 1)
    packed = plain.copy()
    packed[0, :LANES] = 1.0
    packed[0, LANES:] = 2.0 * (np.arange(LANES) % 2) - 1.0
    return np.stack([split_table(packed), split_table(plain)])


def east_tables(east):
    bands = east // LANES
    cos, sin = unit_turn(np.outer(np.arange(LANES), np.arange(LANES)), LANES)
    forward = np.block([[cos, -sin], [sin, cos]])
    inverse = np.block([[cos, sin], [-sin, cos]])
    turn_cos, turn_sin = unit_turn(np.outer(np.arange(bands), np.arange(LANES)), east)
    turns = np.stack([turn_cos, -turn_sin]).astype(np.float32)
    return split_table(forward), split_table(inverse), turns


def hat_table(fine_count, coarse_count):
    offset = (np.arange(fine_count)[:, None] + 0.5) / REFINE - 0.5 - np.arange(coarse_count)[None, :]
    return np.maximum(0.0, 1.0 - np.abs(offset))


def north_hat_table(rows, cols):
    north = rows * LANES
    coarse = rows * SRC_ROWS
    own = HALF // cols
    spectrum = np.fft.fft(hat_table(north, coarse), axis=0)
    out = np.zeros((rows, cols, 2 * own, coarse))
    for group in range(rows):
        for col in range(cols):
            index = group_start(group, rows) + rows * (col * own + np.arange(own))
            part = spectrum[index % north]
            out[group, col, :own] = part.real
            out[group, col, own:] = part.imag
    out[0, 0, own] = spectrum[north // 2].real
    out = out.reshape(rows * cols, 2 * own, 2 * rows, 4).transpose(0, 3, 1, 2)
    return np.moveaxis(split_table(out.reshape(rows * cols, 8 * own, 2 * rows)), 0, 1)


def split(x):
    high = x.astype(BF16)
    return high, (x - high.astype(F32)).astype(BF16)


def dot(a, b, dims):
    return lax.dot_general(a, b, dims, preferred_element_type=F32)


def mul_table(x, high, low, dims=NN):
    x_high, x_low = split(x)
    return dot(x_high, high, dims) + (dot(x_low, high, dims) + dot(x_high, low, dims))


def table_mul(high, low, x, dims=NN):
    x_high, x_low = split(x)
    return dot(high, x_high, dims) + (dot(high, x_low, dims) + dot(low, x_high, dims))


def transform_list(values, sign):
    count = len(values)
    if count == 1:
        return values
    even = transform_list(values[0::2], sign)
    odd = transform_list(values[1::2], sign)
    first, second = [], []
    for k in range(count // 2):
        re, im = odd[k]
        if k == 0:
            turned = (re, im)
        elif 4 * k == count:
            turned = (im, -re) if sign < 0 else (-im, re)
        else:
            cos = float(np.cos(2.0 * np.pi * k / count))
            sin = sign * float(np.sin(2.0 * np.pi * k / count))
            if 8 * k == count or 8 * k == 3 * count:
                if cos * sin > 0:
                    turned = (cos * (re - im), cos * (re + im))
                else:
                    turned = (cos * (re + im), cos * (im - re))
            else:
                turned = (re * cos - im * sin, re * sin + im * cos)
        first.append((even[k][0] + turned[0], even[k][1] + turned[1]))
        second.append((even[k][0] - turned[0], even[k][1] - turned[1]))
    return first + second


def total(x):
    lanes = jnp.sum(jnp.sum(x, axis=0), axis=0, keepdims=True)
    return jnp.sum(lanes, axis=1, keepdims=True)


def neighbour(code, row, col, rows, cols):
    near_row = row + code // 3 - 1
    near_col = col + code % 3 - 1
    inside = (near_row >= 0) & (near_row < rows) & (near_col >= 0) & (near_col < cols)
    device = jnp.clip(near_row * cols + near_col, 0, rows * cols - 1)
    return device, inside


def near_blocks(codes, place, vector, rows, cols):
    blocks = []
    for k in range(FOOTPRINT):
        device, inside = neighbour(codes[k], place[0], place[1], rows, cols)
        blocks.append(vector[device] * jnp.where(inside, 1.0, 0.0))
    return blocks


def apply_forward(tiles, blocks, count, out):
    slots = tiles.shape[1]
    parts = tiles.shape[2] // LANES
    spread = [
        [jnp.broadcast_to(block[p : p + 1], (SUB, LANES)) for p in range(parts)] for block in blocks
    ]

    def step(t, squares):
        at = pl.multiple_of(t * SUB, SUB)
        sums = [None] * parts
        for k in range(FOOTPRINT):
            for p in range(parts):
                term = tiles[k, pl.ds(at, SUB), p * LANES : (p + 1) * LANES] * spread[k][p]
                sums[p] = term if sums[p] is None else sums[p] + term
        acc = functools.reduce(jnp.add, sums)
        slot = at + lax.broadcasted_iota(jnp.int32, (SUB, LANES), 0)
        value = jnp.where(slot < count, jnp.sum(acc, axis=1, keepdims=True), 0.0)
        if out is not None:
            out[pl.ds(at, SUB), :] = value
        return squares + value * value

    zero = jnp.zeros((SUB, LANES), F32)
    squares = lax.fori_loop(0, slots // SUB, step, zero, unroll=4)
    return jnp.sum(squares, axis=0, keepdims=True)


def apply_adjoint(tile, values, out, device):
    slots, width = tile.shape
    for p in range(width // LANES):
        sums = [None] * 4
        for t in range(slots // SUB):
            term = tile[t * SUB : (t + 1) * SUB, p * LANES : (p + 1) * LANES] * values[
                t * SUB : (t + 1) * SUB, :
            ]
            sums[t % 4] = term if sums[t % 4] is None else sums[t % 4] + term
        acc = functools.reduce(jnp.add, sums)
        out[pl.ds(device, 1), p, :] = jnp.sum(acc, axis=0, keepdims=True)


def send_adjoint(tiles, values, codes, place, out, rows, cols):
    out[...] = jnp.zeros(out.shape, F32)
    for k in range(FOOTPRINT):
        device, inside = neighbour(codes[k], place[0], place[1], rows, cols)

        @pl.when(inside)
        def _():
            apply_adjoint(tiles.at[k], values, out, device)


def start_kernel(rows, cols, codes, counts, place, readings, tile, out, values):
    k = pl.program_id(0)

    @pl.when(k == 0)
    def _():
        out[...] = jnp.zeros(out.shape, F32)
        slots = readings.shape[1]
        slot = lax.broadcasted_iota(jnp.int32, (1, slots), 1)
        live = jnp.where(slot < counts[0], readings[...], 0.0)
        for t in range(slots // LANES):
            square = jnp.broadcast_to(live[:, t * LANES : (t + 1) * LANES], (LANES, LANES))
            values[t * LANES : (t + 1) * LANES, :] = square.T

    device, inside = neighbour(codes[k], place[0], place[1], rows, cols)

    @pl.when(inside)
    def _():
        apply_adjoint(tile.at[0, 0, 0], values, out, device)


def gather_kernel(arrived, own, everywhere):
    block = jnp.sum(arrived[...], axis=0)
    own[...] = block
    everywhere[...] = jnp.broadcast_to(block[None], everywhere.shape)


def normal_kernel(rows, cols, codes, counts, place, tiles, vector, out, values):
    blocks = near_blocks(codes, place, vector, rows, cols)
    apply_forward(tiles.at[0, 0], blocks, counts[0], values)
    send_adjoint(tiles.at[0, 0], values, codes, place, out, rows, cols)


def applied_kernel(damping, arrived, own, everywhere):
    block = jnp.sum(arrived[...], axis=0) + damping[0] * own[...]
    everywhere[...] = jnp.broadcast_to(block[None], everywhere.shape)


def north_kernel(place, planes, turns, table, out):
    rows = planes.shape[0]
    re = planes[0] * turns[0, 0, 0:1]
    im = planes[0] * turns[1, 0, 0:1]
    for r in range(1, rows):
        re = re + planes[r] * turns[0, 0, r : r + 1]
        im = im + planes[r] * turns[1, 0, r : r + 1]
    both = jnp.concatenate([re, im], axis=1)
    out[...] = table_mul(table[0, 0], table[0, 1], both, NT)


def pole(north, east, trig):
    square = north * north + east * east
    inverse = jnp.where(square > 0.0, lax.rsqrt(jnp.where(square > 0.0, square, 1.0)), 0.0)
    a0 = (trig[1] * north + trig[2] * east) * inverse
    a1 = (trig[4] * north + trig[5] * east) * inverse
    v0, v1 = trig[0], trig[3]
    scale = 1.0 / ((v0 * v0 + a0 * a0) * (v1 * v1 + a1 * a1))
    return (v0 * v1 - a0 * a1) * scale, -(v0 * a1 + v1 * a0) * scale, square * inverse


def filter_kernel(rows, cols, place, trig, depth, main_re, main_im, side_re, side_im):
    _, bands, own, _ = main_re.shape
    north_len, east_len = rows * LANES, bands * LANES
    scale = 1.0 / (north_len * east_len)
    row, col = place[0], place[1]
    start = jnp.where(
        row == 0, 0, jnp.where(row == 1, rows // 2, row // 2 + HALF * rows * (row % 2))
    )

    def signed(index, length):
        return jnp.where(index < length // 2, index, index - length).astype(F32) / length

    def north_of(shape):
        index = start + rows * (col * own + lax.broadcasted_iota(jnp.int32, shape, 0))
        return signed(index, north_len)

    def weights(re, im, radius):
        damp = [None] + [jnp.exp(radius * (-2.0 * np.pi * depth[l])) for l in range(LAYERS)]
        return [(re, im) if d is None else (re * d, im * d) for d in damp]

    lane = lax.broadcasted_iota(jnp.int32, (own, LANES), 1)
    north = north_of((own, LANES))
    for band in range(bands):
        east = signed(band + bands * lane, east_len)
        re, im, radius = pole(north, east, trig)
        if band == 0:
            re2, im2, _ = pole(north, jnp.where(lane == HALF, 0.5, east), trig)
            re, im = 0.5 * (re + re2), 0.5 * (im + im2)
        for q, (wr, wi) in enumerate(weights(re * scale, im * scale, radius)):
            main_re[q, band] = wr
            main_im[q, band] = wi
    side_re[...] = jnp.zeros(side_re.shape, F32)
    side_im[...] = jnp.zeros(side_im.shape, F32)

    @pl.when((row == 0) & (col == 0))
    def _():
        band = lax.broadcasted_iota(jnp.int32, (bands, LANES), 0)
        lanes = lax.broadcasted_iota(jnp.int32, (bands, LANES), 1)
        east = signed(band + bands * lanes, east_len)
        flipped = jnp.where((band == 0) & (lanes == HALF), 0.5, east)
        pairs = []
        for one, other in ((0.0, 0.0), (-0.5, 0.5)):
            re, im, radius = pole(jnp.full_like(east, one), east, trig)
            re2, im2, _ = pole(jnp.full_like(east, other), flipped, trig)
            half = 0.5 * scale
            pairs.append(weights(half * (re + re2), half * (im + im2), radius))
        for q in range(1 + LAYERS):
            (r0, i0), (r1, i1) = pairs[0][q], pairs[1][q]
            side_re[q] = 0.5 * (r0 - r1)
            side_im[q] = 0.5 * (i0 - i1)
            for b in range(bands):
                main_re[q, b, 0:1, :] = 0.5 * (r0 + r1)[b : b + 1]
                main_im[q, b, 0:1, :] = 0.5 * (i0 + i1)[b : b + 1]


def east_forward(get, own, bands, turns, table, work):
    for g in range(own // SUB):
        values = transform_list([get(m, g) for m in range(bands)], -1.0)
        for b in range(bands):
            cos, sin = turns[0, b : b + 1, :], turns[1, b : b + 1, :]
            re, im = values[b]
            at = b * own + g * SUB
            work[at : at + SUB, :LANES] = re * cos - im * sin
            work[at : at + SUB, LANES:] = re * sin + im * cos
            if g == 0:
                re, im = values[(bands - b) % bands]
                re, im = re[0:1], -im[0:1]
                at = bands * own + b
                work[at : at + 1, :LANES] = re * cos - im * sin
                work[at : at + 1, LANES:] = re * sin + im * cos
    return mul_table(work[...], table[0], table[1])


def weigh(spectrum, q, own, bands, main_re, main_im, side_re, side_im, into, first):
    rows = own * bands
    re, im = spectrum[:rows, :LANES], spectrum[:rows, LANES:]
    wr = main_re[q].reshape(rows, LANES)
    wi = main_im[q].reshape(rows, LANES)
    out_re, out_im = re * wr - im * wi, re * wi + im * wr
    if first:
        into[:, :LANES] = out_re
        into[:, LANES:] = out_im
    else:
        into[:, :LANES] += out_re
        into[:, LANES:] += out_im
    re, im = spectrum[rows:, :LANES], spectrum[rows:, LANES:]
    wr, wi = side_re[q], side_im[q]
    add_re, add_im = re * wr - im * wi, re * wi + im * wr
    for b in range(bands):
        into[b * own : b * own + 1, :LANES] += add_re[b : b + 1]
        into[b * own : b * own + 1, LANES:] += add_im[b : b + 1]


def east_inverse(spectrum, own, bands, turns, table, work, store):
    work[...] = mul_table(spectrum[...], table[0], table[1])
    for g in range(own // SUB):
        values = []
        for b in range(bands):
            at = b * own + g * SUB
            re, im = work[at : at + SUB, :LANES], work[at : at + SUB, LANES:]
            cos, sin = turns[0, b : b + 1, :], turns[1, b : b + 1, :]
            values.append((re * cos + im * sin, im * cos - re * sin))
        values = transform_list(values, 1.0)
        for b in range(bands):
            store(b, g, *values[b])


def store_pieces(out, base, width):
    per_band = LANES // width

    def store(band, g, re, im):
        for s in range(per_band):
            cut = slice(s * width, (s + 1) * width)
            piece = jnp.concatenate([re[:, cut], im[:, cut]], axis=1)
            at = base + 2 * g
            out[band * per_band + s, at] = piece[:4]
            out[band * per_band + s, at + 1] = piece[4:]

    return store


def model_rows(vector, hats, rows, cols, coarse):
    own2 = hats.shape[1] // 4
    for i in range(rows):
        for j in range(cols):
            block = vector[i * cols + j]
            for layer in range(LAYERS):
                coarse[layer, 2 * i : 2 * i + 2, j * LANES : (j + 1) * LANES] = block[
                    2 * layer : 2 * layer + 2
                ]
    out = []
    tiles = cols * SRC_COLS // LANES
    lane = lax.broadcasted_iota(jnp.int32, (own2, LANES), 1) // SRC_COLS
    for layer in range(LAYERS):
        mixed = table_mul(hats[0], hats[1], coarse[layer])
        whole = []
        for tile in range(tiles):
            joined = None
            for place in range(LANES // SRC_COLS):
                j = tile * (LANES // SRC_COLS) + place
                summed = None
                for part in range(4):
                    piece = mixed[part * own2 : (part + 1) * own2, j * LANES : (j + 1) * LANES]
                    shift = ((place - part) * SRC_COLS) % LANES
                    if shift:
                        piece = pltpu.roll(piece, shift, 1)
                    summed = piece if summed is None else summed + piece
                joined = summed if joined is None else jnp.where(lane == place, summed, joined)
            whole.append(joined)
        out.append(whole[0] if tiles == 1 else jnp.concatenate(whole, axis=1))
    return out


def model_spectra(
    vector, hats, up_east, rows, cols, own, bands, turns, table, coarse, fine, work
):
    planes = model_rows(vector, hats, rows, cols, coarse)
    high, low = split(jnp.concatenate(planes, axis=0))
    fine[...] = dot(high, up_east[...], NN) + dot(low, up_east[...], NN)
    for layer in range(LAYERS):

        def get(m, g, base=2 * own * layer):
            at = base + g * SUB
            cut = slice(m * LANES, (m + 1) * LANES)
            return fine[at : at + SUB, cut], fine[at + own : at + own + SUB, cut]

        yield 1 + layer, east_forward(get, own, bands, turns, table, work)


def early_kernel(
    rows, cols, width, place, spec_re, spec_im, vector, hats, up_east, turns, forward, inverse,
    main_re, main_im, side_re, side_im, out_resid, out_first, coarse, fine, work, mixed, back,
):
    _, bands, own, _ = main_re.shape
    per = spec_re.shape[2] // LANES

    def get(m, g):
        cut = slice((m % per) * LANES, (m % per + 1) * LANES)
        at = slice(g * SUB, (g + 1) * SUB)
        return spec_re[m // per, at, cut], spec_im[m // per, at, cut]

    sides = (main_re, main_im, side_re, side_im)
    spectrum = east_forward(get, own, bands, turns, forward, work)
    weigh(spectrum, 0, own, bands, *sides, mixed, True)
    east_inverse(mixed, own, bands, turns, inverse, back, store_pieces(out_resid, 0, width))
    for q, spectrum in model_spectra(
        vector, hats[0], up_east, rows, cols, own, bands, turns, forward, coarse, fine, work
    ):
        weigh(spectrum, q, own, bands, *sides, mixed, q == 1)
    east_inverse(mixed, own, bands, turns, inverse, back, store_pieces(out_first, 0, width))


def late_kernel(
    rows, cols, width, codes, counts, place, damping, tiles, first, applied, early, early_first,
    hats, up_east, turns, forward, inverse, main_re, main_im, side_re, side_im,
    out, own_first, own_second, stats, second, coarse, fine, work, mixed, back,
):
    _, bands, own, _ = main_re.shape
    groups = own // 4
    norm = total(first[...] * first[...])
    step = norm / total(first[...] * applied[...])
    residual = first[...] - step[None] * applied[...]
    norm_next = total(residual * residual)
    second[...] = residual + (norm_next / norm)[None] * first[...]
    ridge = damping[0] * total(second[...] * second[...])
    me = place[0] * cols + place[1]
    own_first[...] = step * first[me]
    own_second[...] = second[me]
    stats[0] = jnp.broadcast_to(norm_next, stats.shape[1:])
    stats[1] = jnp.broadcast_to(ridge, stats.shape[1:])

    blocks = near_blocks(codes, place, second, rows, cols)
    squares = apply_forward(tiles.at[0, 0], blocks, counts[0], None)
    out[:, 2 * groups] = jnp.broadcast_to(
        squares[None, :, : out.shape[3]], (out.shape[0], 4, out.shape[3])
    )
    out[:, :groups] = early[...] + step[None, None] * early_first[...]
    sides = (main_re, main_im, side_re, side_im)
    for q, spectrum in model_spectra(
        second, hats[0], up_east, rows, cols, own, bands, turns, forward, coarse, fine, work
    ):
        weigh(spectrum, q, own, bands, *sides, mixed, q == 1)
    east_inverse(mixed, own, bands, turns, inverse, back, store_pieces(out, groups, width))


def finish_kernel(
    rows, cols, arrived, own_first, own_second, stats, turns, table, coefficients, out, mixed, waves
):
    groups = (arrived.shape[1] - 1) // 2
    width = out.shape[0]
    own = 4 * groups
    measured = jnp.sum(arrived[:, 2 * groups], axis=0)[0:1, 0:1]
    step = stats[0, 0:1, 0:1] / (measured + stats[1, 0:1, 0:1])
    solved = own_first[...] + step * own_second[...]
    for p in range(solved.shape[0]):
        coefficients[:, p * LANES : (p + 1) * LANES] = solved[p : p + 1]
    for i in range(rows):
        for j in range(cols):
            source = i * cols + j
            for q in range(groups):
                at = j * own + 4 * q
                mixed[i, at : at + 4, :] = (
                    arrived[source, q] + step * arrived[source, groups + q]
                )
        kind = min(i, 1)
        both = mul_table(mixed[i], table[kind, 0], table[kind, 1], TN)
        top, bottom = both[:width], both[width:]
        waves[i, :, :LANES] = top[:, :LANES] - bottom[:, LANES:]
        waves[i, :, LANES:] = top[:, LANES:] + bottom[:, :LANES]
    for at in range(0, width, SUB):
        parts = [None] * rows
        for i in range(rows):
            re = waves[i, at : at + SUB, :LANES]
            im = waves[i, at : at + SUB, LANES:]
            for n in range(rows):
                term = re * turns[0, i, n : n + 1] + im * turns[1, i, n : n + 1]
                parts[n] = term if i == 0 else parts[n] + term
        for n in range(rows):
            out[at : at + SUB, n * LANES : (n + 1) * LANES] = parts[n]


def shape(*dims):
    return jax.ShapeDtypeStruct(dims, F32)


def scratch(*dims):
    return pltpu.VMEM(dims, F32)


def call(kernel, outs, ins, work=(), **grid):
    if not grid:
        grid = dict(in_specs=[spec for spec, _ in ins], out_specs=jax.tree.map(lambda _: VMEM, outs))
    return pl.pallas_call(
        kernel,
        out_shape=outs,
        scratch_shapes=list(work),
        compiler_params=pltpu.CompilerParams(vmem_limit_bytes=VMEM_BYTES),
        **grid,
    )(*[value for _, value in ins])


def exchange(pieces):
    return lax.all_to_all(pieces, BOTH, 0, 0, tiled=True)


def on_device(
    kernel_tiles, footprints, counts, readings, damping, layer_depth, inclinations, declinations,
    resid_grid,
):
    rows, cols = lax.axis_size("row"), lax.axis_size("col")
    devices = rows * cols
    row, col = lax.axis_index("row"), lax.axis_index("col")
    place = jnp.stack([row, col]).astype(jnp.int32)
    codes, counts = footprints.reshape(-1), counts.reshape(-1)
    _, _, _, slots, sources = kernel_tiles.shape
    parts = sources // LANES
    tile_east = resid_grid.shape[0]
    east = cols * tile_east
    bands = east // LANES
    own = HALF // cols
    width = east // devices
    groups = own // 4

    turns = north_turns(rows)
    east_table, back_table, east_turns = east_tables(east)
    hats = north_hat_table(rows, cols)
    up_east = hat_table(east, cols * SRC_COLS).T.astype(ml_dtypes.bfloat16)

    planes = lax.all_gather(resid_grid, "row", axis=0)

    tile_shape = (1, 1, 1, slots, sources)
    partial_sums = call(
        functools.partial(start_kernel, rows, cols),
        shape(devices, parts, LANES),
        [(None, codes), (None, counts), (None, place), (None, readings.reshape(1, slots)), (None, kernel_tiles)],
        [scratch(slots, LANES)],
        grid=(FOOTPRINT,),
        in_specs=[SMEM, SMEM, SMEM, VMEM, pl.BlockSpec(tile_shape, lambda k: (0, 0, k, 0, 0))],
        out_specs=VMEM,
    )
    right_own, right_all = call(
        gather_kernel,
        (shape(parts, LANES), shape(devices, parts, LANES)),
        [(VMEM, exchange(partial_sums))],
    )
    right_side = exchange(right_all)
    partial_sums = call(
        functools.partial(normal_kernel, rows, cols),
        shape(devices, parts, LANES),
        [(SMEM, codes), (SMEM, counts), (SMEM, place), (VMEM, kernel_tiles), (VMEM, right_side)],
        [scratch(slots, LANES)],
    )

    trig = []
    for m in range(2):
        flat = jnp.cos(inclinations[m])
        trig += [jnp.sin(inclinations[m]), flat * jnp.cos(declinations[m]), flat * jnp.sin(declinations[m])]
    sides = call(
        functools.partial(filter_kernel, rows, cols),
        (shape(3, bands, own, LANES),) * 2 + (shape(3, bands, LANES),) * 2,
        [(SMEM, place), (SMEM, jnp.stack(trig)), (SMEM, layer_depth)],
    )

    chunk = LANES
    spectrum = pl.pallas_call(
        north_kernel,
        out_shape=shape(2 * HALF, tile_east),
        grid_spec=pltpu.PrefetchScalarGridSpec(
            num_scalar_prefetch=1,
            grid=(tile_east // chunk,),
            in_specs=[
                pl.BlockSpec((rows, chunk, LANES), lambda c, at: (0, c, 0)),
                pl.BlockSpec((2, 1, rows, LANES), lambda c, at: (0, at[0], 0, 0)),
                pl.BlockSpec((1, 2, 2 * HALF, 2 * LANES), lambda c, at: (jnp.minimum(at[0], 1), 0, 0, 0)),
            ],
            out_specs=pl.BlockSpec((2 * HALF, chunk), lambda c, at: (0, c)),
        ),
        compiler_params=pltpu.CompilerParams(vmem_limit_bytes=VMEM_BYTES),
    )(place, planes, turns, north_forward_table())
    spectrum = lax.all_gather(spectrum, "col", axis=0)

    applied_all = call(
        applied_kernel,
        shape(devices, parts, LANES),
        [(SMEM, damping), (VMEM, exchange(partial_sums)), (VMEM, right_own)],
    )
    applied = exchange(applied_all)

    work = [
        scratch(LAYERS, 2 * rows, cols * LANES),
        scratch(LAYERS * 2 * own, east),
        scratch((own + 1) * bands, 2 * LANES),
        scratch(own * bands, 2 * LANES),
        scratch(own * bands, 2 * LANES),
    ]
    full = pl.BlockSpec((None,) * 0)
    whole = lambda a: pl.BlockSpec(a.shape, lambda _, at, n=a.ndim: (0,) * n)
    mine = pl.BlockSpec((1,) + hats.shape[1:], lambda _, at: (at[0] * cols + at[1], 0, 0, 0))
    del full
    pieces = shape(devices, groups, 4, 2 * width)
    early, early_first = pl.pallas_call(
        functools.partial(early_kernel, rows, cols, width),
        out_shape=(pieces, pieces),
        grid_spec=pltpu.PrefetchScalarGridSpec(
            num_scalar_prefetch=1,
            grid=(1,),
            in_specs=[
                pl.BlockSpec((cols, own, tile_east), lambda _, at: (0, at[1], 0)),
                pl.BlockSpec((cols, own, tile_east), lambda _, at: (0, cols + at[1], 0)),
                whole(right_side),
                mine,
                whole(up_east),
                whole(east_turns),
                whole(east_table),
                whole(back_table),
            ]
            + [whole(side) for side in sides],
            out_specs=(whole(pieces),) * 2,
            scratch_shapes=work,
        ),
        compiler_params=pltpu.CompilerParams(vmem_limit_bytes=VMEM_BYTES),
    )(place, spectrum, spectrum, right_side, hats, up_east, east_turns, east_table, back_table, *sides)

    late_out = (
        shape(devices, 2 * groups + 1, 4, 2 * width),
        shape(parts, LANES),
        shape(parts, LANES),
        shape(2, SUB, LANES),
    )
    my_hats = lax.dynamic_index_in_dim(jnp.asarray(hats), row * cols + col, 0, keepdims=True)
    pieces, own_first, own_second, stats = call(
        functools.partial(late_kernel, rows, cols, width),
        late_out,
        [
            (SMEM, codes),
            (SMEM, counts),
            (SMEM, place),
            (SMEM, damping),
            (VMEM, kernel_tiles),
            (VMEM, right_side),
            (VMEM, applied),
            (VMEM, early),
            (VMEM, early_first),
            (VMEM, my_hats),
            (VMEM, up_east),
            (VMEM, east_turns),
            (VMEM, east_table),
            (VMEM, back_table),
        ]
        + [(VMEM, side) for side in sides],
        [scratch(devices, parts, LANES)] + work,
    )
    coefficients, rtp_map = call(
        functools.partial(finish_kernel, rows, cols),
        (shape(1, sources), shape(width, rows * LANES)),
        [
            (VMEM, exchange(pieces)),
            (VMEM, own_first),
            (VMEM, own_second),
            (VMEM, stats),
            (VMEM, turns),
            (VMEM, north_inverse_table()),
        ],
        [scratch(rows, HALF, 2 * width), scratch(rows, width, 2 * LANES)],
    )
    return coefficients.reshape(1, 1, sources), rtp_map


def solution(mesh):
    in_specs = (
        P("row", "col", None, None, None),
        P("row", "col", None),
        P("row", "col"),
        P("row", "col", None),
        P(),
        P(),
        P(),
        P(),
        P("col", "row"),
    )
    out_specs = (P("row", "col", None), P(("row", "col"), None))
    return jax.shard_map(
        on_device, mesh=mesh, in_specs=in_specs, out_specs=out_specs, check_vma=False
    )
```

time: 526 us -> 157 us (0.30); the launches traced: 516 us -> 155 us
  starting transfers between devices: 184 us -> 5.19 us
  blocking collectives: 134 us -> 44.8 us
  matrix products: 52.2 us -> 0 us
  waiting for transfers between devices: 66.2 us -> 39.4 us
  local copies, waits for them, and re-layouts: 49.4 us -> 27.8 us
  Pallas kernels: 0 us -> 16.3 us
  other arithmetic: 14.3 us -> 0.08 us
  between operations: 15.6 us -> 21.2 us
    ppermute x48 -> x0, starting transfers between devices: 162 us -> none  [shifted(): return lax.ppermute(x, axis, pairs)]
    psum x2 -> x0, blocking collectives: 97.5 us -> none  [two_products(): lax.psum((jnp.sum(residual * residual), jnp.sum(residual * applied)), ('r...]
    dot_general x40 -> x0, matrix products: 52.2 us -> none  [the longest x2 12.3 us: forward(): jnp.einsum('krs,ks->r', kernels, chosen, precision=HIGHEST_PRECISION)]
    all_to_all x3 -> x2, waiting for transfers between devices: 57.5 us -> 6.19 us  [exchange(): return lax.all_to_all(pieces, BOTH, 0, 0, tiled=True)]
    all_gather x0 -> x2, waiting for transfers between devices: none -> 32.5 us  [the longest x1 32.5 us: on_device(): planes = lax.all_gather(resid_grid, 'row', axis=0)]
    all_to_all x3 -> x2, starting transfers between devices: 22 us -> 5.11 us  [exchange(): return lax.all_to_all(pieces, BOTH, 0, 0, tiled=True)]
    pallas_call x0 -> x9, Pallas kernels: none -> 16.3 us  [the longest x7 10.7 us: call(): pl.pallas_call(kernel, out_shape=outs, scratch_shapes=list(work), compile...]
    unnamed x21 -> x76, local copies, waits for them, and re-layouts: 13.2 us -> 25.2 us
  transfers between devices with their start and end apart: 51 -> 4, of which waited for: 9 -> 2; matrix products, arithmetic and copies ran while one was open for 0% -> 2% of each run, Pallas kernels for 0% -> 5%
where the time goes in v1:
time: 157 us; the launch traced here: 155 us
  blocking collectives  44.8 us (29%)
  waiting for transfers between devices  39.4 us (25%)
  local copies, waits for them, and re-layouts  27.8 us (18%)
  between operations  21.2 us (14%)
  Pallas kernels  16.3 us (10%)
  starting transfers between devices  5.19 us (3%)
    all_to_all x3, blocking collectives, exchange(): return lax.all_to_all(pieces, BOTH, 0, 0, tiled=True)  44.8 us
    all_gather x1, waiting for transfers between devices, on_device(): planes = lax.all_gather(resid_grid, 'row', axis=0)  32.5 us
    unnamed x76, local copies, waits for them, and re-layouts  25.2 us
    pallas_call x7, Pallas kernels, call(): pl.pallas_call(kernel, out_shape=outs, scratch_shapes=list(work), compile...  10.7 us
    all_to_all x2, waiting for transfers between devices, exchange(): return lax.all_to_all(pieces, BOTH, 0, 0, tiled=True)  6.19 us
    all_to_all x2, starting transfers between devices, exchange(): return lax.all_to_all(pieces, BOTH, 0, 0, tiled=True)  5.11 us
  transfers between devices with their start and end apart: 4, of which 2 were waited for; matrix products, arithmetic and copies ran while one was open for 2% of the time, Pallas kernels for 5%

profile of v1, /device:TPU:0, one launch (start us, length us, event | category | flops | bytes accessed | tf_op | source)
XLA Modules:
  0.0 154.8 jit_solution(7162734142034288801)
XLA Ops:
  7.2 0.7 all-gather.5.cloned.1.call-update
  8.0 0.1 pad_add_fusion.place
  8.0 32.5 %all-gather.5.cloned.1.call-done = f32[4096,128]{1,0:T(8,128)} async-done(((f32[512,128]{1,0:T(8,128)}), f32[4096,128]{1,0:T(8,128)}) %all-gather.5.cloned.1.call-update) | async-done | bytes 2097168 | tf_op jit(solution)/shard_map/all_gather | solution.py:593
  40.5 1.6 %copy-done.5 = f32[4096,128]{1,0:T(8,128)S(1)} copy-done((f32[4096,128]{1,0:T(8,128)S(1)}, f32[4096,128]{1,0:T(8,128)}, u32[]{:S(2)}) %copy-start.5) | copy-done | bytes 2097176
  42.1 0.9 copy-done.12
  43.1 0.8 copy-done.17
  43.9 2.8 %shard_map.180 = f32[128,512]{1,0:T(8,128)} custom-call(s32[2]{0:T(128)S(1)} %pad_add_fusion.place, f32[8,512,128]{2,1,0:T(8,128)S(1)} %bitcast.13, f32[2,8,8,128]{3,2,1,0:T(8,128)S(1)} %copy-done.17, bf16[2,2,128,256]{3,2,1,0:T(8,128)(2,1)S(1)} %copy-done.12), custom_call_target="tpu_custom_call" | custom-call | tf_op jit(solution)/shard_map/pallas_call | solution.py:629
  47.4 2.3 %copy-done = f32[1,1,9,256,512]{4,3,2,1,0:T(8,128)S(1)} copy-done((f32[1,1,9,256,512]{4,3,2,1,0:T(8,128)S(1)}, f32[1,1,9,256,512]{4,3,2,1,0:T(8,128)}, u32[]{:S(2)}) %copy-start) | copy-done | bytes 4718616
  49.7 1.3 shard_map.176
  51.0 13.0 %all_to_all.25.arrived = f32[32,4,128]{2,1,0:T(4,128)S(1)} all-to-all(f32[32,4,128]{2,1,0:T(4,128)S(1)} %shard_map.176), channel_id=1, replica_groups=mesh['row'=8,'col'=4] {'row','col'}, dimensions={0} | all-to-all | bytes 131072 | tf_op jit(solution)/shard_map/all_to_all | solution.py:567
  64.1 10.5 %all_to_all.26.vector.first = f32[32,4,128]{2,1,0:T(4,128)S(1)} all-to-all(f32[32,4,128]{2,1,0:T(4,128)S(1)} %get-tuple-element.16), channel_id=1, replica_groups=mesh['row'=8,'col'=4] {'row','col'}, dimensions={0} | all-to-all | bytes 131072 | tf_op jit(solution)/shard_map/all_to_all | solution.py:567
  74.7 2.6 %shard_map.178 = f32[32,4,128]{2,1,0:T(4,128)} custom-call(s32[9]{0:T(128)S(1)} %bitcast.15, s32[1]{0:T(128)} %bitcast.9.counts, s32[2]{0:T(128)S(1)} %pad_add_fusion.place, f32[1,1,9,256,512]{4,3,2,1,0:T(8,128)S(1)} %copy-done.1, f32[32,4,128]{2,1,0:T(4,128)S(1)} %all_to_all.26.vector.first), custom_call_target="tpu_custom_call" | custom-call | tf_op jit(solution)/shard_map/pallas_call | solution.py:557
  77.3 2.6 %all-to-all-start.2 = ((f32[32,4,128]{2,1,0:T(4,128)}), f32[32,4,128]{2,1,0:T(4,128)S(1)}, u32[]{:S(2)}, u32[]{:S(2)}) async-start(f32[32,4,128]{2,1,0:T(4,128)} %shard_map.178), calls=%async_computation.2 | async-start | bytes 131072 | tf_op jit(solution)/shard_map/all_to_all | solution.py:567
  80.5 0.7 fusion.1
  81.2 6.2 %all-to-all-done.2.arrived = f32[32,4,128]{2,1,0:T(4,128)S(1)} async-done(((f32[32,4,128]{2,1,0:T(4,128)}), f32[32,4,128]{2,1,0:T(4,128)S(1)}, u32[]{:S(2)}, u32[]{:S(2)}) %all-to-all-start.2) | async-done | bytes 65568 | tf_op jit(solution)/shard_map/all_to_all | solution.py:567
  87.4 0.7 shard_map.179
  88.1 2.6 %all-to-all-start.3 = ((f32[32,4,128]{2,1,0:T(4,128)}), f32[32,4,128]{2,1,0:T(4,128)S(1)}, u32[]{:S(2)}, u32[]{:S(2)}) async-start(f32[32,4,128]{2,1,0:T(4,128)} %shard_map.179), calls=%async_computation.3 | async-start | bytes 131072 | tf_op jit(solution)/shard_map/all_to_all | solution.py:567
  90.6 0.6 fusion
  96.9 0.7 stack.21.trig
  97.6 0.6 copy-done.28
  98.2 0.7 copy-done.34
  98.9 0.7 copy-done.35
  99.5 0.8 shard_map.181
  100.3 0.6 copy-done.20
  100.9 0.6 copy-done.23
  101.6 0.6 constant_dynamic-slice_fusion.hats
  102.2 1.2 copy-done.3
  103.4 0.9 copy-done.7
  104.4 0.9 copy-done.9
  105.3 0.7 copy-done.21
  106.1 0.7 copy-done.24
  106.8 0.6 copy-done.29
  107.4 2.9 %shard_map.182 = (f32[32,4,4,128]{3,2,1,0:T(4,128)S(1)}, f32[32,4,4,128]{3,2,1,0:T(4,128)S(1)}) custom-call(s32[2]{0:T(128)S(1)} %copy-done.29, f32[4,128,512]{2,1,0:T(8,128)S(1)} %bitcast.11, f32[4,128,512]{2,1,0:T(8,128)S(1)} %bitcast.12, f32[32,4,128]{2,1,0:T(4,128)S(1)} %all_to_all.26.vector.first, bf16[32,2,128,16]{3,2,1,0:T(8,128)(2,1)S(1)} %copy-done.4, ...), custom_call_target="tpu_custom_call" | custom-call | tf_op jit(solution)/shard_map/pallas_call | solution.py:665
  110.3 0.7 copy-done.13
  111.0 0.7 copy-done.15
  111.7 2.3 %copy-done.2 = f32[1,1,9,256,512]{4,3,2,1,0:T(8,128)S(1)} copy-done((f32[1,1,9,256,512]{4,3,2,1,0:T(8,128)S(1)}, f32[1,1,9,256,512]{4,3,2,1,0:T(8,128)}, u32[]{:S(2)}) %copy-start.2) | copy-done | bytes 4718616
  114.1 0.9 copy-done.8
  115.0 0.9 copy-done.10
  116.0 0.8 copy-done.11
  116.8 0.9 copy-done.14
  117.8 0.9 copy-done.16
  118.7 0.7 copy-done.22
  119.4 0.7 copy-done.25
  120.2 0.6 copy-done.30
  120.8 0.7 copy-done.32
  121.4 3.8 %shard_map.183 = (f32[32,9,4,128]{3,2,1,0:T(4,128)S(1)}, f32[4,128]{1,0:T(4,128)S(1)}, f32[4,128]{1,0:T(4,128)S(1)}, f32[2,8,128]{2,1,0:T(8,128)S(1)}) custom-call(s32[9]{0:T(128)S(1)} %bitcast.16, s32[1]{0:T(128)} %bitcast.10.counts, s32[2]{0:T(128)S(1)} %copy-done.30, f32[1]{0:T(128)S(6)} %copy.20.damping, f32[1,1,9,256,512]{4,3,2,1,0:T(8,128)S(1)} %copy-done.2, ...), custom_call_target="tpu_custom_call" | custom-call | tf_op jit(solution)/shard_map/pallas_call | solution.py:557
  125.2 21.2 %all_to_all.27.arrived = f32[32,9,4,128]{3,2,1,0:T(4,128)S(1)} all-to-all(f32[32,9,4,128]{3,2,1,0:T(4,128)S(1)} %get-tuple-element.24), channel_id=1, replica_groups=mesh['row'=8,'col'=4] {'row','col'}, dimensions={0} | all-to-all | bytes 1179648 | tf_op jit(solution)/shard_map/all_to_all | solution.py:567
  146.5 1.5 shard_map.184
  (55 shorter events, 0.2 us)
Async XLA Ops:
  7.2 40.2 %copy-start.31 = (s32[1,1,9]{2,1,0:T(1,128)S(1)}, s32[1,1,9]{2,1,0:T(1,128)}, u32[]{:S(2)}) copy-start(s32[1,1,9]{2,1,0:T(1,128)} %param.18) | copy-start | bytes 112
  7.2 40.2 %copy-start.33 = (f32[1,1,256]{2,1,0:T(1,128)S(1)}, f32[1,1,256]{2,1,0:T(1,128)}, u32[]{:S(2)}) copy-start(f32[1,1,256]{2,1,0:T(1,128)} %param.20) | copy-start | bytes 3076
  7.2 33.4 %all-gather.5.cloned.1.call-start = ((), (), s32[]{:S(2)}) async-start(), calls=%async_computation.5 | async-start | bytes 2359296 | tf_op jit(solution)/shard_map/all_gather | solution.py:593
  7.9 94.3 %all-gather.7.cloned.1.call-start = ((), (), s32[]{:S(2)}) async-start(), calls=%async_computation.6 | async-start | bytes 1310720 | tf_op jit(solution)/shard_map/all_gather | solution.py:644
  8.0 66.6 %copy-start.27 = (s32[2]{0:T(128)}, s32[2]{0:T(128)S(1)}, u32[]{:S(2)}) copy-start(s32[2]{0:T(128)S(1)} %pad_add_fusion.place) | copy-start | bytes 28
  40.5 1.6 %copy-start.5 = (f32[4096,128]{1,0:T(8,128)S(1)}, f32[4096,128]{1,0:T(8,128)}, u32[]{:S(2)}) copy-start(f32[4096,128]{1,0:T(8,128)} %all-gather.5.cloned.1.call-done) | copy-start | bytes 6291460
  42.1 0.9 copy-start.12
  43.1 0.8 copy-start.17
  47.4 2.3 %copy-start = (f32[1,1,9,256,512]{4,3,2,1,0:T(8,128)S(1)}, f32[1,1,9,256,512]{4,3,2,1,0:T(8,128)}, u32[]{:S(2)}) copy-start(f32[1,1,9,256,512]{4,3,2,1,0:T(8,128)} %tiles.3) | copy-start | bytes 14155780
  49.7 24.9 %copy-start.1 = (f32[1,1,9,256,512]{4,3,2,1,0:T(8,128)S(1)}, f32[1,1,9,256,512]{4,3,2,1,0:T(8,128)}, u32[]{:S(2)}) copy-start(f32[1,1,9,256,512]{4,3,2,1,0:T(8,128)} %tiles.3) | copy-start | bytes 14155780
  74.7 5.9 %copy-start.36 = (f32[2]{0:T(128)S(1)}, f32[2]{0:T(128)}, u32[]{:S(2)}) copy-start(f32[2]{0:T(128)} %param.23) | copy-start | bytes 28
  74.7 16.0 %copy-start.37 = (f32[2]{0:T(128)S(1)}, f32[2]{0:T(128)}, u32[]{:S(2)}) copy-start(f32[2]{0:T(128)} %param.24) | copy-start | bytes 28
  74.7 26.9 %copy-start.4 = (bf16[32,2,128,16]{3,2,1,0:T(8,128)(2,1)S(1)}, bf16[32,2,128,16]{3,2,1,0:T(8,128)(2,1)}, u32[]{:S(2)}) copy-start(bf16[32,2,128,16]{3,2,1,0:T(8,128)(2,1)} %constant.35.clone.hats) | copy-start | bytes 786436
  74.7 27.5 %copy-start.6 = (bf16[128,2048]{1,0:T(8,128)(2,1)S(1)}, bf16[128,2048]{1,0:T(8,128)(2,1)}, u32[]{:S(2)}) copy-start(bf16[128,2048]{1,0:T(8,128)(2,1)} %constant.36.clone.up_east) | copy-start | bytes 1572868
  74.7 27.5 %copy-start.26 = (f32[2,16,128]{2,1,0:T(8,128)S(1)}, f32[2,16,128]{2,1,0:T(8,128)}, u32[]{:S(2)}) copy-start(f32[2,16,128]{2,1,0:T(8,128)} %constant.37.clone.turns) | copy-start | bytes 49156
  77.3 10.1 %all-to-all-start.2 = ((f32[32,4,128]{2,1,0:T(4,128)}), f32[32,4,128]{2,1,0:T(4,128)S(1)}, u32[]{:S(2)}, u32[]{:S(2)}) async-start(f32[32,4,128]{2,1,0:T(4,128)} %shard_map.178), calls=%async_computation.2 | async-start | bytes 131072 | tf_op jit(solution)/shard_map/all_to_all | solution.py:567
  88.1 23.7 %all-to-all-start.3 = ((f32[32,4,128]{2,1,0:T(4,128)}), f32[32,4,128]{2,1,0:T(4,128)S(1)}, u32[]{:S(2)}, u32[]{:S(2)}) async-start(f32[32,4,128]{2,1,0:T(4,128)} %shard_map.179), calls=%async_computation.3 | async-start | bytes 131072 | tf_op jit(solution)/shard_map/all_to_all | solution.py:567
  97.6 0.6 copy-start.28
  98.2 0.7 copy-start.34
  98.9 0.7 copy-start.35
  100.3 0.6 copy-start.20
  100.9 0.6 copy-start.23
  102.2 1.2 copy-start.3
  103.4 0.9 copy-start.7
  104.4 0.9 copy-start.9
  105.3 0.7 copy-start.21
  106.1 0.7 copy-start.24
  106.8 0.6 copy-start.29
  110.3 0.7 copy-start.13
  111.0 0.7 copy-start.15
  111.7 2.3 %copy-start.2 = (f32[1,1,9,256,512]{4,3,2,1,0:T(8,128)S(1)}, f32[1,1,9,256,512]{4,3,2,1,0:T(8,128)}, u32[]{:S(2)}) copy-start(f32[1,1,9,256,512]{4,3,2,1,0:T(8,128)} %tiles.3) | copy-start | bytes 14155780
  114.1 0.9 copy-start.8
  115.0 0.9 copy-start.10
  116.0 0.8 copy-start.11
  116.8 0.9 copy-start.14
  117.8 0.9 copy-start.16
  118.7 0.7 copy-start.22
  119.4 0.7 copy-start.25
  120.2 0.6 copy-start.30
  120.8 0.7 copy-start.32
  121.4 25.0 %copy-start.18 = (f32[2,8,8,128]{3,2,1,0:T(8,128)S(1)}, f32[2,8,8,128]{3,2,1,0:T(8,128)}, u32[]{:S(2)}) copy-start(f32[2,8,8,128]{3,2,1,0:T(8,128)} %constant.33.clone.turns) | copy-start | bytes 196612
  121.4 25.0 %copy-start.19 = (bf16[2,2,64,256]{3,2,1,0:T(8,128)(2,1)S(1)}, bf16[2,2,64,256]{3,2,1,0:T(8,128)(2,1)}, u32[]{:S(2)}) copy-start(bf16[2,2,64,256]{3,2,1,0:T(8,128)(2,1)} %constant.40.clone.table) | copy-start | bytes 393220
Sparse Core Ops, SparseCore 0:
  9.9 30.5 all-gather.4
  46.8 31.2 all-gather.6

commit v2 on v1

v2 whole, which is shorter than its diff:
```python
import functools

import jax
import jax.numpy as jnp
import ml_dtypes
import numpy as np
from jax import lax
from jax.experimental import pallas as pl
from jax.experimental.pallas import tpu as pltpu
from jax.sharding import PartitionSpec as P

SRC_ROWS = 8
SRC_COLS = 32
LAYERS = 2
REFINE = 16
FOOTPRINT = 9
LANES = 128
SUB = 8
HALF = 64
BOTH = ("row", "col")
COUNT, ROW, COL = 9, 10, 11
NORTH_STEPS = 2
MIB = 1024 * 1024
SMALL, LARGE = 24 * MIB, 62 * MIB
F32 = jnp.float32
BF16 = jnp.bfloat16

VMEM = pl.BlockSpec(memory_space=pltpu.VMEM)
SMEM = pl.BlockSpec(memory_space=pltpu.SMEM)
HBM = pl.BlockSpec(memory_space=pltpu.HBM)
NN = (((1,), (0,)), ((), ()))
NT = (((1,), (1,)), ((), ()))
TN = (((0,), (0,)), ((), ()))


def split_table(table):
    high = table.astype(ml_dtypes.bfloat16)
    low = (table - high.astype(np.float64)).astype(ml_dtypes.bfloat16)
    return np.stack([high, low])


def group_start(group, rows):
    if group == 0:
        return 0
    if group == 1:
        return rows // 2
    return group // 2 + HALF * rows * (group % 2)


def unit_turn(product, period):
    angle = 2.0 * np.pi * (product % period) / period
    return np.cos(angle), np.sin(angle)


def north_turns(rows):
    north = rows * LANES
    starts = np.array([group_start(g, rows) for g in range(rows)])
    cos, sin = unit_turn(starts[:, None] * np.arange(north)[None, :], north)
    turns = np.stack([cos, -sin]).reshape(2, rows, rows, LANES)
    return turns.astype(np.float32)


def north_forward_table(cols):
    cos, sin = unit_turn(np.outer(np.arange(HALF), np.arange(LANES)), LANES)
    plain = np.concatenate(
        [np.concatenate([cos, sin], 1), np.concatenate([-sin, cos], 1)], 0
    )
    packed = plain.copy()
    packed[HALF, :LANES] = 1.0 - 2.0 * (np.arange(LANES) % 2)
    order = np.arange(2 * HALF).reshape(2, cols, -1).transpose(1, 0, 2).reshape(-1)
    return np.stack([split_table(packed[order]), split_table(plain[order])])


def north_inverse_table():
    cos, sin = unit_turn(np.outer(np.arange(HALF), np.arange(LANES)), LANES)
    plain = 2.0 * np.concatenate([cos, sin], 1)
    packed = plain.copy()
    packed[0, :LANES] = 1.0
    packed[0, LANES:] = 2.0 * (np.arange(LANES) % 2) - 1.0
    return np.stack([split_table(packed), split_table(plain)])


def east_tables(east):
    bands = east // LANES
    cos, sin = unit_turn(np.outer(np.arange(LANES), np.arange(LANES)), LANES)
    forward = np.block([[cos, -sin], [sin, cos]])
    inverse = np.block([[cos, sin], [-sin, cos]])
    turn_cos, turn_sin = unit_turn(np.outer(np.arange(bands), np.arange(LANES)), east)
    turns = np.concatenate([turn_cos, -turn_sin]).astype(np.float32)
    up_east = hat_table(east, east // REFINE).reshape(-1, 2 * LANES, east // REFINE)
    up_east = up_east.transpose(0, 2, 1).reshape(-1, 2 * LANES).astype(ml_dtypes.bfloat16)
    tables = [split_table(forward), split_table(inverse)]
    return np.concatenate([t.reshape(-1, 2 * LANES) for t in tables] + [up_east]), turns


def hat_table(fine_count, coarse_count):
    offset = (np.arange(fine_count)[:, None] + 0.5) / REFINE - 0.5 - np.arange(coarse_count)[None, :]
    return np.maximum(0.0, 1.0 - np.abs(offset))


def north_hat_table(rows, cols):
    north = rows * LANES
    coarse = rows * SRC_ROWS
    own = HALF // cols
    spectrum = np.fft.fft(hat_table(north, coarse), axis=0)
    out = np.zeros((rows, cols, 2 * own, coarse))
    for group in range(rows):
        for col in range(cols):
            index = group_start(group, rows) + rows * (col * own + np.arange(own))
            part = spectrum[index % north]
            out[group, col, :own] = part.real
            out[group, col, own:] = part.imag
    out[0, 0, own] = spectrum[north // 2].real
    out = out.reshape(rows * cols, 2 * own, 2 * rows, 4).transpose(0, 2, 3, 1)
    out = out.reshape(rows * cols, 2 * rows, 8 * own)
    return np.pad(out, ((0, 0), (0, 0), (0, LANES - 8 * own))).astype(np.float32)


def split(x):
    high = x.astype(BF16)
    return high, (x - high.astype(F32)).astype(BF16)


def dot(a, b, dims):
    return lax.dot_general(a, b, dims, preferred_element_type=F32)


def mul_table(x, high, low, dims=NN):
    x_high, x_low = split(x)
    return dot(x_high, high, dims) + (dot(x_low, high, dims) + dot(x_high, low, dims))


def table_mul(high, low, x, dims=NN):
    x_high, x_low = split(x)
    return dot(high, x_high, dims) + (dot(high, x_low, dims) + dot(low, x_high, dims))


def transform_list(values, sign):
    count = len(values)
    if count == 1:
        return values
    even = transform_list(values[0::2], sign)
    odd = transform_list(values[1::2], sign)
    first, second = [], []
    for k in range(count // 2):
        re, im = odd[k]
        if k == 0:
            turned = (re, im)
        elif 4 * k == count:
            turned = (im, -re) if sign < 0 else (-im, re)
        else:
            cos = float(np.cos(2.0 * np.pi * k / count))
            sin = sign * float(np.sin(2.0 * np.pi * k / count))
            if 8 * k == count or 8 * k == 3 * count:
                if cos * sin > 0:
                    turned = (cos * (re - im), cos * (re + im))
                else:
                    turned = (cos * (re + im), cos * (im - re))
            else:
                turned = (re * cos - im * sin, re * sin + im * cos)
        first.append((even[k][0] + turned[0], even[k][1] + turned[1]))
        second.append((even[k][0] - turned[0], even[k][1] - turned[1]))
    return first + second


def total(x):
    lanes = jnp.sum(jnp.sum(x, axis=0), axis=0, keepdims=True)
    return jnp.sum(lanes, axis=1, keepdims=True)


def neighbour(k, ints, rows, cols):
    code = ints[k]
    near_row = ints[ROW] + code // 3 - 1
    near_col = ints[COL] + code % 3 - 1
    inside = (near_row >= 0) & (near_row < rows) & (near_col >= 0) & (near_col < cols)
    device = jnp.clip(near_row * cols + near_col, 0, rows * cols - 1)
    return device, inside


def near_blocks(ints, vector, rows, cols):
    blocks = []
    for k in range(FOOTPRINT):
        device, inside = neighbour(k, ints, rows, cols)
        blocks.append(vector[device] * jnp.where(inside, 1.0, 0.0))
    return blocks


def apply_forward(tiles, copies, blocks, count, out, work):
    slots, width = tiles.shape[1:]
    parts = width // LANES
    squares = jnp.zeros((SUB, LANES), F32)
    for group in range(0, FOOTPRINT, 3):
        for k in range(group, group + 3):
            copies[k].wait()
        spread = [
            [jnp.broadcast_to(blocks[k][p : p + 1], (SUB, LANES)) for p in range(parts)]
            for k in range(group, group + 3)
        ]

        def step(t, squares, group=group, spread=spread):
            at = pl.multiple_of(t * SUB, SUB)
            sums = [None] * parts
            for k in range(3):
                for p in range(parts):
                    tile = tiles[group + k, pl.ds(at, SUB), p * LANES : (p + 1) * LANES]
                    term = tile * spread[k][p]
                    sums[p] = term if sums[p] is None else sums[p] + term
            acc = functools.reduce(jnp.add, sums)
            if group > 0:
                acc = acc + work[pl.ds(at, SUB), :]
            if group + 3 < FOOTPRINT:
                work[pl.ds(at, SUB), :] = acc
                return squares
            slot = at + lax.broadcasted_iota(jnp.int32, (SUB, LANES), 0)
            value = jnp.where(slot < count, jnp.sum(acc, axis=1, keepdims=True), 0.0)
            if out is not None:
                out[pl.ds(at, SUB), :] = value
            return squares + value * value

        squares = lax.fori_loop(0, slots // SUB, step, squares, unroll=8)
    return jnp.sum(squares, axis=0, keepdims=True)


def apply_adjoint(tile, values, out, device):
    slots, width = tile.shape
    for p in range(width // LANES):
        sums = [None] * 4
        for t in range(slots // SUB):
            term = tile[t * SUB : (t + 1) * SUB, p * LANES : (p + 1) * LANES] * values[
                t * SUB : (t + 1) * SUB, :
            ]
            sums[t % 4] = term if sums[t % 4] is None else sums[t % 4] + term
        acc = functools.reduce(jnp.add, sums)
        out[pl.ds(device, 1), p, :] = jnp.sum(acc, axis=0, keepdims=True)


def send_adjoint(tile, values, k, ints, out, rows, cols):
    device, inside = neighbour(k, ints, rows, cols)

    @pl.when(inside)
    def _():
        apply_adjoint(tile, values, out, device)


def tile_copies(source, tiles, sems):
    copies = [
        pltpu.make_async_copy(source.at[0, 0, k], tiles.at[k], sems.at[k]) for k in range(FOOTPRINT)
    ]
    for copy in copies:
        copy.start()
    return copies


def start_kernel(rows, cols, ints, readings, source, out, tiles, values, sems):
    copies = tile_copies(source, tiles, sems)
    out[...] = jnp.zeros(out.shape, F32)
    slots = readings.shape[1]
    slot = lax.broadcasted_iota(jnp.int32, (1, slots), 1)
    live = jnp.where(slot < ints[COUNT], readings[...], 0.0)
    for t in range(slots // LANES):
        square = jnp.broadcast_to(live[:, t * LANES : (t + 1) * LANES], (LANES, LANES))
        values[t * LANES : (t + 1) * LANES, :] = square.T
    for k in range(FOOTPRINT):
        copies[k].wait()
        send_adjoint(tiles.at[k], values, k, ints, out, rows, cols)


def gather_kernel(arrived, everywhere):
    block = jnp.sum(arrived[...], axis=0)
    everywhere[...] = jnp.broadcast_to(block[None], everywhere.shape)


def normal_kernel(rows, cols, ints, floats, source, vector, out, tiles, sems, values, work):
    copies = tile_copies(source, tiles, sems)
    blocks = near_blocks(ints, vector, rows, cols)
    apply_forward(tiles, copies, blocks, ints[COUNT], values, work)
    out[...] = jnp.zeros(out.shape, F32)
    for k in range(FOOTPRINT):
        send_adjoint(tiles.at[k], values, k, ints, out, rows, cols)
    me = ints[ROW] * cols + ints[COL]
    out[me] = out[me] + floats[0] * vector[me]


def north_kernel(cols, ints, planes, turns, table, *outs):
    outs, mixed = outs[:-1], outs[-1]
    rows = planes.shape[0]
    re = planes[0] * turns[0, 0, 0:1]
    im = planes[0] * turns[1, 0, 0:1]
    for r in range(1, rows):
        re = re + planes[r] * turns[0, 0, r : r + 1]
        im = im + planes[r] * turns[1, 0, r : r + 1]
    both = jnp.concatenate([re, im], axis=1)
    result = table_mul(table[0, 0], table[0, 1], both, NT)
    own2 = outs[0].shape[0]
    for col in range(cols):
        mixed[col] = result[col * own2 : (col + 1) * own2]
    for step in range(cols):
        outs[step][...] = mixed[ints[COL] ^ step]


def pole(north, east, trig):
    square = north * north + east * east
    inverse = jnp.where(square > 0.0, lax.rsqrt(jnp.where(square > 0.0, square, 1.0)), 0.0)
    a0 = (trig[1] * north + trig[2] * east) * inverse
    a1 = (trig[4] * north + trig[5] * east) * inverse
    v0, v1 = trig[0], trig[3]
    scale = 1.0 / ((v0 * v0 + a0 * a0) * (v1 * v1 + a1 * a1))
    return (v0 * v1 - a0 * a1) * scale, -(v0 * a1 + v1 * a0) * scale, square * inverse


def side_rows(own, bands, rows):
    span = (own + 1) * bands
    turns = 2 * (1 + LAYERS) * span
    return span, turns, turns + 2 * bands, turns + 2 * bands + 2 * rows


def filter_kernel(rows, cols, own, bands, ints, floats, turns, hats, side):
    span, turns_at, hats_at, end = side_rows(own, bands, rows)
    side[turns_at:hats_at, :] = turns[...]
    side[hats_at:end, :] = hats[0]
    depth = [floats[1 + l] for l in range(LAYERS)]
    trig = [floats[1 + LAYERS + t] for t in range(6)]

    def put(part, q, at, value):
        base = (part * (1 + LAYERS) + q) * span + at
        side[base : base + value.shape[0], :] = value

    north_len, east_len = rows * LANES, bands * LANES
    scale = 1.0 / (north_len * east_len)
    row, col = ints[ROW], ints[COL]
    start = jnp.where(
        row == 0, 0, jnp.where(row == 1, rows // 2, row // 2 + HALF * rows * (row % 2))
    )

    def signed(index, length):
        return jnp.where(index < length // 2, index, index - length).astype(F32) / length

    def north_of(shape):
        index = start + rows * (col * own + lax.broadcasted_iota(jnp.int32, shape, 0))
        return signed(index, north_len)

    def weights(re, im, radius):
        damp = [None] + [jnp.exp(radius * (-2.0 * np.pi * depth[l])) for l in range(LAYERS)]
        return [(re, im) if d is None else (re * d, im * d) for d in damp]

    lane = lax.broadcasted_iota(jnp.int32, (own, LANES), 1)
    north = north_of((own, LANES))
    for band in range(bands):
        east = signed(band + bands * lane, east_len)
        re, im, radius = pole(north, east, trig)
        if band == 0:
            re2, im2, _ = pole(north, jnp.where(lane == HALF, 0.5, east), trig)
            re, im = 0.5 * (re + re2), 0.5 * (im + im2)
        for q, (wr, wi) in enumerate(weights(re * scale, im * scale, radius)):
            put(0, q, band * own, wr)
            put(1, q, band * own, wi)
            put(0, q, bands * own, jnp.zeros((bands, LANES), F32))
            put(1, q, bands * own, jnp.zeros((bands, LANES), F32))

    @pl.when((row == 0) & (col == 0))
    def _():
        band = lax.broadcasted_iota(jnp.int32, (bands, LANES), 0)
        lanes = lax.broadcasted_iota(jnp.int32, (bands, LANES), 1)
        east = signed(band + bands * lanes, east_len)
        flipped = jnp.where((band == 0) & (lanes == HALF), 0.5, east)
        pairs = []
        for one, other in ((0.0, 0.0), (-0.5, 0.5)):
            re, im, radius = pole(jnp.full_like(east, one), east, trig)
            re2, im2, _ = pole(jnp.full_like(east, other), flipped, trig)
            half = 0.5 * scale
            pairs.append(weights(half * (re + re2), half * (im + im2), radius))
        for q in range(1 + LAYERS):
            (r0, i0), (r1, i1) = pairs[0][q], pairs[1][q]
            put(0, q, bands * own, 0.5 * (r0 - r1))
            put(1, q, bands * own, 0.5 * (i0 - i1))
            for b in range(bands):
                put(0, q, b * own, 0.5 * (r0 + r1)[b : b + 1])
                put(1, q, b * own, 0.5 * (i0 + i1)[b : b + 1])


def turn_rows(side, turns_at, band, bands):
    cos, sin = turns_at + band, turns_at + bands + band
    return side[cos : cos + 1, :], side[sin : sin + 1, :]


def east_table(tables, index):
    span = 2 * LANES
    return tables[2 * index * span : (2 * index + 1) * span], tables[
        (2 * index + 1) * span : (2 * index + 2) * span
    ]


def east_forward(get, sizes, side, tables, work):
    rows, _, own, bands = sizes
    turns_at = side_rows(own, bands, rows)[1]
    for g in range(own // SUB):
        values = transform_list([get(m, g) for m in range(bands)], -1.0)
        for b in range(bands):
            cos, sin = turn_rows(side, turns_at, b, bands)
            re, im = values[b]
            at = b * own + g * SUB
            work[at : at + SUB, :LANES] = re * cos - im * sin
            work[at : at + SUB, LANES:] = re * sin + im * cos
            if g == 0:
                re, im = values[(bands - b) % bands]
                re, im = re[0:1], -im[0:1]
                at = bands * own + b
                work[at : at + 1, :LANES] = re * cos - im * sin
                work[at : at + 1, LANES:] = re * sin + im * cos
    return mul_table(work[...], *east_table(tables, 0))


def weigh(spectrum, q, sizes, side, into, first):
    rows, _, own, bands = sizes
    span = side_rows(own, bands, rows)[0]
    re, im = spectrum[:, :LANES], spectrum[:, LANES:]
    wr = side[q * span : (q + 1) * span, :]
    wi = side[(1 + LAYERS + q) * span : (2 + LAYERS + q) * span, :]
    out_re, out_im = re * wr - im * wi, re * wi + im * wr
    main = own * bands
    if first:
        into[:, :LANES] = out_re[:main]
        into[:, LANES:] = out_im[:main]
    else:
        into[:, :LANES] += out_re[:main]
        into[:, LANES:] += out_im[:main]
    for b in range(bands):
        into[b * own : b * own + 1, :LANES] += out_re[main + b : main + b + 1]
        into[b * own : b * own + 1, LANES:] += out_im[main + b : main + b + 1]


def east_inverse(spectrum, sizes, side, tables, work, store):
    rows, _, own, bands = sizes
    turns_at = side_rows(own, bands, rows)[1]
    work[...] = mul_table(spectrum[...], *east_table(tables, 1))
    for g in range(own // SUB):
        values = []
        for b in range(bands):
            at = b * own + g * SUB
            re, im = work[at : at + SUB, :LANES], work[at : at + SUB, LANES:]
            cos, sin = turn_rows(side, turns_at, b, bands)
            values.append((re * cos + im * sin, im * cos - re * sin))
        values = transform_list(values, 1.0)
        for b in range(bands):
            store(b, g, *values[b])


def store_pieces(out, width):
    per_band = LANES // width

    def store(band, g, re, im):
        for s in range(per_band):
            cut = slice(s * width, (s + 1) * width)
            piece = jnp.concatenate([re[:, cut], im[:, cut]], axis=1)
            out[band * per_band + s, g * SUB : (g + 1) * SUB] = piece

    return store


def model_rows(vector, sizes, side, coarse):
    rows, cols, own, bands = sizes
    own2 = 2 * own
    for i in range(rows):
        for j in range(cols):
            block = vector[i * cols + j]
            for layer in range(LAYERS):
                coarse[layer, 2 * i : 2 * i + 2, j * LANES : (j + 1) * LANES] = block[
                    2 * layer : 2 * layer + 2
                ]
    out = []
    _, _, hats_at, end = side_rows(own, bands, rows)
    high, low = split(side[hats_at:end, :])
    tiles = cols * SRC_COLS // LANES
    lane = lax.broadcasted_iota(jnp.int32, (own2, LANES), 1) // SRC_COLS
    for layer in range(LAYERS):
        mixed = table_mul(high, low, coarse[layer], TN)
        whole = []
        for tile in range(tiles):
            joined = None
            for place in range(LANES // SRC_COLS):
                j = tile * (LANES // SRC_COLS) + place
                summed = None
                for part in range(4):
                    piece = mixed[part * own2 : (part + 1) * own2, j * LANES : (j + 1) * LANES]
                    shift = ((place - part) * SRC_COLS) % LANES
                    if shift:
                        piece = pltpu.roll(piece, shift, 1)
                    summed = piece if summed is None else summed + piece
                joined = summed if joined is None else jnp.where(lane == place, summed, joined)
            whole.append(joined)
        out.append(whole[0] if tiles == 1 else jnp.concatenate(whole, axis=1))
    return out


def model_response(vector, sizes, side, tables, store, coarse, fine, work, mixed, back):
    rows, cols, own, bands = sizes
    depth = cols * SRC_COLS
    high, low = split(jnp.concatenate(model_rows(vector, sizes, side, coarse), axis=0))
    for c in range(bands // 2):
        at = 8 * LANES + c * depth
        table = tables[at : at + depth, :]
        fine[:, 2 * LANES * c : 2 * LANES * (c + 1)] = dot(high, table, NN) + dot(low, table, NN)
    for layer in range(LAYERS):

        def get(m, g, base=2 * own * layer):
            at = base + g * SUB
            cut = slice(m * LANES, (m + 1) * LANES)
            return fine[at : at + SUB, cut], fine[at + own : at + own + SUB, cut]

        spectrum = east_forward(get, sizes, side, tables, work)
        weigh(spectrum, 1 + layer, sizes, side, mixed, layer == 0)
    east_inverse(mixed, sizes, side, tables, back, store)


def resid_kernel(sizes, width, ints, *refs):
    rows, cols, own, bands = sizes
    arrived, (tables, side, out, spec, work, mixed, back) = refs[:cols], refs[cols:]
    per = arrived[0].shape[1] // LANES
    for step in range(cols):
        spec[ints[COL] ^ step] = arrived[step][...]

    def get(m, g):
        cut = slice((m % per) * LANES, (m % per + 1) * LANES)
        at = g * SUB
        return spec[m // per, at : at + SUB, cut], spec[m // per, own + at : own + at + SUB, cut]

    spectrum = east_forward(get, sizes, side, tables, work)
    weigh(spectrum, 0, sizes, side, mixed, True)
    east_inverse(mixed, sizes, side, tables, back, store_pieces(out, width))


def first_kernel(sizes, width, vector, tables, side, out, *work):
    model_response(vector, sizes, side, tables, store_pieces(out, width), *work)


def direction_kernel(
    rows, cols, ints, floats, source, first, applied, second, measured, carry, tiles, sems, work
):
    copies = tile_copies(source, tiles, sems)
    norm = total(first[...] * first[...])
    step = norm / total(first[...] * applied[...])
    residual = first[...] - step[None] * applied[...]
    norm_next = total(residual * residual)
    second[...] = residual + (norm_next / norm)[None] * first[...]
    blocks = near_blocks(ints, second, rows, cols)
    squares = apply_forward(tiles, copies, blocks, ints[COUNT], None, work)
    measured[...] = jnp.broadcast_to(squares[None], measured.shape)
    ridge = floats[0] * total(second[...] * second[...])
    me = ints[ROW] * cols + ints[COL]
    carry[0] = step * first[me]
    carry[1] = second[me]
    for at, value in ((2, norm_next), (3, ridge), (4, step)):
        carry[at] = jnp.broadcast_to(value, carry.shape[1:])


def second_kernel(sizes, width, vector, tables, side, early, early_first, carry, known, out, *work):
    known[...] = early[...] + carry[4, 0:1, 0:1][None] * early_first[...]
    model_response(vector, sizes, side, tables, store_pieces(out, width), *work)


def combine_kernel(measured, carry, known, response, out, coefficients):
    squares = jnp.sum(measured[:, 0:1], axis=0)
    step = carry[2, 0:1, 0:1] / (squares[:, 0:1] + carry[3, 0:1, 0:1])
    out[...] = known[...] + step[None] * response[...]
    solved = carry[0] + step * carry[1]
    for p in range(solved.shape[0]):
        coefficients[:, p * LANES : (p + 1) * LANES] = solved[p : p + 1]


def finish_kernel(rows, cols, arrived, turns, table, out, mixed, waves):
    own = arrived.shape[1]
    width = out.shape[0]
    for i in range(rows):
        for j in range(cols):
            mixed[i, j * own : (j + 1) * own, :] = arrived[i * cols + j]
        kind = min(i, 1)
        both = mul_table(mixed[i], table[kind, 0], table[kind, 1], TN)
        top, bottom = both[:width], both[width:]
        waves[i, :, :LANES] = top[:, :LANES] - bottom[:, LANES:]
        waves[i, :, LANES:] = top[:, LANES:] + bottom[:, :LANES]
    for at in range(0, width, SUB):
        parts = [None] * rows
        for i in range(rows):
            re = waves[i, at : at + SUB, :LANES]
            im = waves[i, at : at + SUB, LANES:]
            for n in range(rows):
                term = re * turns[0, i, n : n + 1] + im * turns[1, i, n : n + 1]
                parts[n] = term if i == 0 else parts[n] + term
        for n in range(rows):
            out[at : at + SUB, n * LANES : (n + 1) * LANES] = parts[n]


def shape(*dims):
    return jax.ShapeDtypeStruct(dims, F32)


def scratch(*dims):
    return pltpu.VMEM(dims, F32)


def call(kernel, outs, ins, work=(), limit=SMALL):
    return pl.pallas_call(
        kernel,
        out_shape=outs,
        in_specs=[spec for spec, _ in ins],
        out_specs=jax.tree.map(lambda _: VMEM, outs),
        scratch_shapes=list(work),
        compiler_params=pltpu.CompilerParams(vmem_limit_bytes=limit),
    )(*[value for _, value in ins])


def placed_call(kernel, out, ints, ins, work=(), limit=SMALL, steps=1, out_block=None):
    def whole(a):
        return pl.BlockSpec(a.shape, lambda step, at, n=a.ndim: (0,) * n)

    return pl.pallas_call(
        kernel,
        out_shape=out,
        grid_spec=pltpu.PrefetchScalarGridSpec(
            num_scalar_prefetch=1,
            grid=(steps,),
            in_specs=[whole(value) if spec is None else spec for spec, value in ins],
            out_specs=whole(out) if out_block is None else out_block,
            scratch_shapes=list(work),
        ),
        compiler_params=pltpu.CompilerParams(vmem_limit_bytes=limit),
    )(ints, *[value for _, value in ins])


def exchange(pieces):
    return lax.all_to_all(pieces, BOTH, 0, 0, tiled=True)


def on_device(
    kernel_tiles, footprints, counts, readings, damping, layer_depth, inclinations, declinations,
    resid_grid,
):
    rows, cols = lax.axis_size("row"), lax.axis_size("col")
    devices = rows * cols
    place = jnp.stack([lax.axis_index("row"), lax.axis_index("col")]).astype(jnp.int32)
    ints = jnp.concatenate([footprints.reshape(-1), counts.reshape(-1), place])
    slots, sources = kernel_tiles.shape[3:]
    parts = sources // LANES
    tile_east = resid_grid.shape[0]
    east = cols * tile_east
    bands = east // LANES
    own = HALF // cols
    width = east // devices
    sizes = (rows, cols, own, bands)

    turns = north_turns(rows)
    tables, east_turns = east_tables(east)
    hats = north_hat_table(rows, cols)

    planes = lax.all_gather(resid_grid, "row", axis=0)

    kernel_tiles = pltpu.with_memory_space_constraint(kernel_tiles, pltpu.HBM)
    tile_scratch = scratch(FOOTPRINT, slots, sources)
    tile_sems = pltpu.SemaphoreType.DMA((FOOTPRINT,))

    sums = call(
        functools.partial(start_kernel, rows, cols),
        shape(devices, parts, LANES),
        [(SMEM, ints), (VMEM, readings.reshape(1, slots)), (HBM, kernel_tiles)],
        [tile_scratch, scratch(slots, LANES), tile_sems],
    )
    sums, damping, layer_depth, inclinations, declinations = lax.optimization_barrier(
        (sums, damping, layer_depth, inclinations, declinations)
    )
    flat = jnp.cos(inclinations)
    trig = [jnp.sin(inclinations), flat * jnp.cos(declinations), flat * jnp.sin(declinations)]
    floats = jnp.concatenate([damping, layer_depth, jnp.stack(trig, axis=1).reshape(-1)])
    side = placed_call(
        functools.partial(filter_kernel, rows, cols, own, bands),
        shape(side_rows(own, bands, rows)[-1], LANES),
        ints,
        [
            (SMEM, floats),
            (None, east_turns),
            (pl.BlockSpec((1,) + hats.shape[1:], lambda _, at: (at[ROW] * cols + at[COL], 0, 0)), hats),
        ],
    )
    everywhere = shape(devices, parts, LANES)
    right_all = call(gather_kernel, everywhere, [(VMEM, exchange(sums))])
    right_all, side = lax.optimization_barrier((right_all, side))
    right_side = exchange(right_all)

    sums = call(
        functools.partial(normal_kernel, rows, cols),
        everywhere,
        [(SMEM, ints), (SMEM, floats), (HBM, kernel_tiles), (VMEM, right_side)],
        [tile_scratch, tile_sems, scratch(slots, LANES), scratch(slots, LANES)],
    )
    sums, planes, right_side = lax.optimization_barrier((sums, planes, right_side))
    chunk = tile_east // NORTH_STEPS
    spectra = placed_call(
        functools.partial(north_kernel, cols),
        [shape(2 * own, tile_east)] * cols,
        ints,
        [
            (pl.BlockSpec((rows, chunk, LANES), lambda c, at: (0, c, 0)), pltpu.with_memory_space_constraint(planes, pltpu.HBM)),
            (pl.BlockSpec((2, 1, rows, LANES), lambda c, at: (0, at[ROW], 0, 0)), turns),
            (
                pl.BlockSpec(
                    (1, 2, 2 * HALF, 2 * LANES), lambda c, at: (jnp.minimum(at[ROW], 1), 0, 0, 0)
                ),
                north_forward_table(cols),
            ),
        ],
        [scratch(cols, 2 * own, chunk)],
        steps=NORTH_STEPS,
        out_block=[pl.BlockSpec((2 * own, chunk), lambda c, at: (0, c))] * cols,
        limit=48 * MIB,
    )
    right_side, spectra = lax.optimization_barrier((right_side, spectra))
    spectra = list(spectra[:1]) + [
        lax.ppermute(spectra[s], "col", [(c, c ^ s) for c in range(cols)]) for s in range(1, cols)
    ]
    work = [
        scratch((own + 1) * bands, 2 * LANES),
        scratch(own * bands, 2 * LANES),
        scratch(own * bands, 2 * LANES),
    ]
    model_work = [scratch(LAYERS, 2 * rows, cols * LANES), scratch(LAYERS * 2 * own, east)] + work
    pieces = shape(devices, own, 2 * width)
    early_first = call(
        functools.partial(first_kernel, sizes, width),
        pieces,
        [(VMEM, right_side), (VMEM, tables), (VMEM, side)],
        model_work,
    )
    applied_all = call(gather_kernel, everywhere, [(VMEM, exchange(sums))])
    applied_all, early_first = lax.optimization_barrier((applied_all, early_first))
    applied = exchange(applied_all)

    second, measured, carry = call(
        functools.partial(direction_kernel, rows, cols),
        (everywhere, everywhere, shape(5, parts, LANES)),
        [(SMEM, ints), (SMEM, floats), (HBM, kernel_tiles), (VMEM, right_side), (VMEM, applied)],
        [tile_scratch, tile_sems, scratch(slots, LANES)],
    )
    measured, spectra = lax.optimization_barrier((measured, spectra))
    early = call(
        functools.partial(resid_kernel, sizes, width),
        pieces,
        [(SMEM, ints)] + [(VMEM, part) for part in spectra] + [(VMEM, tables), (VMEM, side)],
        [scratch(cols, 2 * own, tile_east)] + work,
    )

    known, response = call(
        functools.partial(second_kernel, sizes, width),
        (pieces, pieces),
        [
            (VMEM, second),
            (VMEM, tables),
            (VMEM, side),
            (VMEM, early),
            (VMEM, early_first),
            (VMEM, carry),
        ],
        model_work,
    )
    outgoing, coefficients = call(
        combine_kernel,
        (pieces, shape(1, sources)),
        [(VMEM, exchange(measured)), (VMEM, carry), (VMEM, known), (VMEM, response)],
    )
    rtp_map = call(
        functools.partial(finish_kernel, rows, cols),
        shape(width, rows * LANES),
        [(VMEM, exchange(outgoing)), (VMEM, turns), (VMEM, north_inverse_table())],
        [scratch(rows, HALF, 2 * width), scratch(rows, width, 2 * LANES)],
    )
    return coefficients.reshape(1, 1, sources), rtp_map


def solution(mesh):
    in_specs = (
        P("row", "col", None, None, None),
        P("row", "col", None),
        P("row", "col"),
        P("row", "col", None),
        P(),
        P(),
        P(),
        P(),
        P("col", "row"),
    )
    out_specs = (P("row", "col", None), P(("row", "col"), None))
    return jax.shard_map(
        on_device, mesh=mesh, in_specs=in_specs, out_specs=out_specs, check_vma=False
    )
```

time: 157 us -> 100 us (0.64); the launches traced: 155 us -> 100 us
  local copies, waits for them, and re-layouts: 27.8 us -> 0.95 us
  blocking collectives: 44.8 us -> 21.1 us
  waiting for transfers between devices: 39.4 us -> 16.4 us
  starting transfers between devices: 5.19 us -> 21.3 us
  Pallas kernels: 16.3 us -> 23.9 us
  between operations: 21.2 us -> 15.6 us
    all_gather x1, waiting for transfers between devices: 32.5 us -> 0.02 us  [on_device(): planes = lax.all_gather(resid_grid, 'row', axis=0)]
    unnamed x76 -> x20, local copies, waits for them, and re-layouts: 25.2 us -> 0.73 us
    all_to_all x3 -> x2, blocking collectives: 44.8 us -> 21.1 us  [exchange(): return lax.all_to_all(pieces, BOTH, 0, 0, tiled=True)]
    all_to_all x2 -> x4, starting transfers between devices: 5.11 us -> 16.8 us  [exchange(): return lax.all_to_all(pieces, BOTH, 0, 0, tiled=True)]
    all_to_all x2 -> x4, waiting for transfers between devices: 6.19 us -> 15.7 us  [exchange(): return lax.all_to_all(pieces, BOTH, 0, 0, tiled=True)]
    pallas_call x9 -> x12, Pallas kernels: 16.3 us -> 23.9 us  [the longest x10 19.9 us: call(): pl.pallas_call(kernel, out_shape=outs, in_specs=[spec for spec, _ in ins]...]
    ppermute x0 -> x3, starting transfers between devices: none -> 4.45 us  [on_device(): lax.ppermute(spectra[s], 'col', [(c, c ^ s) for c in range(cols)])]
  transfers between devices with their start and end apart: 4 -> 8, of which waited for: 2 -> 4; matrix products, arithmetic and copies ran while one was open for 2% -> 1% of each run, Pallas kernels for 5% -> 21%
where the time goes in v2:
time: 100 us
  Pallas kernels  23.9 us (24%)
  starting transfers between devices  21.3 us (21%)
  blocking collectives  21.1 us (21%)
  waiting for transfers between devices  16.4 us (16%)
  between operations  15.6 us (16%)
    all_to_all x2, blocking collectives, exchange(): return lax.all_to_all(pieces, BOTH, 0, 0, tiled=True)  21.1 us
    pallas_call x10, Pallas kernels, call(): pl.pallas_call(kernel, out_shape=outs, in_specs=[spec for spec, _ in ins]...  19.9 us
    all_to_all x4, starting transfers between devices, exchange(): return lax.all_to_all(pieces, BOTH, 0, 0, tiled=True)  16.8 us
    all_to_all x4, waiting for transfers between devices, exchange(): return lax.all_to_all(pieces, BOTH, 0, 0, tiled=True)  15.7 us
    ppermute x3, starting transfers between devices, on_device(): lax.ppermute(spectra[s], 'col', [(c, c ^ s) for c in range(cols)])  4.45 us
    pallas_call x2, Pallas kernels, placed_call(): pl.pallas_call(kernel, out_shape=out, grid_spec=pltpu.PrefetchScalarGridS...  3.97 us
  transfers between devices with their start and end apart: 8, of which 4 were waited for; matrix products, arithmetic and copies ran while one was open for 1% of the time, Pallas kernels for 21%

profile of v2, /device:TPU:0, one launch (start us, length us, event | category | flops | bytes accessed | tf_op | source)
XLA Modules:
  0.0 100.0 jit_solution(10746828495940426708)
XLA Ops:
  7.2 0.0 copy-start.1
  7.2 0.0 copy-start.5
  7.2 0.0 copy-start.7
  7.2 0.0 copy-start.9
  7.2 0.0 copy-start.8
  7.2 0.0 all-gather.3.cloned.1.call-start
  7.3 0.7 all-gather.3.cloned.1.call-update
  8.6 0.7 pad_add_fusion.ints
  9.3 0.7 copy-done.6
  10.0 3.6 %shard_map.158 = f32[32,4,128]{2,1,0:T(4,128)} custom-call(s32[12]{0:T(128)S(1)} %pad_add_fusion.ints, f32[1,256]{1,0:T(1,128)S(1)} %bitcast.14, f32[1,1,9,256,512]{4,3,2,1,0:T(8,128)} %source.5), custom_call_target="tpu_custom_call" | custom-call | tf_op jit(solution)/shard_map/pallas_call | solution.py:602
  13.6 0.0 copy-start
  13.6 7.4 %all-to-all-start = ((f32[32,4,128]{2,1,0:T(4,128)}), f32[32,4,128]{2,1,0:T(4,128)S(1)}, u32[]{:S(2)}, u32[]{:S(2)}) async-start(f32[32,4,128]{2,1,0:T(4,128)} %shard_map.158), calls=%async_computation | async-start | bytes 131072 | tf_op jit(solution)/shard_map/all_to_all | solution.py:631
  21.0 0.0 copy-done.9
  21.0 0.0 copy-done.7
  21.7 0.1 copy.17
  21.8 0.1 reshape.22
  21.9 0.0 copy-done.8
  21.9 0.1 pad_maximum_fusion.1.floats
  22.0 0.0 copy-done.1
  22.0 0.0 copy-done.5
  22.0 1.3 %shard_map.160.side.refs_5_ = f32[1680,128]{1,0:T(8,128)S(1)} custom-call(s32[12]{0:T(128)S(1)} %pad_add_fusion.ints, f32[9]{0:T(128)S(1)} %pad_maximum_fusion.1.floats, f32[32,128]{1,0:T(8,128)S(1)} %copy-done.5, f32[32,16,128]{2,1,0:T(8,128)S(1)} %copy-done.1), custom_call_target="tpu_custom_call" | custom-call | tf_op jit(solution)/shard_map/pallas_call | solution.py:616
  23.3 5.1 %all-to-all-done.arrived = f32[32,4,128]{2,1,0:T(4,128)S(1)} async-done(((f32[32,4,128]{2,1,0:T(4,128)}), f32[32,4,128]{2,1,0:T(4,128)S(1)}, u32[]{:S(2)}, u32[]{:S(2)}) %all-to-all-start) | async-done | bytes 65568 | tf_op jit(solution)/shard_map/all_to_all | solution.py:631
  28.5 9.2 %all_to_all.30.vector.first = f32[32,4,128]{2,1,0:T(4,128)S(1)} all-to-all(f32[32,4,128]{2,1,0:T(4,128)S(1)} %shard_map.159), channel_id=1, replica_groups=mesh['row'=8,'col'=4] {'row','col'}, dimensions={0} | all-to-all | bytes 131072 | tf_op jit(solution)/shard_map/all_to_all | solution.py:631
  37.7 4.5 %shard_map.161 = f32[32,4,128]{2,1,0:T(4,128)} custom-call(s32[12]{0:T(128)S(1)} %pad_add_fusion.ints, f32[9]{0:T(128)S(1)} %pad_maximum_fusion.1.floats, f32[1,1,9,256,512]{4,3,2,1,0:T(8,128)} %source.5, f32[32,4,128]{2,1,0:T(4,128)S(1)} %all_to_all.30.vector.first), custom_call_target="tpu_custom_call" | custom-call | tf_op jit(solution)/shard_map/pallas_call | solution.py:602
  42.2 0.0 all-gather.3.cloned.1.call-done
  42.2 3.8 %all-to-all-start.2 = ((f32[32,4,128]{2,1,0:T(4,128)}), f32[32,4,128]{2,1,0:T(4,128)S(1)}, u32[]{:S(2)}, u32[]{:S(2)}) async-start(f32[32,4,128]{2,1,0:T(4,128)} %shard_map.161), calls=%async_computation.2 | async-start | bytes 131072 | tf_op jit(solution)/shard_map/all_to_all | solution.py:631
  46.0 2.6 %shard_map.162 = (f32[32,512]{1,0:T(8,128)S(1)}, f32[32,512]{1,0:T(8,128)S(1)}, f32[32,512]{1,0:T(8,128)S(1)}, f32[32,512]{1,0:T(8,128)S(1)}) custom-call(s32[12]{0:T(128)S(1)} %pad_add_fusion.ints, f32[8,512,128]{2,1,0:T(8,128)} %bitcast.15, f32[2,8,8,128]{3,2,1,0:T(8,128)S(1)} %copy-done.3, bf16[2,2,128,256]{3,2,1,0:T(8,128)(2,1)S(1)} %copy-done.2), custom_call_target="tpu_custom_call" | custom-call | tf_op jit(solution)/shard_map/pallas_call | solution.py:616
  48.7 1.8 %shard_map.164.early_first = f32[32,16,128]{2,1,0:T(8,128)S(1)} custom-call(f32[32,4,128]{2,1,0:T(4,128)S(1)} %all_to_all.30.vector.first, bf16[2048,256]{1,0:T(8,128)(2,1)S(1)} %copy-done, f32[1680,128]{1,0:T(8,128)S(1)} %shard_map.160.side.refs_5_), custom_call_target="tpu_custom_call" | custom-call | tf_op jit(solution)/shard_map/pallas_call | solution.py:602
  50.5 3.0 %all-to-all-done.2.arrived = f32[32,4,128]{2,1,0:T(4,128)S(1)} async-done(((f32[32,4,128]{2,1,0:T(4,128)}), f32[32,4,128]{2,1,0:T(4,128)S(1)}, u32[]{:S(2)}, u32[]{:S(2)}) %all-to-all-start.2) | async-done | bytes 65568 | tf_op jit(solution)/shard_map/all_to_all | solution.py:631
  53.5 0.7 shard_map.163
  54.1 2.9 %all-to-all-start.3 = ((f32[32,4,128]{2,1,0:T(4,128)}), f32[32,4,128]{2,1,0:T(4,128)S(1)}, u32[]{:S(2)}, u32[]{:S(2)}) async-start(f32[32,4,128]{2,1,0:T(4,128)} %shard_map.163), calls=%async_computation.3 | async-start | bytes 131072 | tf_op jit(solution)/shard_map/all_to_all | solution.py:631
  57.0 0.0 copy-start.4
  57.0 1.8 %collective-permute-start = (f32[32,512]{1,0:T(8,128)S(1)}, f32[32,512]{1,0:T(8,128)S(1)}, u32[]{:S(2)}, u32[]{:S(2)}) collective-permute-start(f32[32,512]{1,0:T(8,128)S(1)} %get-tuple-element.53), channel_id=1, source_target_pairs={{0,1},{1,0},{2,3},{3,2},{4,5},{5,4},{6,7},{7,6},{8,9},{9,8},{10,11... | collective-permute-start | bytes 196616 | tf_op jit(solution)/shard_map/ppermute | solution.py:717
  58.9 2.4 %collective-permute-start.1 = (f32[32,512]{1,0:T(8,128)S(1)}, f32[32,512]{1,0:T(8,128)S(1)}, u32[]{:S(2)}, u32[]{:S(2)}) collective-permute-start(f32[32,512]{1,0:T(8,128)S(1)} %get-tuple-element.54), channel_id=1, source_target_pairs={{0,2},{1,3},{2,0},{3,1},{4,6},{5,7},{6,4},{7,5},{8,10},{9,11},{10,... | collective-permute-start | bytes 196616 | tf_op jit(solution)/shard_map/ppermute | solution.py:717
  61.3 0.2 collective-permute-start.2
  61.5 3.4 %all-to-all-done.3.applied = f32[32,4,128]{2,1,0:T(4,128)S(1)} async-done(((f32[32,4,128]{2,1,0:T(4,128)}), f32[32,4,128]{2,1,0:T(4,128)S(1)}, u32[]{:S(2)}, u32[]{:S(2)}) %all-to-all-start.3) | async-done | bytes 65568 | tf_op jit(solution)/shard_map/all_to_all | solution.py:631
  64.8 4.0 %shard_map.165 = (f32[32,4,128]{2,1,0:T(4,128)S(1)}, f32[32,4,128]{2,1,0:T(4,128)}, f32[5,4,128]{2,1,0:T(4,128)S(1)}) custom-call(s32[12]{0:T(128)S(1)} %pad_add_fusion.ints, f32[9]{0:T(128)S(1)} %pad_maximum_fusion.1.floats, f32[1,1,9,256,512]{4,3,2,1,0:T(8,128)} %source.5, f32[32,4,128]{2,1,0:T(4,128)S(1)} %all_to_all.30.vector.first, ...), custom_call_target="tpu_custom_call" | custom-call | tf_op jit(solution)/shard_map/pallas_call | solution.py:602
  68.9 0.0 collective-permute-done.refs_1_
  68.9 0.0 collective-permute-done.1.refs_2_
  68.9 0.0 collective-permute-done.2.refs_3_
  68.9 2.8 %all-to-all-start.4 = ((f32[32,4,128]{2,1,0:T(4,128)}), f32[32,4,128]{2,1,0:T(4,128)S(1)}, u32[]{:S(2)}, u32[]{:S(2)}) async-start(f32[32,4,128]{2,1,0:T(4,128)} %get-tuple-element.56), calls=%async_computation.4 | async-start | bytes 131072 | tf_op jit(solution)/shard_map/all_to_all | solution.py:631
  71.7 1.4 %shard_map.166.early = f32[32,16,128]{2,1,0:T(8,128)S(1)} custom-call(s32[12]{0:T(128)S(1)} %pad_add_fusion.ints, f32[32,512]{1,0:T(8,128)S(1)} %get-tuple-element.59.refs_0_, f32[32,512]{1,0:T(8,128)S(1)} %collective-permute-done.refs_1_, f32[32,512]{1,0:T(8,128)S(1)} %collective-permute-done.1.refs_2_, f32[32,512]{1,0:T(8,128)S(1)} %collective-permute-done.2.refs_3_, ...), custom_call_target="tpu_custom_call" | custom-call | tf_op jit(solution)/shard_map/pallas_call | solution.py:602
  73.2 1.9 %shard_map.167 = (f32[32,16,128]{2,1,0:T(8,128)S(1)}, f32[32,16,128]{2,1,0:T(8,128)S(1)}) custom-call(f32[32,4,128]{2,1,0:T(4,128)S(1)} %get-tuple-element.58.vector, bf16[2048,256]{1,0:T(8,128)(2,1)S(1)} %copy-done, f32[1680,128]{1,0:T(8,128)S(1)} %shard_map.160.side.refs_5_, f32[32,16,128]{2,1,0:T(8,128)S(1)} %shard_map.166.early, ...), custom_call_target="tpu_custom_call" | custom-call | tf_op jit(solution)/shard_map/pallas_call | solution.py:602
  75.0 4.2 %all-to-all-done.4.measured = f32[32,4,128]{2,1,0:T(4,128)S(1)} async-done(((f32[32,4,128]{2,1,0:T(4,128)}), f32[32,4,128]{2,1,0:T(4,128)S(1)}, u32[]{:S(2)}, u32[]{:S(2)}) %all-to-all-start.4) | async-done | bytes 65568 | tf_op jit(solution)/shard_map/all_to_all | solution.py:631
  79.2 0.7 shard_map.168
  79.9 11.9 %all_to_all.31.arrived = f32[32,16,128]{2,1,0:T(8,128)S(1)} all-to-all(f32[32,16,128]{2,1,0:T(8,128)S(1)} %get-tuple-element.67), channel_id=1, replica_groups=mesh['row'=8,'col'=4] {'row','col'}, dimensions={0} | all-to-all | bytes 524288 | tf_op jit(solution)/shard_map/all_to_all | solution.py:631
  91.8 0.0 copy-done.4
  91.8 1.4 %shard_map.169 = f32[64,1024]{1,0:T(8,128)} custom-call(f32[32,16,128]{2,1,0:T(8,128)S(1)} %all_to_all.31.arrived, f32[2,8,8,128]{3,2,1,0:T(8,128)S(1)} %copy-done.3, bf16[2,2,64,256]{3,2,1,0:T(8,128)(2,1)S(1)} %copy-done.4), custom_call_target="tpu_custom_call" | custom-call | tf_op jit(solution)/shard_map/pallas_call | solution.py:602
  (10 shorter events, 0.1 us)
Async XLA Ops:
  7.2 14.8 %copy-start.1 = (f32[32,16,128]{2,1,0:T(8,128)S(1)}, f32[32,16,128]{2,1,0:T(8,128)}, u32[]{:S(2)}) copy-start(f32[32,16,128]{2,1,0:T(8,128)} %constant.22.clone.hats) | copy-start | bytes 786436
  7.2 14.8 %copy-start.5 = (f32[32,128]{1,0:T(8,128)S(1)}, f32[32,128]{1,0:T(8,128)}, u32[]{:S(2)}) copy-start(f32[32,128]{1,0:T(8,128)} %constant.21.clone.turns) | copy-start | bytes 49156
  7.2 13.8 %copy-start.7 = (f32[2]{0:T(128)S(1)}, f32[2]{0:T(128)}, u32[]{:S(2)}) copy-start(f32[2]{0:T(128)} %param.22) | copy-start | bytes 28
  7.2 13.8 %copy-start.9 = (f32[2]{0:T(128)S(1)}, f32[2]{0:T(128)}, u32[]{:S(2)}) copy-start(f32[2]{0:T(128)} %param.21) | copy-start | bytes 28
  7.2 14.7 %copy-start.8 = (f32[2]{0:T(128)S(1)}, f32[2]{0:T(128)}, u32[]{:S(2)}) copy-start(f32[2]{0:T(128)} %param.20) | copy-start | bytes 28
  7.2 35.0 %all-gather.3.cloned.1.call-start = ((), (), s32[]{:S(2)}) async-start(), calls=%async_computation.6 | async-start | bytes 2359296 | tf_op jit(solution)/shard_map/all_gather | solution.py:655
  9.3 0.7 copy-start.6
  10.0 36.0 %copy-start.2 = (bf16[2,2,128,256]{3,2,1,0:T(8,128)(2,1)S(1)}, bf16[2,2,128,256]{3,2,1,0:T(8,128)(2,1)}, u32[]{:S(2)}) copy-start(bf16[2,2,128,256]{3,2,1,0:T(8,128)(2,1)} %constant.24.clone.table) | copy-start | bytes 786436
  10.0 36.0 %copy-start.3 = (f32[2,8,8,128]{3,2,1,0:T(8,128)S(1)}, f32[2,8,8,128]{3,2,1,0:T(8,128)}, u32[]{:S(2)}) copy-start(f32[2,8,8,128]{3,2,1,0:T(8,128)} %constant.23.clone.turns) | copy-start | bytes 196612
  13.6 35.1 %copy-start = (bf16[2048,256]{1,0:T(8,128)(2,1)S(1)}, bf16[2048,256]{1,0:T(8,128)(2,1)}, u32[]{:S(2)}) copy-start(bf16[2048,256]{1,0:T(8,128)(2,1)} %constant.25.clone.tables.refs_4_) | copy-start | bytes 3145732
  13.6 14.9 %all-to-all-start = ((f32[32,4,128]{2,1,0:T(4,128)}), f32[32,4,128]{2,1,0:T(4,128)S(1)}, u32[]{:S(2)}, u32[]{:S(2)}) async-start(f32[32,4,128]{2,1,0:T(4,128)} %shard_map.158), calls=%async_computation | async-start | bytes 131072 | tf_op jit(solution)/shard_map/all_to_all | solution.py:631
  42.2 11.3 %all-to-all-start.2 = ((f32[32,4,128]{2,1,0:T(4,128)}), f32[32,4,128]{2,1,0:T(4,128)S(1)}, u32[]{:S(2)}, u32[]{:S(2)}) async-start(f32[32,4,128]{2,1,0:T(4,128)} %shard_map.161), calls=%async_computation.2 | async-start | bytes 131072 | tf_op jit(solution)/shard_map/all_to_all | solution.py:631
  54.1 10.7 %all-to-all-start.3 = ((f32[32,4,128]{2,1,0:T(4,128)}), f32[32,4,128]{2,1,0:T(4,128)S(1)}, u32[]{:S(2)}, u32[]{:S(2)}) async-start(f32[32,4,128]{2,1,0:T(4,128)} %shard_map.163), calls=%async_computation.3 | async-start | bytes 131072 | tf_op jit(solution)/shard_map/all_to_all | solution.py:631
  57.0 34.8 %copy-start.4 = (bf16[2,2,64,256]{3,2,1,0:T(8,128)(2,1)S(1)}, bf16[2,2,64,256]{3,2,1,0:T(8,128)(2,1)}, u32[]{:S(2)}) copy-start(bf16[2,2,64,256]{3,2,1,0:T(8,128)(2,1)} %constant.26.clone.table) | copy-start | bytes 393220
  57.0 11.8 %collective-permute-start = (f32[32,512]{1,0:T(8,128)S(1)}, f32[32,512]{1,0:T(8,128)S(1)}, u32[]{:S(2)}, u32[]{:S(2)}) collective-permute-start(f32[32,512]{1,0:T(8,128)S(1)} %get-tuple-element.53), channel_id=1, source_target_pairs={{0,1},{1,0},{2,3},{3,2},{4,5},{5,4},{6,7},{7,6},{8,9},{9,8},{10,11... | collective-permute-start | bytes 196616 | tf_op jit(solution)/shard_map/ppermute | solution.py:717
  58.9 10.0 %collective-permute-start.1 = (f32[32,512]{1,0:T(8,128)S(1)}, f32[32,512]{1,0:T(8,128)S(1)}, u32[]{:S(2)}, u32[]{:S(2)}) collective-permute-start(f32[32,512]{1,0:T(8,128)S(1)} %get-tuple-element.54), channel_id=1, source_target_pairs={{0,2},{1,3},{2,0},{3,1},{4,6},{5,7},{6,4},{7,5},{8,10},{9,11},{10,... | collective-permute-start | bytes 196616 | tf_op jit(solution)/shard_map/ppermute | solution.py:717
  61.3 7.6 %collective-permute-start.2 = (f32[32,512]{1,0:T(8,128)S(1)}, f32[32,512]{1,0:T(8,128)S(1)}, u32[]{:S(2)}, u32[]{:S(2)}) collective-permute-start(f32[32,512]{1,0:T(8,128)S(1)} %get-tuple-element.55), channel_id=1, source_target_pairs={{0,3},{1,2},{2,1},{3,0},{4,7},{5,6},{6,5},{7,4},{8,11},{9,10},{10,... | collective-permute-start | bytes 196616 | tf_op jit(solution)/shard_map/ppermute | solution.py:717
  68.9 10.3 %all-to-all-start.4 = ((f32[32,4,128]{2,1,0:T(4,128)}), f32[32,4,128]{2,1,0:T(4,128)S(1)}, u32[]{:S(2)}, u32[]{:S(2)}) async-start(f32[32,4,128]{2,1,0:T(4,128)} %get-tuple-element.56), calls=%async_computation.4 | async-start | bytes 131072 | tf_op jit(solution)/shard_map/all_to_all | solution.py:631
Sparse Core Ops, SparseCore 0:
  9.9 31.8 all-gather.2

commit v3 on v2

--- a/solution.py
+++ b/solution.py
@@ -19,7 +19,6 @@
 HALF = 64
 BOTH = ("row", "col")
 COUNT, ROW, COL = 9, 10, 11
-NORTH_STEPS = 2
 MIB = 1024 * 1024
 SMALL, LARGE = 24 * MIB, 62 * MIB
 F32 = jnp.float32
@@ -28,6 +27,7 @@
 VMEM = pl.BlockSpec(memory_space=pltpu.VMEM)
 SMEM = pl.BlockSpec(memory_space=pltpu.SMEM)
 HBM = pl.BlockSpec(memory_space=pltpu.HBM)
+ANY = pl.BlockSpec(memory_space=pl.ANY)
 NN = (((1,), (0,)), ((), ()))
 NT = (((1,), (1,)), ((), ()))
 TN = (((0,), (0,)), ((), ()))
@@ -60,15 +60,14 @@
     return turns.astype(np.float32)
 
 
-def north_forward_table(cols):
+def north_forward_table():
     cos, sin = unit_turn(np.outer(np.arange(HALF), np.arange(LANES)), LANES)
     plain = np.concatenate(
         [np.concatenate([cos, sin], 1), np.concatenate([-sin, cos], 1)], 0
     )
     packed = plain.copy()
     packed[HALF, :LANES] = 1.0 - 2.0 * (np.arange(LANES) % 2)
-    order = np.arange(2 * HALF).reshape(2, cols, -1).transpose(1, 0, 2).reshape(-1)
-    return np.stack([split_table(packed[order]), split_table(plain[order])])
+    return np.stack([split_table(packed), split_table(plain)])
 
 
 def north_inverse_table():
@@ -189,18 +188,18 @@
     slots, width = tiles.shape[1:]
     parts = width // LANES
     squares = jnp.zeros((SUB, LANES), F32)
-    for group in range(0, FOOTPRINT, 3):
-        for k in range(group, group + 3):
+    for group, end in ((0, 4), (4, 8), (8, FOOTPRINT)):
+        for k in range(group, end):
             copies[k].wait()
         spread = [
             [jnp.broadcast_to(blocks[k][p : p + 1], (SUB, LANES)) for p in range(parts)]
-            for k in range(group, group + 3)
+            for k in range(group, end)
         ]
 
         def step(t, squares, group=group, spread=spread):
             at = pl.multiple_of(t * SUB, SUB)
             sums = [None] * parts
-            for k in range(3):
+            for k in range(len(spread)):
                 for p in range(parts):
                     tile = tiles[group + k, pl.ds(at, SUB), p * LANES : (p + 1) * LANES]
                     term = tile * spread[k][p]
@@ -208,11 +207,11 @@
             acc = functools.reduce(jnp.add, sums)
             if group > 0:
                 acc = acc + work[pl.ds(at, SUB), :]
-            if group + 3 < FOOTPRINT:
+            if group + len(spread) < FOOTPRINT:
                 work[pl.ds(at, SUB), :] = acc
                 return squares
             slot = at + lax.broadcasted_iota(jnp.int32, (SUB, LANES), 0)
-            value = jnp.where(slot < count, jnp.sum(acc, axis=1, keepdims=True), 0.0)
+            value = jnp.where(slot.astype(F32) < count, jnp.sum(acc, axis=1, keepdims=True), 0.0)
             if out is not None:
                 out[pl.ds(at, SUB), :] = value
             return squares + value * value
@@ -221,25 +220,26 @@
     return jnp.sum(squares, axis=0, keepdims=True)
 
 
-def apply_adjoint(tile, values, out, device):
+def apply_adjoint(tile, values):
     slots, width = tile.shape
-    for p in range(width // LANES):
-        sums = [None] * 4
-        for t in range(slots // SUB):
-            term = tile[t * SUB : (t + 1) * SUB, p * LANES : (p + 1) * LANES] * values[
-                t * SUB : (t + 1) * SUB, :
-            ]
-            sums[t % 4] = term if sums[t % 4] is None else sums[t % 4] + term
-        acc = functools.reduce(jnp.add, sums)
-        out[pl.ds(device, 1), p, :] = jnp.sum(acc, axis=0, keepdims=True)
+    parts = width // LANES
+    sums = [[None, None] for _ in range(parts)]
+    for t in range(slots // SUB):
+        rows = slice(t * SUB, (t + 1) * SUB)
+        weight = values[rows, :]
+        for p in range(parts):
+            term = tile[rows, p * LANES : (p + 1) * LANES] * weight
+            sums[p][t % 2] = term if t < 2 else sums[p][t % 2] + term
+    return jnp.concatenate([jnp.sum(a + b, axis=0, keepdims=True) for a, b in sums], axis=0)
 
 
 def send_adjoint(tile, values, k, ints, out, rows, cols):
     device, inside = neighbour(k, ints, rows, cols)
-
-    @pl.when(inside)
-    def _():
-        apply_adjoint(tile, values, out, device)
+    block = jnp.where(inside, apply_adjoint(tile, values), 0.0)
+    if len(out.shape) == 4:
+        out[device, 0] = out[device, 0] + block
+    else:
+        out[device] = out[device] + block
 
 
 def tile_copies(source, tiles, sems):
@@ -251,51 +251,122 @@
     return copies
 
 
-def start_kernel(rows, cols, ints, readings, source, out, tiles, values, sems):
+def start_kernel(
+    sizes, codes, counts, damping, readings, depth, inclinations, declinations, turns, hats, resid,
+    source, out, side, meta, codes_in, counts_in, damping_in, depth_in, angles, read, map_rows, tiles, values, sems, more,
+):
+    rows, cols, own, bands = sizes
+    row, col = lax.axis_index("row"), lax.axis_index("col")
+    _, turns_at, hats_at, end = side_rows(own, bands, rows)
+    pairs = [
+        (codes.at[0], codes_in),
+        (counts, counts_in),
+        (damping, damping_in),
+        (depth, depth_in),
+        (inclinations, angles.at[0]),
+        (declinations, angles.at[1]),
+        (readings.at[0], read),
+        (turns, side.at[turns_at:hats_at]),
+        (hats.at[row * cols + col], side.at[hats_at:end]),
+        (resid, map_rows),
+    ]
+    first = [pltpu.make_async_copy(a, b, more.at[n]) for n, (a, b) in enumerate(pairs)]
+    for copy in first:
+        copy.start()
     copies = tile_copies(source, tiles, sems)
     out[...] = jnp.zeros(out.shape, F32)
-    slots = readings.shape[1]
+    for copy in first:
+        copy.wait()
+    if len(out.shape) == 4:
+        place_rows(out, lambda d, g: map_rows[(4 * d + g) * 4 : (4 * d + g + 1) * 4])
+    ints = [codes_in[0, k] for k in range(FOOTPRINT)] + [counts_in[0, 0], row, col]
+    meta[0:1, :] = jnp.full((1, LANES), counts_in[0, 0].astype(F32), F32)
+    meta[1:2, :] = jnp.full((1, LANES), damping_in[0], F32)
+    slots = read.shape[1]
     slot = lax.broadcasted_iota(jnp.int32, (1, slots), 1)
-    live = jnp.where(slot < ints[COUNT], readings[...], 0.0)
+    live = jnp.where(slot < ints[COUNT], read[...], 0.0)
     for t in range(slots // LANES):
         square = jnp.broadcast_to(live[:, t * LANES : (t + 1) * LANES], (LANES, LANES))
         values[t * LANES : (t + 1) * LANES, :] = square.T
+    trig = []
+    for m in range(2):
+        up = jnp.full((1, LANES), angles[0, m], F32)
+        turn = jnp.full((1, LANES), angles[1, m], F32)
+        flat = jnp.cos(up)
+        trig += [jnp.sin(up), flat * jnp.cos(turn), flat * jnp.sin(turn)]
+    put_weights(sizes, row, col, [depth_in[l] for l in range(LAYERS)], trig, side)
     for k in range(FOOTPRINT):
         copies[k].wait()
         send_adjoint(tiles.at[k], values, k, ints, out, rows, cols)
 
 
+def place_rows(out, get):
+    for d in range(out.shape[0]):
+        for g in range(out.shape[1] - 1):
+            out[d, 1 + g] = get(d, g)
+
+
 def gather_kernel(arrived, everywhere):
-    block = jnp.sum(arrived[...], axis=0)
+    block = jnp.sum(arrived[:, 0] if len(arrived.shape) == 4 else arrived[...], axis=0)
     everywhere[...] = jnp.broadcast_to(block[None], everywhere.shape)
 
 
-def normal_kernel(rows, cols, ints, floats, source, vector, out, tiles, sems, values, work):
+def normal_kernel(
+    rows, cols, codes, meta, source, vector, arrived, turns, table, out, *refs
+):
+    (*apart, codes_in, tiles, sems, values, work, planes, codes_sem) = refs
+    fetch = pltpu.make_async_copy(codes.at[0], codes_in, codes_sem.at[0])
+    fetch.start()
     copies = tile_copies(source, tiles, sems)
+    row, col = lax.axis_index("row"), lax.axis_index("col")
+    fetch.wait()
+    ints = [codes_in[0, k] for k in range(FOOTPRINT)] + [None, row, col]
     blocks = near_blocks(ints, vector, rows, cols)
-    apply_forward(tiles, copies, blocks, ints[COUNT], values, work)
+    me = row * cols + col
     out[...] = jnp.zeros(out.shape, F32)
+    ridge = meta[1:2, :] * vector[me]
+    if apart:
+        out[me] = ridge
+    else:
+        out[me, 0] = ridge
+
+    def store(device, piece):
+        if apart:
+            apart[0][device] = piece
+        else:
+            for g in range(out.shape[1] - 1):
+                out[device, 1 + g] = piece[4 * g : 4 * g + 4]
+
+    north_transform(rows, cols, arrived, turns, table, planes, store)
+    apply_forward(tiles, copies, blocks, meta[0:1, :], values, work)
     for k in range(FOOTPRINT):
         send_adjoint(tiles.at[k], values, k, ints, out, rows, cols)
-    me = ints[ROW] * cols + ints[COL]
-    out[me] = out[me] + floats[0] * vector[me]
-
-
-def north_kernel(cols, ints, planes, turns, table, *outs):
-    outs, mixed = outs[:-1], outs[-1]
-    rows = planes.shape[0]
-    re = planes[0] * turns[0, 0, 0:1]
-    im = planes[0] * turns[1, 0, 0:1]
-    for r in range(1, rows):
-        re = re + planes[r] * turns[0, 0, r : r + 1]
-        im = im + planes[r] * turns[1, 0, r : r + 1]
-    both = jnp.concatenate([re, im], axis=1)
-    result = table_mul(table[0, 0], table[0, 1], both, NT)
-    own2 = outs[0].shape[0]
-    for col in range(cols):
-        mixed[col] = result[col * own2 : (col + 1) * own2]
-    for step in range(cols):
-        outs[step][...] = mixed[ints[COL] ^ step]
+
+
+def north_transform(rows, cols, arrived, turns, table, planes, store):
+    width = planes.shape[1]
+    each = width // cols
+    own = HALF // cols
+    for i in range(rows):
+        for j in range(cols):
+            if len(arrived.shape) == 4:
+                for g in range(each // 4):
+                    at = j * each + 4 * g
+                    planes[i, at : at + 4, :] = arrived[i * cols + j, 1 + g]
+            else:
+                planes[i, j * each : (j + 1) * each, :] = arrived[i * cols + j]
+    for group in range(rows):
+        re = planes[0] * turns[0, group, 0:1]
+        im = planes[0] * turns[1, group, 0:1]
+        for i in range(1, rows):
+            re = re + planes[i] * turns[0, group, i : i + 1]
+            im = im + planes[i] * turns[1, group, i : i + 1]
+        kind = min(group, 1)
+        both = jnp.concatenate([re, im], axis=1)
+        result = table_mul(table[kind, 0], table[kind, 1], both, NT)
+        for j in range(cols):
+            real, imag = result[j * own : (j + 1) * own], result[HALF + j * own : HALF + (j + 1) * own]
+            store(group * cols + j, jnp.concatenate([real, imag], axis=1))
 
 
 def pole(north, east, trig):
@@ -314,12 +385,9 @@
     return span, turns, turns + 2 * bands, turns + 2 * bands + 2 * rows
 
 
-def filter_kernel(rows, cols, own, bands, ints, floats, turns, hats, side):
-    span, turns_at, hats_at, end = side_rows(own, bands, rows)
-    side[turns_at:hats_at, :] = turns[...]
-    side[hats_at:end, :] = hats[0]
-    depth = [floats[1 + l] for l in range(LAYERS)]
-    trig = [floats[1 + LAYERS + t] for t in range(6)]
+def put_weights(sizes, row, col, depth, trig, side):
+    rows, _, own, bands = sizes
+    span = side_rows(own, bands, rows)[0]
 
     def put(part, q, at, value):
         base = (part * (1 + LAYERS) + q) * span + at
@@ -327,7 +395,6 @@
 
     north_len, east_len = rows * LANES, bands * LANES
     scale = 1.0 / (north_len * east_len)
-    row, col = ints[ROW], ints[COL]
     start = jnp.where(
         row == 0, 0, jnp.where(row == 1, rows // 2, row // 2 + HALF * rows * (row % 2))
     )
@@ -492,10 +559,11 @@
     return out
 
 
-def model_response(vector, sizes, side, tables, store, coarse, fine, work, mixed, back):
+def model_mix(vector, scale, sizes, side, tables, coarse, fine, work, mixed, first):
     rows, cols, own, bands = sizes
     depth = cols * SRC_COLS
-    high, low = split(jnp.concatenate(model_rows(vector, sizes, side, coarse), axis=0))
+    planes = jnp.concatenate(model_rows(vector, sizes, side, coarse), axis=0)
+    high, low = split(planes if scale is None else planes * scale)
     for c in range(bands // 2):
         at = 8 * LANES + c * depth
         table = tables[at : at + depth, :]
@@ -508,16 +576,48 @@
             return fine[at : at + SUB, cut], fine[at + own : at + own + SUB, cut]
 
         spectrum = east_forward(get, sizes, side, tables, work)
-        weigh(spectrum, 1 + layer, sizes, side, mixed, layer == 0)
-    east_inverse(mixed, sizes, side, tables, back, store)
-
-
-def resid_kernel(sizes, width, ints, *refs):
+        weigh(spectrum, 1 + layer, sizes, side, mixed, first and layer == 0)
+
+
+def swap_groups(values, size):
+    group = lax.broadcasted_iota(jnp.int32, values[0].shape, 1) // size
+    bit = len(values) // 2
+    while bit:
+        low = (group & bit) == 0
+        for s in range(len(values)):
+            if not s & bit:
+                x, y = values[s], values[s | bit]
+                values[s] = jnp.where(low, x, pltpu.roll(y, bit * size, 1))
+                values[s | bit] = jnp.where(low, pltpu.roll(x, LANES - bit * size, 1), y)
+        bit //= 2
+    return values
+
+
+def sort_east(arrived, sizes, spec):
     rows, cols, own, bands = sizes
-    arrived, (tables, side, out, spec, work, mixed, back) = refs[:cols], refs[cols:]
-    per = arrived[0].shape[1] // LANES
-    for step in range(cols):
-        spec[ints[COL] ^ step] = arrived[step][...]
+    count = 2 * cols
+    for a in range(rows * cols // count):
+        for g in range(own // SUB):
+            values = []
+            for s in range(count):
+                at = 1 + 2 * g
+                both = [arrived[a * count + s, at], arrived[a * count + s, at + 1]]
+                values.append(jnp.concatenate(both, axis=0))
+            values = swap_groups(values, LANES // count)
+            for t in range(count):
+                at = (t // cols) * own + g * SUB
+                spec[t % cols, at : at + SUB, a * LANES : (a + 1) * LANES] = values[t]
+
+
+def map_kernel(
+    sizes, width, arrived, first, second, carry, tables, side, known, response,
+    coarse, fine, work, mixed, back, *spec,
+):
+    rows, cols, own, bands = sizes
+    if spec:
+        sort_east(arrived, sizes, spec[0])
+    spec = spec[0] if spec else arrived
+    per = spec.shape[2] // LANES
 
     def get(m, g):
         cut = slice((m % per) * LANES, (m % per + 1) * LANES)
@@ -526,48 +626,53 @@
 
     spectrum = east_forward(get, sizes, side, tables, work)
     weigh(spectrum, 0, sizes, side, mixed, True)
-    east_inverse(mixed, sizes, side, tables, back, store_pieces(out, width))
-
-
-def first_kernel(sizes, width, vector, tables, side, out, *work):
-    model_response(vector, sizes, side, tables, store_pieces(out, width), *work)
+    model_mix(first, carry[4, 0:1, 0:1], sizes, side, tables, coarse, fine, work, mixed, False)
+    east_inverse(mixed, sizes, side, tables, back, store_pieces(known, width))
+    model_mix(second, None, sizes, side, tables, coarse, fine, work, mixed, True)
+    east_inverse(mixed, sizes, side, tables, back, store_pieces(response, width))
 
 
 def direction_kernel(
-    rows, cols, ints, floats, source, first, applied, second, measured, carry, tiles, sems, work
+    rows, cols, codes, meta, source, first, applied, second, measured, carry,
+    codes_in, tiles, sems, work, codes_sem,
 ):
+    fetch = pltpu.make_async_copy(codes.at[0], codes_in, codes_sem.at[0])
+    fetch.start()
     copies = tile_copies(source, tiles, sems)
+    row, col = lax.axis_index("row"), lax.axis_index("col")
     norm = total(first[...] * first[...])
     step = norm / total(first[...] * applied[...])
     residual = first[...] - step[None] * applied[...]
     norm_next = total(residual * residual)
     second[...] = residual + (norm_next / norm)[None] * first[...]
-    blocks = near_blocks(ints, second, rows, cols)
-    squares = apply_forward(tiles, copies, blocks, ints[COUNT], None, work)
-    measured[...] = jnp.broadcast_to(squares[None], measured.shape)
-    ridge = floats[0] * total(second[...] * second[...])
-    me = ints[ROW] * cols + ints[COL]
+    ridge = meta[1:2, 0:1] * total(second[...] * second[...])
+    me = row * cols + col
     carry[0] = step * first[me]
     carry[1] = second[me]
     for at, value in ((2, norm_next), (3, ridge), (4, step)):
         carry[at] = jnp.broadcast_to(value, carry.shape[1:])
-
-
-def second_kernel(sizes, width, vector, tables, side, early, early_first, carry, known, out, *work):
-    known[...] = early[...] + carry[4, 0:1, 0:1][None] * early_first[...]
-    model_response(vector, sizes, side, tables, store_pieces(out, width), *work)
-
-
-def combine_kernel(measured, carry, known, response, out, coefficients):
+    fetch.wait()
+    ints = [codes_in[0, k] for k in range(FOOTPRINT)] + [None, row, col]
+    blocks = near_blocks(ints, second, rows, cols)
+    squares = apply_forward(tiles, copies, blocks, meta[0:1, :], None, work)
+    measured[...] = jnp.broadcast_to(squares[None], measured.shape)
+
+
+def last_step(measured, carry):
     squares = jnp.sum(measured[:, 0:1], axis=0)
-    step = carry[2, 0:1, 0:1] / (squares[:, 0:1] + carry[3, 0:1, 0:1])
-    out[...] = known[...] + step[None] * response[...]
-    solved = carry[0] + step * carry[1]
+    return carry[2, 0:1, 0:1] / (squares[:, 0:1] + carry[3, 0:1, 0:1])
+
+
+def combine_kernel(measured, carry, known, response, out):
+    out[...] = known[...] + last_step(measured, carry)[None] * response[...]
+
+
+def finish_kernel(
+    rows, cols, arrived, measured, carry, turns, table, coefficients, out, mixed, waves
+):
+    solved = carry[0] + last_step(measured, carry) * carry[1]
     for p in range(solved.shape[0]):
         coefficients[:, p * LANES : (p + 1) * LANES] = solved[p : p + 1]
-
-
-def finish_kernel(rows, cols, arrived, turns, table, out, mixed, waves):
     own = arrived.shape[1]
     width = out.shape[0]
     for i in range(rows):
@@ -609,24 +714,6 @@
     )(*[value for _, value in ins])
 
 
-def placed_call(kernel, out, ints, ins, work=(), limit=SMALL, steps=1, out_block=None):
-    def whole(a):
-        return pl.BlockSpec(a.shape, lambda step, at, n=a.ndim: (0,) * n)
-
-    return pl.pallas_call(
-        kernel,
-        out_shape=out,
-        grid_spec=pltpu.PrefetchScalarGridSpec(
-            num_scalar_prefetch=1,
-            grid=(steps,),
-            in_specs=[whole(value) if spec is None else spec for spec, value in ins],
-            out_specs=whole(out) if out_block is None else out_block,
-            scratch_shapes=list(work),
-        ),
-        compiler_params=pltpu.CompilerParams(vmem_limit_bytes=limit),
-    )(ints, *[value for _, value in ins])
-
-
 def exchange(pieces):
     return lax.all_to_all(pieces, BOTH, 0, 0, tiled=True)
 
@@ -637,8 +724,6 @@
 ):
     rows, cols = lax.axis_size("row"), lax.axis_size("col")
     devices = rows * cols
-    place = jnp.stack([lax.axis_index("row"), lax.axis_index("col")]).astype(jnp.int32)
-    ints = jnp.concatenate([footprints.reshape(-1), counts.reshape(-1), place])
     slots, sources = kernel_tiles.shape[3:]
     parts = sources // LANES
     tile_east = resid_grid.shape[0]
@@ -652,123 +737,121 @@
     tables, east_turns = east_tables(east)
     hats = north_hat_table(rows, cols)
 
-    planes = lax.all_gather(resid_grid, "row", axis=0)
-
-    kernel_tiles = pltpu.with_memory_space_constraint(kernel_tiles, pltpu.HBM)
+    joined = 2 * width == LANES
+    everywhere = shape(devices, parts, LANES)
+    beside = shape(devices, 1 + own // 4, 4, LANES) if joined else everywhere
+    pieces = shape(devices, own, 2 * width)
+
+    def apart(value):
+        return HBM, pltpu.with_memory_space_constraint(value, pltpu.HBM)
+
     tile_scratch = scratch(FOOTPRINT, slots, sources)
     tile_sems = pltpu.SemaphoreType.DMA((FOOTPRINT,))
-
-    sums = call(
-        functools.partial(start_kernel, rows, cols),
-        shape(devices, parts, LANES),
-        [(SMEM, ints), (VMEM, readings.reshape(1, slots)), (HBM, kernel_tiles)],
-        [tile_scratch, scratch(slots, LANES), tile_sems],
-    )
-    sums, damping, layer_depth, inclinations, declinations = lax.optimization_barrier(
-        (sums, damping, layer_depth, inclinations, declinations)
-    )
-    flat = jnp.cos(inclinations)
-    trig = [jnp.sin(inclinations), flat * jnp.cos(declinations), flat * jnp.sin(declinations)]
-    floats = jnp.concatenate([damping, layer_depth, jnp.stack(trig, axis=1).reshape(-1)])
-    side = placed_call(
-        functools.partial(filter_kernel, rows, cols, own, bands),
-        shape(side_rows(own, bands, rows)[-1], LANES),
-        ints,
+    codes_scratch = pltpu.SMEM((1, FOOTPRINT), jnp.int32)
+    one_sem = pltpu.SemaphoreType.DMA((1,))
+    resid = resid_grid if joined else resid_grid[:SUB]
+
+    sums, side, meta = call(
+        functools.partial(start_kernel, sizes),
+        (beside, shape(side_rows(own, bands, rows)[-1], LANES), shape(2, LANES)),
+        [apart(footprints), (ANY, counts), (ANY, damping)]
+        + [
+            apart(value)
+            for value in (
+                readings, layer_depth, inclinations, declinations,
+                jnp.asarray(east_turns), jnp.asarray(hats), resid, kernel_tiles,
+            )
+        ],
         [
-            (SMEM, floats),
-            (None, east_turns),
-            (pl.BlockSpec((1,) + hats.shape[1:], lambda _, at: (at[ROW] * cols + at[COL], 0, 0)), hats),
+            codes_scratch,
+            pltpu.SMEM((1, 1), jnp.int32),
+            pltpu.SMEM((1,), F32),
+            pltpu.SMEM((LAYERS,), F32),
+            pltpu.SMEM((2, 2), F32),
+            scratch(1, slots),
+            scratch(*resid.shape),
+            tile_scratch,
+            scratch(slots, LANES),
+            tile_sems,
+            pltpu.SemaphoreType.DMA((10,)),
         ],
     )
-    everywhere = shape(devices, parts, LANES)
-    right_all = call(gather_kernel, everywhere, [(VMEM, exchange(sums))])
-    right_all, side = lax.optimization_barrier((right_all, side))
+    sums = exchange(sums)
+    right_all = call(gather_kernel, everywhere, [(VMEM, sums)])
+    if not joined:
+        right_all, resid_grid = lax.optimization_barrier((right_all, resid_grid))
+    planes = sums if joined else exchange(resid_grid.reshape(devices, -1, LANES))
     right_side = exchange(right_all)
 
     sums = call(
         functools.partial(normal_kernel, rows, cols),
-        everywhere,
-        [(SMEM, ints), (SMEM, floats), (HBM, kernel_tiles), (VMEM, right_side)],
-        [tile_scratch, tile_sems, scratch(slots, LANES), scratch(slots, LANES)],
-    )
-    sums, planes, right_side = lax.optimization_barrier((sums, planes, right_side))
-    chunk = tile_east // NORTH_STEPS
-    spectra = placed_call(
-        functools.partial(north_kernel, cols),
-        [shape(2 * own, tile_east)] * cols,
-        ints,
+        beside if joined else (everywhere, pieces),
         [
-            (pl.BlockSpec((rows, chunk, LANES), lambda c, at: (0, c, 0)), pltpu.with_memory_space_constraint(planes, pltpu.HBM)),
-            (pl.BlockSpec((2, 1, rows, LANES), lambda c, at: (0, at[ROW], 0, 0)), turns),
-            (
-                pl.BlockSpec(
-                    (1, 2, 2 * HALF, 2 * LANES), lambda c, at: (jnp.minimum(at[ROW], 1), 0, 0, 0)
-                ),
-                north_forward_table(cols),
-            ),
+            apart(footprints),
+            (VMEM, meta),
+            apart(kernel_tiles),
+            (VMEM, right_side),
+            (VMEM, planes),
+            (VMEM, turns),
+            (VMEM, north_forward_table()),
         ],
-        [scratch(cols, 2 * own, chunk)],
-        steps=NORTH_STEPS,
-        out_block=[pl.BlockSpec((2 * own, chunk), lambda c, at: (0, c))] * cols,
-        limit=48 * MIB,
-    )
-    right_side, spectra = lax.optimization_barrier((right_side, spectra))
-    spectra = list(spectra[:1]) + [
-        lax.ppermute(spectra[s], "col", [(c, c ^ s) for c in range(cols)]) for s in range(1, cols)
-    ]
+        [codes_scratch, tile_scratch, tile_sems, scratch(slots, LANES), scratch(slots, LANES)]
+        + [scratch(rows, width, LANES), one_sem],
+    )
+    if not joined:
+        sums, spectrum = sums
+    sums = exchange(sums)
+    applied_all = call(gather_kernel, everywhere, [(VMEM, sums)])
+    applied = exchange(applied_all)
+    if joined:
+        spectrum, sorted_work = sums, [scratch(cols, 2 * own, tile_east)]
+    else:
+        spectrum, sorted_work = exchange(spectrum), []
+        spectrum = spectrum.reshape(devices, own, 2, cols, width // cols).transpose(3, 2, 1, 0, 4)
+        spectrum = spectrum.reshape(cols, 2 * own, tile_east)
+
+    second, measured, carry = call(
+        functools.partial(direction_kernel, rows, cols),
+        (everywhere, everywhere, shape(5, parts, LANES)),
+        [apart(footprints), (VMEM, meta), apart(kernel_tiles), (VMEM, right_side), (VMEM, applied)],
+        [codes_scratch, tile_scratch, tile_sems, scratch(slots, LANES), one_sem],
+    )
     work = [
+        scratch(LAYERS, 2 * rows, cols * LANES),
+        scratch(LAYERS * 2 * own, east),
         scratch((own + 1) * bands, 2 * LANES),
         scratch(own * bands, 2 * LANES),
         scratch(own * bands, 2 * LANES),
     ]
-    model_work = [scratch(LAYERS, 2 * rows, cols * LANES), scratch(LAYERS * 2 * own, east)] + work
-    pieces = shape(devices, own, 2 * width)
-    early_first = call(
-        functools.partial(first_kernel, sizes, width),
-        pieces,
-        [(VMEM, right_side), (VMEM, tables), (VMEM, side)],
-        model_work,
-    )
-    applied_all = call(gather_kernel, everywhere, [(VMEM, exchange(sums))])
-    applied_all, early_first = lax.optimization_barrier((applied_all, early_first))
-    applied = exchange(applied_all)
-
-    second, measured, carry = call(
-        functools.partial(direction_kernel, rows, cols),
-        (everywhere, everywhere, shape(5, parts, LANES)),
-        [(SMEM, ints), (SMEM, floats), (HBM, kernel_tiles), (VMEM, right_side), (VMEM, applied)],
-        [tile_scratch, tile_sems, scratch(slots, LANES)],
-    )
-    measured, spectra = lax.optimization_barrier((measured, spectra))
-    early = call(
-        functools.partial(resid_kernel, sizes, width),
-        pieces,
-        [(SMEM, ints)] + [(VMEM, part) for part in spectra] + [(VMEM, tables), (VMEM, side)],
-        [scratch(cols, 2 * own, tile_east)] + work,
-    )
-
     known, response = call(
-        functools.partial(second_kernel, sizes, width),
+        functools.partial(map_kernel, sizes, width),
         (pieces, pieces),
         [
+            (VMEM, spectrum),
+            (VMEM, right_side),
             (VMEM, second),
+            (VMEM, carry),
             (VMEM, tables),
             (VMEM, side),
-            (VMEM, early),
-            (VMEM, early_first),
+        ],
+        work + sorted_work,
+    )
+    measured = exchange(measured)
+    outgoing = call(
+        combine_kernel,
+        pieces,
+        [(VMEM, measured), (VMEM, carry), (VMEM, known), (VMEM, response)],
+    )
+    coefficients, rtp_map = call(
+        functools.partial(finish_kernel, rows, cols),
+        (shape(1, sources), shape(width, rows * LANES)),
+        [
+            (VMEM, exchange(outgoing)),
+            (VMEM, measured),
             (VMEM, carry),
+            (VMEM, turns),
+            (VMEM, north_inverse_table()),
         ],
-        model_work,
-    )
-    outgoing, coefficients = call(
-        combine_kernel,
-        (pieces, shape(1, sources)),
-        [(VMEM, exchange(measured)), (VMEM, carry), (VMEM, known), (VMEM, response)],
-    )
-    rtp_map = call(
-        functools.partial(finish_kernel, rows, cols),
-        shape(width, rows * LANES),
-        [(VMEM, exchange(outgoing)), (VMEM, turns), (VMEM, north_inverse_table())],
         [scratch(rows, HALF, 2 * width), scratch(rows, width, 2 * LANES)],
     )
     return coefficients.reshape(1, 1, sources), rtp_map

time: 100 us -> 87.9 us (0.88)
  blocking collectives: 21.1 us -> 64 us
  starting transfers between devices: 21.3 us -> 2.59 us
  between operations: 15.6 us -> 2.05 us
  waiting for transfers between devices: 16.4 us -> 3.8 us
  Pallas kernels: 23.9 us -> 15.2 us
    all_to_all x2 -> x5, blocking collectives: 21.1 us -> 64 us  [exchange(): return lax.all_to_all(pieces, BOTH, 0, 0, tiled=True)]
    all_to_all x4 -> x1, starting transfers between devices: 16.8 us -> 2.59 us  [exchange(): return lax.all_to_all(pieces, BOTH, 0, 0, tiled=True)]
    all_to_all x4 -> x1, waiting for transfers between devices: 15.7 us -> 3.8 us  [exchange(): return lax.all_to_all(pieces, BOTH, 0, 0, tiled=True)]
    pallas_call x10 -> x8, Pallas kernels: 19.9 us -> 15.2 us  [call(): pl.pallas_call(kernel, out_shape=outs, in_specs=[spec for spec, _ in ins]...]
    ppermute x3 -> x0, starting transfers between devices: 4.45 us -> none  [on_device(): lax.ppermute(spectra[s], 'col', [(c, c ^ s) for c in range(cols)])]
    pallas_call x2 -> x0, Pallas kernels: 3.97 us -> none  [placed_call(): pl.pallas_call(kernel, out_shape=out, grid_spec=pltpu.PrefetchScalarGridS...]
  transfers between devices with their start and end apart: 8 -> 1, of which waited for: 4 -> 1; matrix products, arithmetic and copies ran while one was open for 1% -> 0% of each run, Pallas kernels for 21% -> 4%
where the time goes in v3:
time: 87.9 us; the launch traced here: 87.7 us
  blocking collectives  64 us (73%)
  Pallas kernels  15.2 us (17%)
  waiting for transfers between devices  3.8 us (4%)
  starting transfers between devices  2.59 us (3%)
  between operations  2.05 us (2%)
    all_to_all x5, blocking collectives, exchange(): return lax.all_to_all(pieces, BOTH, 0, 0, tiled=True)  64 us
    pallas_call x8, Pallas kernels, call(): pl.pallas_call(kernel, out_shape=outs, in_specs=[spec for spec, _ in ins]...  15.2 us
    all_to_all x1, waiting for transfers between devices, exchange(): return lax.all_to_all(pieces, BOTH, 0, 0, tiled=True)  3.8 us
    all_to_all x1, starting transfers between devices, exchange(): return lax.all_to_all(pieces, BOTH, 0, 0, tiled=True)  2.59 us
  transfers between devices with their start and end apart: 1, of which 1 were waited for; matrix products, arithmetic and copies ran while one was open for 0% of the time, Pallas kernels for 4%

profile of v3, /device:TPU:0, one launch (start us, length us, event | category | flops | bytes accessed | tf_op | source)
XLA Modules:
  0.0 87.7 jit_solution(17557117461396575134)
XLA Ops:
  0.6 0.0 copy-start.1
  0.6 0.0 copy-start.2
  2.0 3.2 %shard_map.158 = (f32[32,5,4,128]{3,2,1,0:T(4,128)S(1)}, f32[1680,128]{1,0:T(8,128)S(1)}, f32[2,128]{1,0:T(2,128)S(1)}) custom-call(s32[1,1,9]{2,1,0:T(1,128)} %codes.5, s32[1,1]{1,0:T(1,128)S(6)} %copy.17.counts, f32[1]{0:T(128)S(6)} %copy.18.damping, f32[1,1,256]{2,1,0:T(1,128)} %readings.1, f32[2]{0:T(128)} %depth.1, f32[2]{0:T(128)} %inclinations.1, ...), custom_call_target="tpu_custom_call" | custom-call | tf_op jit(solution)/shard_map/pallas_call | solution.py:707
  5.2 18.0 %all_to_all.30.arrived = f32[32,5,4,128]{3,2,1,0:T(4,128)S(1)} all-to-all(f32[32,5,4,128]{3,2,1,0:T(4,128)S(1)} %get-tuple-element.13), channel_id=1, replica_groups=mesh['row'=8,'col'=4] {'row','col'}, dimensions={0} | all-to-all | bytes 655360 | tf_op jit(solution)/shard_map/all_to_all | solution.py:718
  23.3 10.6 %all_to_all.31.vector.first = f32[32,4,128]{2,1,0:T(4,128)S(1)} all-to-all(f32[32,4,128]{2,1,0:T(4,128)S(1)} %shard_map.159), channel_id=1, replica_groups=mesh['row'=8,'col'=4] {'row','col'}, dimensions={0} | all-to-all | bytes 131072 | tf_op jit(solution)/shard_map/all_to_all | solution.py:718
  33.9 0.0 copy-done.1
  33.9 0.0 copy-done.2
  33.9 0.0 copy-start
  33.9 3.2 %shard_map.160 = f32[32,5,4,128]{3,2,1,0:T(4,128)S(1)} custom-call(s32[1,1,9]{2,1,0:T(1,128)} %codes.5, f32[2,128]{1,0:T(2,128)S(1)} %get-tuple-element.12.meta, f32[1,1,9,256,512]{4,3,2,1,0:T(8,128)} %source.5, f32[32,4,128]{2,1,0:T(4,128)S(1)} %all_to_all.31.vector.first, f32[32,5,4,128]{3,2,1,0:T(4,128)S(1)} %all_to_all.30.arrived, ...), custom_call_target="tpu_custom_call" | custom-call | tf_op jit(solution)/shard_map/pallas_call | solution.py:707
  37.1 12.7 %all_to_all.32.arrived = f32[32,5,4,128]{3,2,1,0:T(4,128)S(1)} all-to-all(f32[32,5,4,128]{3,2,1,0:T(4,128)S(1)} %shard_map.160), channel_id=1, replica_groups=mesh['row'=8,'col'=4] {'row','col'}, dimensions={0} | all-to-all | bytes 655360 | tf_op jit(solution)/shard_map/all_to_all | solution.py:718
  49.8 0.0 copy-start.3
  49.9 10.6 %all_to_all.33.applied = f32[32,4,128]{2,1,0:T(4,128)S(1)} all-to-all(f32[32,4,128]{2,1,0:T(4,128)S(1)} %shard_map.161), channel_id=1, replica_groups=mesh['row'=8,'col'=4] {'row','col'}, dimensions={0} | all-to-all | bytes 131072 | tf_op jit(solution)/shard_map/all_to_all | solution.py:718
  60.5 3.5 %shard_map.162 = (f32[32,4,128]{2,1,0:T(4,128)S(1)}, f32[32,4,128]{2,1,0:T(4,128)}, f32[5,4,128]{2,1,0:T(4,128)S(1)}) custom-call(s32[1,1,9]{2,1,0:T(1,128)} %codes.5, f32[2,128]{1,0:T(2,128)S(1)} %get-tuple-element.12.meta, f32[1,1,9,256,512]{4,3,2,1,0:T(8,128)} %source.5, f32[32,4,128]{2,1,0:T(4,128)S(1)} %all_to_all.31.vector.first, ...), custom_call_target="tpu_custom_call" | custom-call | tf_op jit(solution)/shard_map/pallas_call | solution.py:707
  64.0 2.6 %all-to-all-start.4 = ((f32[32,4,128]{2,1,0:T(4,128)}), f32[32,4,128]{2,1,0:T(4,128)S(1)}, u32[]{:S(2)}, u32[]{:S(2)}) async-start(f32[32,4,128]{2,1,0:T(4,128)} %get-tuple-element.14), calls=%async_computation.4 | async-start | bytes 131072 | tf_op jit(solution)/shard_map/all_to_all | solution.py:718
  66.6 0.0 copy-done
  66.6 3.7 %shard_map.163 = (f32[32,16,128]{2,1,0:T(8,128)S(1)}, f32[32,16,128]{2,1,0:T(8,128)S(1)}) custom-call(f32[32,5,4,128]{3,2,1,0:T(4,128)S(1)} %all_to_all.32.arrived, f32[32,4,128]{2,1,0:T(4,128)S(1)} %all_to_all.31.vector.first, f32[32,4,128]{2,1,0:T(4,128)S(1)} %get-tuple-element.16.second, f32[5,4,128]{2,1,0:T(4,128)S(1)} %get-tuple-element.15.carry, ...), custom_call_target="tpu_custom_call" | custom-call | tf_op jit(solution)/shard_map/pallas_call | solution.py:707
  70.3 3.8 %all-to-all-done.4.measured = f32[32,4,128]{2,1,0:T(4,128)S(1)} async-done(((f32[32,4,128]{2,1,0:T(4,128)}), f32[32,4,128]{2,1,0:T(4,128)S(1)}, u32[]{:S(2)}, u32[]{:S(2)}) %all-to-all-start.4) | async-done | bytes 65568 | tf_op jit(solution)/shard_map/all_to_all | solution.py:718
  74.1 0.1 shard_map.164
  74.2 12.1 %all_to_all.34.arrived = f32[32,16,128]{2,1,0:T(8,128)S(1)} all-to-all(f32[32,16,128]{2,1,0:T(8,128)S(1)} %shard_map.164), channel_id=1, replica_groups=mesh['row'=8,'col'=4] {'row','col'}, dimensions={0} | all-to-all | bytes 524288 | tf_op jit(solution)/shard_map/all_to_all | solution.py:718
  86.2 0.0 copy-done.3
  86.2 1.4 %shard_map.165 = (f32[1,512]{1,0:T(1,128)}, f32[64,1024]{1,0:T(8,128)}) custom-call(f32[32,16,128]{2,1,0:T(8,128)S(1)} %all_to_all.34.arrived, f32[32,4,128]{2,1,0:T(4,128)S(1)} %all-to-all-done.4.measured, f32[5,4,128]{2,1,0:T(4,128)S(1)} %get-tuple-element.15.carry, f32[2,8,8,128]{3,2,1,0:T(8,128)S(1)} %copy-done.1, bf16[2,2,64,256]{3,2,1,0:T(8,128)(2,1)S(1)} %copy-done.3), custom_call_target="tpu_custom_call" | custom-call | tf_op jit(solution)/shard_map/pallas_call | solution.py:707
  (2 shorter events, 0.1 us)
Async XLA Ops:
  0.6 33.3 %copy-start.1 = (f32[2,8,8,128]{3,2,1,0:T(8,128)S(1)}, f32[2,8,8,128]{3,2,1,0:T(8,128)}, u32[]{:S(2)}) copy-start(f32[2,8,8,128]{3,2,1,0:T(8,128)} %constant.14.clone.turns) | copy-start | bytes 196612
  0.6 33.3 %copy-start.2 = (bf16[2,2,128,256]{3,2,1,0:T(8,128)(2,1)S(1)}, bf16[2,2,128,256]{3,2,1,0:T(8,128)(2,1)}, u32[]{:S(2)}) copy-start(bf16[2,2,128,256]{3,2,1,0:T(8,128)(2,1)} %constant.15.clone.table) | copy-start | bytes 786436
  33.9 32.6 %copy-start = (bf16[2048,256]{1,0:T(8,128)(2,1)S(1)}, bf16[2048,256]{1,0:T(8,128)(2,1)}, u32[]{:S(2)}) copy-start(bf16[2048,256]{1,0:T(8,128)(2,1)} %constant.16.clone.tables) | copy-start | bytes 3145732
  49.8 36.4 %copy-start.3 = (bf16[2,2,64,256]{3,2,1,0:T(8,128)(2,1)S(1)}, bf16[2,2,64,256]{3,2,1,0:T(8,128)(2,1)}, u32[]{:S(2)}) copy-start(bf16[2,2,64,256]{3,2,1,0:T(8,128)(2,1)} %constant.17.clone.table) | copy-start | bytes 393220
  64.0 10.1 %all-to-all-start.4 = ((f32[32,4,128]{2,1,0:T(4,128)}), f32[32,4,128]{2,1,0:T(4,128)S(1)}, u32[]{:S(2)}, u32[]{:S(2)}) async-start(f32[32,4,128]{2,1,0:T(4,128)} %get-tuple-element.14), calls=%async_computation.4 | async-start | bytes 131072 | tf_op jit(solution)/shard_map/all_to_all | solution.py:718

commit v4 on v3

--- a/solution.py
+++ b/solution.py
@@ -27,7 +27,6 @@
 VMEM = pl.BlockSpec(memory_space=pltpu.VMEM)
 SMEM = pl.BlockSpec(memory_space=pltpu.SMEM)
 HBM = pl.BlockSpec(memory_space=pltpu.HBM)
-ANY = pl.BlockSpec(memory_space=pl.ANY)
 NN = (((1,), (0,)), ((), ()))
 NT = (((1,), (1,)), ((), ()))
 TN = (((0,), (0,)), ((), ()))
@@ -52,31 +51,33 @@
     return np.cos(angle), np.sin(angle)
 
 
+def north_starts(rows):
+    return [0, rows // 2] + list(range(1, rows // 2))
+
+
 def north_turns(rows):
     north = rows * LANES
-    starts = np.array([group_start(g, rows) for g in range(rows)])
-    cos, sin = unit_turn(starts[:, None] * np.arange(north)[None, :], north)
-    turns = np.stack([cos, -sin]).reshape(2, rows, rows, LANES)
+    starts = np.array(north_starts(rows))
+    cos, sin = unit_turn(starts[:, None] * np.arange(north // 2)[None, :], north)
+    turns = np.stack([cos, -sin]).reshape(2, len(starts), rows // 2, LANES)
     return turns.astype(np.float32)
 
 
-def north_forward_table():
-    cos, sin = unit_turn(np.outer(np.arange(HALF), np.arange(LANES)), LANES)
-    plain = np.concatenate(
-        [np.concatenate([cos, sin], 1), np.concatenate([-sin, cos], 1)], 0
-    )
-    packed = plain.copy()
-    packed[HALF, :LANES] = 1.0 - 2.0 * (np.arange(LANES) % 2)
-    return np.stack([split_table(packed), split_table(plain)])
-
-
-def north_inverse_table():
-    cos, sin = unit_turn(np.outer(np.arange(HALF), np.arange(LANES)), LANES)
+def north_forward_tables():
+    cos, sin = unit_turn(np.outer(np.arange(LANES), np.arange(LANES)), LANES)
+    plain = np.block([[cos, sin], [-sin, cos]])
+    packed = np.concatenate([cos[:HALF], -sin[:HALF]], 0)
+    packed[HALF] = 1.0 - 2.0 * (np.arange(LANES) % 2)
+    return split_table(packed), split_table(plain)
+
+
+def north_inverse_tables():
+    cos, sin = unit_turn(np.outer(np.arange(LANES), np.arange(LANES)), LANES)
     plain = 2.0 * np.concatenate([cos, sin], 1)
-    packed = plain.copy()
+    packed = plain[:HALF].copy()
     packed[0, :LANES] = 1.0
     packed[0, LANES:] = 2.0 * (np.arange(LANES) % 2) - 1.0
-    return np.stack([split_table(packed), split_table(plain)])
+    return split_table(packed), split_table(plain)
 
 
 def east_tables(east):
@@ -189,7 +190,7 @@
     parts = width // LANES
     squares = jnp.zeros((SUB, LANES), F32)
     for group, end in ((0, 4), (4, 8), (8, FOOTPRINT)):
-        for k in range(group, end):
+        for k in range(group, end if copies else group):
             copies[k].wait()
         spread = [
             [jnp.broadcast_to(blocks[k][p : p + 1], (SUB, LANES)) for p in range(parts)]
@@ -253,15 +254,13 @@
 
 def start_kernel(
     sizes, codes, counts, damping, readings, depth, inclinations, declinations, turns, hats, resid,
-    source, out, side, meta, codes_in, counts_in, damping_in, depth_in, angles, read, map_rows, tiles, values, sems, more,
+    source, out, side, meta, codes_in, depth_in, angles, read, map_rows, tiles, values, sems, more,
 ):
     rows, cols, own, bands = sizes
     row, col = lax.axis_index("row"), lax.axis_index("col")
     _, turns_at, hats_at, end = side_rows(own, bands, rows)
     pairs = [
         (codes.at[0], codes_in),
-        (counts, counts_in),
-        (damping, damping_in),
         (depth, depth_in),
         (inclinations, angles.at[0]),
         (declinations, angles.at[1]),
@@ -274,17 +273,21 @@
     for copy in first:
         copy.start()
     copies = tile_copies(source, tiles, sems)
-    out[...] = jnp.zeros(out.shape, F32)
     for copy in first:
         copy.wait()
-    if len(out.shape) == 4:
-        place_rows(out, lambda d, g: map_rows[(4 * d + g) * 4 : (4 * d + g + 1) * 4])
-    ints = [codes_in[0, k] for k in range(FOOTPRINT)] + [counts_in[0, 0], row, col]
-    meta[0:1, :] = jnp.full((1, LANES), counts_in[0, 0].astype(F32), F32)
-    meta[1:2, :] = jnp.full((1, LANES), damping_in[0], F32)
+    width = map_rows.shape[0] // rows
+    for i in range(rows):
+        for g in range(width // 4):
+            at = i * width + 4 * g
+            out[i, FOOTPRINT + g] = map_rows[at : at + 4]
+    ints = [codes_in[0, k] for k in range(FOOTPRINT)] + [None, row, col]
+    meta[0:1, :] = jnp.broadcast_to(counts[...].astype(F32), (1, LANES))
+    for k in range(FOOTPRINT):
+        meta[2 + k : 3 + k, :] = jnp.full((1, LANES), codes_in[0, k].astype(F32), F32)
+    meta[1:2, :] = jnp.broadcast_to(damping[...], (1, LANES))
     slots = read.shape[1]
     slot = lax.broadcasted_iota(jnp.int32, (1, slots), 1)
-    live = jnp.where(slot < ints[COUNT], read[...], 0.0)
+    live = jnp.where(slot < counts[...], read[...], 0.0)
     for t in range(slots // LANES):
         square = jnp.broadcast_to(live[:, t * LANES : (t + 1) * LANES], (LANES, LANES))
         values[t * LANES : (t + 1) * LANES, :] = square.T
@@ -297,7 +300,8 @@
     put_weights(sizes, row, col, [depth_in[l] for l in range(LAYERS)], trig, side)
     for k in range(FOOTPRINT):
         copies[k].wait()
-        send_adjoint(tiles.at[k], values, k, ints, out, rows, cols)
+        block = apply_adjoint(tiles.at[k], values)
+        out[:, ints[k]] = jnp.broadcast_to(block[None], (rows,) + block.shape)
 
 
 def place_rows(out, get):
@@ -306,25 +310,48 @@
             out[d, 1 + g] = get(d, g)
 
 
-def gather_kernel(arrived, everywhere):
+def column_kernel(rows, cols, arrived, out):
+    row, col = lax.axis_index("row"), lax.axis_index("col")
+    for code in range(FOOTPRINT):
+        target, step = row + code // 3 - 1, code % 3 - 1
+        block = None
+        for a in range(3):
+            source = target - (a - 1)
+            here = (source >= 0) & (source < rows)
+            part = arrived[jnp.clip(source, 0, rows - 1), 3 * a + step + 1]
+            part = jnp.where(here, part, 0.0)
+            block = part if block is None else block + part
+        inside = (target >= 0) & (target < rows) & (col + step >= 0) & (col + step < cols)
+        block = jnp.where(inside, block, 0.0)
+        out[:, code] = jnp.broadcast_to(block[None], (cols,) + block.shape)
+
+
+def share_kernel(arrived, own, everywhere):
     block = jnp.sum(arrived[:, 0] if len(arrived.shape) == 4 else arrived[...], axis=0)
-    everywhere[...] = jnp.broadcast_to(block[None], everywhere.shape)
+    both = jnp.stack([own[...], block])
+    everywhere[...] = jnp.broadcast_to(both[None], everywhere.shape)
 
 
 def normal_kernel(
-    rows, cols, codes, meta, source, vector, arrived, turns, table, out, *refs
+    rows, cols, meta, source, summed, arrived, turns, packed, plain, out, own, *refs
 ):
-    (*apart, codes_in, tiles, sems, values, work, planes, codes_sem) = refs
-    fetch = pltpu.make_async_copy(codes.at[0], codes_in, codes_sem.at[0])
-    fetch.start()
-    copies = tile_copies(source, tiles, sems)
+    (*apart, near, values, work, planes) = refs
+    tiles, copies = source.at[0, 0], None
     row, col = lax.axis_index("row"), lax.axis_index("col")
-    fetch.wait()
-    ints = [codes_in[0, k] for k in range(FOOTPRINT)] + [None, row, col]
-    blocks = near_blocks(ints, vector, rows, cols)
+    ints = [meta[2 + k, 0].astype(jnp.int32) for k in range(FOOTPRINT)] + [None, row, col]
+    for code in range(FOOTPRINT):
+        block = None
+        for j in range(cols):
+            step = col + code % 3 - 1 - j
+            part = summed[j, 3 * (code // 3) + jnp.clip(step, -1, 1) + 1]
+            part = jnp.where((step >= -1) & (step <= 1), part, 0.0)
+            block = part if block is None else block + part
+        near[code] = block
+    blocks = [near[ints[k]] for k in range(FOOTPRINT)]
     me = row * cols + col
     out[...] = jnp.zeros(out.shape, F32)
-    ridge = meta[1:2, :] * vector[me]
+    own[...] = near[FOOTPRINT // 2]
+    ridge = meta[1:2, :] * own[...]
     if apart:
         out[me] = ridge
     else:
@@ -337,36 +364,44 @@
             for g in range(out.shape[1] - 1):
                 out[device, 1 + g] = piece[4 * g : 4 * g + 4]
 
-    north_transform(rows, cols, arrived, turns, table, planes, store)
+    north_transform(rows, cols, arrived, turns, (packed, plain), planes, store)
     apply_forward(tiles, copies, blocks, meta[0:1, :], values, work)
     for k in range(FOOTPRINT):
         send_adjoint(tiles.at[k], values, k, ints, out, rows, cols)
 
 
-def north_transform(rows, cols, arrived, turns, table, planes, store):
-    width = planes.shape[1]
-    each = width // cols
+def north_transform(rows, cols, arrived, turns, tables, planes, store):
     own = HALF // cols
+    near, count = rows // 2, planes.shape[1]
     for i in range(rows):
-        for j in range(cols):
-            if len(arrived.shape) == 4:
-                for g in range(each // 4):
-                    at = j * each + 4 * g
-                    planes[i, at : at + 4, :] = arrived[i * cols + j, 1 + g]
-            else:
-                planes[i, j * each : (j + 1) * each, :] = arrived[i * cols + j]
-    for group in range(rows):
-        re = planes[0] * turns[0, group, 0:1]
-        im = planes[0] * turns[1, group, 0:1]
-        for i in range(1, rows):
-            re = re + planes[i] * turns[0, group, i : i + 1]
-            im = im + planes[i] * turns[1, group, i : i + 1]
-        kind = min(group, 1)
-        both = jnp.concatenate([re, im], axis=1)
-        result = table_mul(table[kind, 0], table[kind, 1], both, NT)
-        for j in range(cols):
-            real, imag = result[j * own : (j + 1) * own], result[HALF + j * own : HALF + (j + 1) * own]
-            store(group * cols + j, jnp.concatenate([real, imag], axis=1))
+        for g in range(count // 4):
+            planes[i, 4 * g : 4 * g + 4, :] = arrived[i, FOOTPRINT + g]
+    for i in range(near):
+        one, other = planes[i], planes[i + near]
+        planes[i] = one + other
+        planes[i + near] = one - other
+    packed, plain = tables
+    for n, start in enumerate(north_starts(rows)):
+        base = near * (start % 2)
+        re, im = None, None
+        for i in range(near):
+            plane = planes[base + i]
+            a = plane if start == 0 else plane * turns[0, n, i : i + 1]
+            re = a if re is None else re + a
+            if start:
+                a = plane * turns[1, n, i : i + 1]
+                im = a if im is None else im + a
+        if start == 0:
+            result = table_mul(packed[0], packed[1], re, NT)
+        else:
+            result = table_mul(plain[0], plain[1], jnp.concatenate([re, im], axis=1), NT)
+        imag_at = result.shape[0] // 2
+        groups = [n] if n < 2 else [2 * start, 2 * start + 1]
+        for h, group in enumerate(groups):
+            for j in range(cols):
+                at = h * HALF + j * own
+                real, imag = result[at : at + own], result[imag_at + at : imag_at + at + own]
+                store(group * cols + j, jnp.concatenate([real, imag], axis=1))
 
 
 def pole(north, east, trig):
@@ -579,38 +614,26 @@
         weigh(spectrum, 1 + layer, sizes, side, mixed, first and layer == 0)
 
 
-def swap_groups(values, size):
-    group = lax.broadcasted_iota(jnp.int32, values[0].shape, 1) // size
-    bit = len(values) // 2
-    while bit:
-        low = (group & bit) == 0
-        for s in range(len(values)):
-            if not s & bit:
-                x, y = values[s], values[s | bit]
-                values[s] = jnp.where(low, x, pltpu.roll(y, bit * size, 1))
-                values[s | bit] = jnp.where(low, pltpu.roll(x, LANES - bit * size, 1), y)
-        bit //= 2
-    return values
-
-
 def sort_east(arrived, sizes, spec):
     rows, cols, own, bands = sizes
-    count = 2 * cols
-    for a in range(rows * cols // count):
-        for g in range(own // SUB):
-            values = []
-            for s in range(count):
-                at = 1 + 2 * g
-                both = [arrived[a * count + s, at], arrived[a * count + s, at + 1]]
-                values.append(jnp.concatenate(both, axis=0))
-            values = swap_groups(values, LANES // count)
-            for t in range(count):
-                at = (t // cols) * own + g * SUB
-                spec[t % cols, at : at + SUB, a * LANES : (a + 1) * LANES] = values[t]
+    left = lax.broadcasted_iota(jnp.int32, (SUB, LANES), 1) < HALF
+    for j in range(cols):
+        for i in range(0, rows, 2):
+            for g in range(own // SUB):
+                pair = []
+                for source in (i * cols + j, (i + 1) * cols + j):
+                    at = 1 + 2 * g
+                    both = [arrived[source, at], arrived[source, at + 1]]
+                    pair.append(jnp.concatenate(both, axis=0))
+                cut = slice(i * HALF, (i + 2) * HALF)
+                at = g * SUB
+                spec[j, at : at + SUB, cut] = jnp.where(left, pair[0], pltpu.roll(pair[1], HALF, 1))
+                at = own + g * SUB
+                spec[j, at : at + SUB, cut] = jnp.where(left, pltpu.roll(pair[0], HALF, 1), pair[1])
 
 
 def map_kernel(
-    sizes, width, arrived, first, second, carry, tables, side, known, response,
+    sizes, width, arrived, shared, second, carry, tables, side, known, response,
     coarse, fine, work, mixed, back, *spec,
 ):
     rows, cols, own, bands = sizes
@@ -626,20 +649,19 @@
 
     spectrum = east_forward(get, sizes, side, tables, work)
     weigh(spectrum, 0, sizes, side, mixed, True)
-    model_mix(first, carry[4, 0:1, 0:1], sizes, side, tables, coarse, fine, work, mixed, False)
+    model_mix(shared.at[:, 0], carry[4, 0:1, 0:1], sizes, side, tables, coarse, fine, work, mixed, False)
     east_inverse(mixed, sizes, side, tables, back, store_pieces(known, width))
     model_mix(second, None, sizes, side, tables, coarse, fine, work, mixed, True)
     east_inverse(mixed, sizes, side, tables, back, store_pieces(response, width))
 
 
 def direction_kernel(
-    rows, cols, codes, meta, source, first, applied, second, measured, carry,
-    codes_in, tiles, sems, work, codes_sem,
+    rows, cols, meta, source, shared, second, measured, carry,
+    work,
 ):
-    fetch = pltpu.make_async_copy(codes.at[0], codes_in, codes_sem.at[0])
-    fetch.start()
-    copies = tile_copies(source, tiles, sems)
+    tiles, copies = source.at[0, 0], None
     row, col = lax.axis_index("row"), lax.axis_index("col")
+    first, applied = shared.at[:, 0], shared.at[:, 1]
     norm = total(first[...] * first[...])
     step = norm / total(first[...] * applied[...])
     residual = first[...] - step[None] * applied[...]
@@ -651,8 +673,7 @@
     carry[1] = second[me]
     for at, value in ((2, norm_next), (3, ridge), (4, step)):
         carry[at] = jnp.broadcast_to(value, carry.shape[1:])
-    fetch.wait()
-    ints = [codes_in[0, k] for k in range(FOOTPRINT)] + [None, row, col]
+    ints = [meta[2 + k, 0].astype(jnp.int32) for k in range(FOOTPRINT)] + [None, row, col]
     blocks = near_blocks(ints, second, rows, cols)
     squares = apply_forward(tiles, copies, blocks, meta[0:1, :], None, work)
     measured[...] = jnp.broadcast_to(squares[None], measured.shape)
@@ -668,31 +689,46 @@
 
 
 def finish_kernel(
-    rows, cols, arrived, measured, carry, turns, table, coefficients, out, mixed, waves
+    rows, cols, arrived, measured, carry, turns, packed, plain, coefficients, out, mixed, waves
 ):
     solved = carry[0] + last_step(measured, carry) * carry[1]
     for p in range(solved.shape[0]):
         coefficients[:, p * LANES : (p + 1) * LANES] = solved[p : p + 1]
     own = arrived.shape[1]
     width = out.shape[0]
+    near = rows // 2
     for i in range(rows):
         for j in range(cols):
-            mixed[i, j * own : (j + 1) * own, :] = arrived[i * cols + j]
-        kind = min(i, 1)
-        both = mul_table(mixed[i], table[kind, 0], table[kind, 1], TN)
+            at = i * HALF + j * own
+            mixed[at : at + own, :] = arrived[i * cols + j]
+    starts = north_starts(rows)
+    for n, start in enumerate(starts):
+        if n == 0:
+            both = mul_table(mixed[0:HALF], packed[0], packed[1], TN)
+        elif n == 1:
+            both = mul_table(mixed[HALF : 2 * HALF], plain[0, :HALF], plain[1, :HALF], TN)
+        else:
+            at = 2 * start * HALF
+            both = mul_table(mixed[at : at + 2 * HALF], plain[0], plain[1], TN)
         top, bottom = both[:width], both[width:]
-        waves[i, :, :LANES] = top[:, :LANES] - bottom[:, LANES:]
-        waves[i, :, LANES:] = top[:, LANES:] + bottom[:, :LANES]
+        waves[n, :, :LANES] = top[:, :LANES] - bottom[:, LANES:]
+        waves[n, :, LANES:] = top[:, LANES:] + bottom[:, :LANES]
     for at in range(0, width, SUB):
-        parts = [None] * rows
-        for i in range(rows):
-            re = waves[i, at : at + SUB, :LANES]
-            im = waves[i, at : at + SUB, LANES:]
-            for n in range(rows):
-                term = re * turns[0, i, n : n + 1] + im * turns[1, i, n : n + 1]
-                parts[n] = term if i == 0 else parts[n] + term
-        for n in range(rows):
-            out[at : at + SUB, n * LANES : (n + 1) * LANES] = parts[n]
+        parts = [[None, None] for _ in range(near)]
+        for n, start in enumerate(starts):
+            re = waves[n, at : at + SUB, :LANES]
+            im = waves[n, at : at + SUB, LANES:]
+            for i in range(near):
+                if start == 0:
+                    term = re
+                else:
+                    term = re * turns[0, n, i : i + 1] + im * turns[1, n, i : i + 1]
+                sums = parts[i]
+                sums[start % 2] = term if sums[start % 2] is None else sums[start % 2] + term
+        for i in range(near):
+            even, odd = parts[i]
+            out[at : at + SUB, i * LANES : (i + 1) * LANES] = even + odd
+            out[at : at + SUB, (near + i) * LANES : (near + i + 1) * LANES] = even - odd
 
 
 def shape(*dims):
@@ -734,6 +770,7 @@
     sizes = (rows, cols, own, bands)
 
     turns = north_turns(rows)
+    forward_tables, inverse_tables = north_forward_tables(), north_inverse_tables()
     tables, east_turns = east_tables(east)
     hats = north_hat_table(rows, cols)
 
@@ -748,73 +785,75 @@
     tile_scratch = scratch(FOOTPRINT, slots, sources)
     tile_sems = pltpu.SemaphoreType.DMA((FOOTPRINT,))
     codes_scratch = pltpu.SMEM((1, FOOTPRINT), jnp.int32)
-    one_sem = pltpu.SemaphoreType.DMA((1,))
-    resid = resid_grid if joined else resid_grid[:SUB]
 
     sums, side, meta = call(
         functools.partial(start_kernel, sizes),
-        (beside, shape(side_rows(own, bands, rows)[-1], LANES), shape(2, LANES)),
-        [apart(footprints), (ANY, counts), (ANY, damping)]
+        (
+            shape(rows, FOOTPRINT + width // 4, parts, LANES),
+            shape(side_rows(own, bands, rows)[-1], LANES),
+            shape(2 + FOOTPRINT, LANES),
+        ),
+        [apart(footprints), (VMEM, counts), (VMEM, damping.reshape(1, 1))]
         + [
             apart(value)
             for value in (
                 readings, layer_depth, inclinations, declinations,
-                jnp.asarray(east_turns), jnp.asarray(hats), resid, kernel_tiles,
+                jnp.asarray(east_turns), jnp.asarray(hats), resid_grid, kernel_tiles,
             )
         ],
         [
             codes_scratch,
-            pltpu.SMEM((1, 1), jnp.int32),
-            pltpu.SMEM((1,), F32),
             pltpu.SMEM((LAYERS,), F32),
             pltpu.SMEM((2, 2), F32),
             scratch(1, slots),
-            scratch(*resid.shape),
+            scratch(*resid_grid.shape),
             tile_scratch,
             scratch(slots, LANES),
             tile_sems,
-            pltpu.SemaphoreType.DMA((10,)),
+            pltpu.SemaphoreType.DMA((8,)),
         ],
     )
+    arrived = lax.all_to_all(sums, "row", 0, 0, tiled=True)
+    summed = call(
+        functools.partial(column_kernel, rows, cols),
+        shape(cols, FOOTPRINT, parts, LANES),
+        [(VMEM, arrived)],
+    )
+    summed = lax.all_to_all(summed, "col", 0, 0, tiled=True)
+
+    sums, right_own, *spectrum = call(
+        functools.partial(normal_kernel, rows, cols),
+        (beside, shape(parts, LANES)) if joined else (everywhere, shape(parts, LANES), pieces),
+        [
+            (VMEM, meta),
+            (VMEM, kernel_tiles),
+            (VMEM, summed),
+            (VMEM, arrived),
+            (VMEM, turns),
+            (VMEM, forward_tables[0]),
+            (VMEM, forward_tables[1]),
+        ],
+        [scratch(FOOTPRINT, parts, LANES)]
+        + [scratch(slots, LANES), scratch(slots, LANES)]
+        + [scratch(rows, width, LANES)],
+    )
     sums = exchange(sums)
-    right_all = call(gather_kernel, everywhere, [(VMEM, sums)])
-    if not joined:
-        right_all, resid_grid = lax.optimization_barrier((right_all, resid_grid))
-    planes = sums if joined else exchange(resid_grid.reshape(devices, -1, LANES))
-    right_side = exchange(right_all)
-
-    sums = call(
-        functools.partial(normal_kernel, rows, cols),
-        beside if joined else (everywhere, pieces),
-        [
-            apart(footprints),
-            (VMEM, meta),
-            apart(kernel_tiles),
-            (VMEM, right_side),
-            (VMEM, planes),
-            (VMEM, turns),
-            (VMEM, north_forward_table()),
-        ],
-        [codes_scratch, tile_scratch, tile_sems, scratch(slots, LANES), scratch(slots, LANES)]
-        + [scratch(rows, width, LANES), one_sem],
-    )
-    if not joined:
-        sums, spectrum = sums
-    sums = exchange(sums)
-    applied_all = call(gather_kernel, everywhere, [(VMEM, sums)])
-    applied = exchange(applied_all)
+    shared = call(
+        share_kernel, shape(devices, 2, parts, LANES), [(VMEM, sums), (VMEM, right_own)]
+    )
+    shared = exchange(shared)
     if joined:
         spectrum, sorted_work = sums, [scratch(cols, 2 * own, tile_east)]
     else:
-        spectrum, sorted_work = exchange(spectrum), []
-        spectrum = spectrum.reshape(devices, own, 2, cols, width // cols).transpose(3, 2, 1, 0, 4)
+        spectrum, sorted_work = exchange(spectrum[0]), []
+        spectrum = spectrum.reshape(rows, cols, own, 2, width).transpose(1, 3, 2, 0, 4)
         spectrum = spectrum.reshape(cols, 2 * own, tile_east)
 
     second, measured, carry = call(
         functools.partial(direction_kernel, rows, cols),
         (everywhere, everywhere, shape(5, parts, LANES)),
-        [apart(footprints), (VMEM, meta), apart(kernel_tiles), (VMEM, right_side), (VMEM, applied)],
-        [codes_scratch, tile_scratch, tile_sems, scratch(slots, LANES), one_sem],
+        [(VMEM, meta), (VMEM, kernel_tiles), (VMEM, shared)],
+        [scratch(slots, LANES)],
     )
     work = [
         scratch(LAYERS, 2 * rows, cols * LANES),
@@ -828,7 +867,7 @@
         (pieces, pieces),
         [
             (VMEM, spectrum),
-            (VMEM, right_side),
+            (VMEM, shared),
             (VMEM, second),
             (VMEM, carry),
             (VMEM, tables),
@@ -850,9 +889,10 @@
             (VMEM, measured),
             (VMEM, carry),
             (VMEM, turns),
-            (VMEM, north_inverse_table()),
+            (VMEM, inverse_tables[0]),
+            (VMEM, inverse_tables[1]),
         ],
-        [scratch(rows, HALF, 2 * width), scratch(rows, width, 2 * LANES)],
+        [scratch(rows * HALF, 2 * width), scratch(rows // 2 + 1, width, 2 * LANES)],
     )
     return coefficients.reshape(1, 1, sources), rtp_map
 

time: 87.9 us -> 81.3 us (0.925)
  blocking collectives: 64 us -> 60 us
  Pallas kernels: 15.2 us -> 11.9 us
    all_to_all x5 -> x3, blocking collectives: 64 us -> 36.1 us  [exchange(): return lax.all_to_all(pieces, BOTH, 0, 0, tiled=True)]
    all_to_all x0 -> x2, blocking collectives: none -> 23.9 us  [the longest x1 13.4 us: on_device(): arrived = lax.all_to_all(sums, 'row', 0, 0, tiled=True)]
    pallas_call x8, Pallas kernels: 15.2 us -> 11.9 us  [call(): pl.pallas_call(kernel, out_shape=outs, in_specs=[spec for spec, _ in ins]...]
where the time goes in v4:
time: 81.3 us; the launch traced here: 81 us
  blocking collectives  60 us (74%)
  Pallas kernels  11.9 us (15%)
  waiting for transfers between devices  3.94 us (5%)
  between operations  2.6 us (3%)
  starting transfers between devices  2.57 us (3%)
    all_to_all x3, blocking collectives, exchange(): return lax.all_to_all(pieces, BOTH, 0, 0, tiled=True)  36.1 us
    all_to_all x1, blocking collectives, on_device(): arrived = lax.all_to_all(sums, 'row', 0, 0, tiled=True)  13.4 us
    pallas_call x8, Pallas kernels, call(): pl.pallas_call(kernel, out_shape=outs, in_specs=[spec for spec, _ in ins]...  11.9 us
    all_to_all x1, blocking collectives, on_device(): summed = lax.all_to_all(summed, 'col', 0, 0, tiled=True)  10.4 us
    all_to_all x1, waiting for transfers between devices, exchange(): return lax.all_to_all(pieces, BOTH, 0, 0, tiled=True)  3.94 us
    all_to_all x1, starting transfers between devices, exchange(): return lax.all_to_all(pieces, BOTH, 0, 0, tiled=True)  2.57 us
  transfers between devices with their start and end apart: 1, of which 1 were waited for; matrix products, arithmetic and copies ran while one was open for 0% of the time, Pallas kernels for 4%

profile of v4, /device:TPU:0, one launch (start us, length us, event | category | flops | bytes accessed | tf_op | source)
XLA Modules:
  0.0 81.0 jit_solution(16737002106875676468)
XLA Ops:
  0.6 0.0 copy-start.4
  0.6 0.0 copy-start.5
  0.7 0.0 copy-start.2
  0.7 0.0 copy-start
  2.5 3.2 %shard_map.176 = (f32[8,25,4,128]{3,2,1,0:T(4,128)S(1)}, f32[1680,128]{1,0:T(8,128)S(1)}, f32[11,128]{1,0:T(8,128)S(1)}) custom-call(s32[1,1,9]{2,1,0:T(1,128)} %codes.1, s32[1,1]{1,0:T(1,128)S(6)} %copy.19.counts, f32[1,1]{1,0:T(1,128)} %bitcast.2.damping, f32[1,1,256]{2,1,0:T(1,128)} %readings.1, f32[2]{0:T(128)} %depth.1, f32[2]{0:T(128)} %inclinations.1, ...), custom_call_target="tpu_custom_call" | custom-call | tf_op jit(solution)/shard_map/pallas_call | solution.py:743
  5.8 13.4 %all_to_all.30.arrived = f32[8,25,4,128]{3,2,1,0:T(4,128)S(1)} all-to-all(f32[8,25,4,128]{3,2,1,0:T(4,128)S(1)} %get-tuple-element.15), channel_id=1, replica_groups=mesh['row'=8,'col'=4] {'row'}, dimensions={0} | all-to-all | bytes 819200 | tf_op jit(solution)/shard_map/all_to_all | solution.py:816
  19.2 10.4 %all_to_all.31.summed = f32[4,9,4,128]{3,2,1,0:T(4,128)S(1)} all-to-all(f32[4,9,4,128]{3,2,1,0:T(4,128)S(1)} %shard_map.177), channel_id=1, replica_groups=mesh['row'=8,'col'=4] {'col'}, dimensions={0} | all-to-all | bytes 147456 | tf_op jit(solution)/shard_map/all_to_all | solution.py:822
  29.7 0.0 copy-done.4
  29.7 0.0 copy-done.5
  29.7 0.0 copy-done.2
  29.7 0.0 copy-done
  29.7 0.0 copy-start.1
  29.7 1.9 %shard_map.178 = (f32[32,5,4,128]{3,2,1,0:T(4,128)S(1)}, f32[4,128]{1,0:T(4,128)S(1)}) custom-call(f32[11,128]{1,0:T(8,128)S(1)} %get-tuple-element.14.meta, f32[1,1,9,256,512]{4,3,2,1,0:T(8,128)S(1)} %copy-done, f32[4,9,4,128]{3,2,1,0:T(4,128)S(1)} %all_to_all.31.summed, f32[8,25,4,128]{3,2,1,0:T(4,128)S(1)} %all_to_all.30.arrived, ...), custom_call_target="tpu_custom_call" | custom-call | tf_op jit(solution)/shard_map/pallas_call | solution.py:743
  31.6 12.7 %all_to_all.32.arrived = f32[32,5,4,128]{3,2,1,0:T(4,128)S(1)} all-to-all(f32[32,5,4,128]{3,2,1,0:T(4,128)S(1)} %get-tuple-element.16), channel_id=1, replica_groups=mesh['row'=8,'col'=4] {'row','col'}, dimensions={0} | all-to-all | bytes 655360 | tf_op jit(solution)/shard_map/all_to_all | solution.py:754
  44.3 0.0 copy-start.3
  44.3 0.0 copy-start.6
  44.3 11.5 %all_to_all.33.shared = f32[32,2,4,128]{3,2,1,0:T(4,128)S(1)} all-to-all(f32[32,2,4,128]{3,2,1,0:T(4,128)S(1)} %shard_map.179), channel_id=1, replica_groups=mesh['row'=8,'col'=4] {'row','col'}, dimensions={0} | all-to-all | bytes 262144 | tf_op jit(solution)/shard_map/all_to_all | solution.py:754
  55.8 1.9 %shard_map.180 = (f32[32,4,128]{2,1,0:T(4,128)S(1)}, f32[32,4,128]{2,1,0:T(4,128)}, f32[5,4,128]{2,1,0:T(4,128)S(1)}) custom-call(f32[11,128]{1,0:T(8,128)S(1)} %get-tuple-element.14.meta, f32[1,1,9,256,512]{4,3,2,1,0:T(8,128)S(1)} %copy-done, f32[32,2,4,128]{3,2,1,0:T(4,128)S(1)} %all_to_all.33.shared), custom_call_target="tpu_custom_call" | custom-call | tf_op jit(solution)/shard_map/pallas_call | solution.py:743
  57.7 2.6 %all-to-all-start.4 = ((f32[32,4,128]{2,1,0:T(4,128)}), f32[32,4,128]{2,1,0:T(4,128)S(1)}, u32[]{:S(2)}, u32[]{:S(2)}) async-start(f32[32,4,128]{2,1,0:T(4,128)} %get-tuple-element.18), calls=%async_computation.4 | async-start | bytes 131072 | tf_op jit(solution)/shard_map/all_to_all | solution.py:754
  60.3 0.0 copy-done.1
  60.3 3.5 %shard_map.181 = (f32[32,16,128]{2,1,0:T(8,128)S(1)}, f32[32,16,128]{2,1,0:T(8,128)S(1)}) custom-call(f32[32,5,4,128]{3,2,1,0:T(4,128)S(1)} %all_to_all.32.arrived, f32[32,2,4,128]{3,2,1,0:T(4,128)S(1)} %all_to_all.33.shared, f32[32,4,128]{2,1,0:T(4,128)S(1)} %get-tuple-element.20.second, f32[5,4,128]{2,1,0:T(4,128)S(1)} %get-tuple-element.19.carry, ...), custom_call_target="tpu_custom_call" | custom-call | tf_op jit(solution)/shard_map/pallas_call | solution.py:743
  63.8 3.9 %all-to-all-done.4.measured = f32[32,4,128]{2,1,0:T(4,128)S(1)} async-done(((f32[32,4,128]{2,1,0:T(4,128)}), f32[32,4,128]{2,1,0:T(4,128)S(1)}, u32[]{:S(2)}, u32[]{:S(2)}) %all-to-all-start.4) | async-done | bytes 65568 | tf_op jit(solution)/shard_map/all_to_all | solution.py:754
  67.8 0.1 shard_map.182
  67.9 11.9 %all_to_all.34.arrived = f32[32,16,128]{2,1,0:T(8,128)S(1)} all-to-all(f32[32,16,128]{2,1,0:T(8,128)S(1)} %shard_map.182), channel_id=1, replica_groups=mesh['row'=8,'col'=4] {'row','col'}, dimensions={0} | all-to-all | bytes 524288 | tf_op jit(solution)/shard_map/all_to_all | solution.py:754
  79.8 0.0 copy-done.3
  79.8 0.0 copy-done.6
  79.8 1.2 %shard_map.183 = (f32[1,512]{1,0:T(1,128)}, f32[64,1024]{1,0:T(8,128)}) custom-call(f32[32,16,128]{2,1,0:T(8,128)S(1)} %all_to_all.34.arrived, f32[32,4,128]{2,1,0:T(4,128)S(1)} %all-to-all-done.4.measured, f32[5,4,128]{2,1,0:T(4,128)S(1)} %get-tuple-element.19.carry, f32[2,5,4,128]{3,2,1,0:T(4,128)S(1)} %copy-done.4, bf16[2,64,256]{2,1,0:T(8,128)(2,1)S(1)} %copy-done.6, ...), custom_call_target="tpu_custom_call" | custom-call | tf_op jit(solution)/shard_map/pallas_call | solution.py:743
  (2 shorter events, 0.1 us)
Async XLA Ops:
  0.6 29.0 %copy-start.4 = (f32[2,5,4,128]{3,2,1,0:T(4,128)S(1)}, f32[2,5,4,128]{3,2,1,0:T(4,128)}, u32[]{:S(2)}) copy-start(f32[2,5,4,128]{3,2,1,0:T(4,128)} %constant.18.clone.turns) | copy-start | bytes 61444
  0.6 29.0 %copy-start.5 = (bf16[2,128,128]{2,1,0:T(8,128)(2,1)S(1)}, bf16[2,128,128]{2,1,0:T(8,128)(2,1)}, u32[]{:S(2)}) copy-start(bf16[2,128,128]{2,1,0:T(8,128)(2,1)} %constant.19.clone.packed) | copy-start | bytes 196612
  0.7 29.0 %copy-start.2 = (bf16[2,256,256]{2,1,0:T(8,128)(2,1)S(1)}, bf16[2,256,256]{2,1,0:T(8,128)(2,1)}, u32[]{:S(2)}) copy-start(bf16[2,256,256]{2,1,0:T(8,128)(2,1)} %constant.20.clone.plain) | copy-start | bytes 786436
  0.7 29.0 %copy-start = (f32[1,1,9,256,512]{4,3,2,1,0:T(8,128)S(1)}, f32[1,1,9,256,512]{4,3,2,1,0:T(8,128)}, u32[]{:S(2)}) copy-start(f32[1,1,9,256,512]{4,3,2,1,0:T(8,128)} %source.5) | copy-start | bytes 14155780
  29.7 30.6 %copy-start.1 = (bf16[2048,256]{1,0:T(8,128)(2,1)S(1)}, bf16[2048,256]{1,0:T(8,128)(2,1)}, u32[]{:S(2)}) copy-start(bf16[2048,256]{1,0:T(8,128)(2,1)} %constant.21.clone.tables) | copy-start | bytes 3145732
  44.3 35.5 %copy-start.3 = (bf16[2,128,256]{2,1,0:T(8,128)(2,1)S(1)}, bf16[2,128,256]{2,1,0:T(8,128)(2,1)}, u32[]{:S(2)}) copy-start(bf16[2,128,256]{2,1,0:T(8,128)(2,1)} %constant.23.clone.plain) | copy-start | bytes 393220
  44.3 35.5 %copy-start.6 = (bf16[2,64,256]{2,1,0:T(8,128)(2,1)S(1)}, bf16[2,64,256]{2,1,0:T(8,128)(2,1)}, u32[]{:S(2)}) copy-start(bf16[2,64,256]{2,1,0:T(8,128)(2,1)} %constant.22.clone.packed) | copy-start | bytes 196612
  57.7 10.1 %all-to-all-start.4 = ((f32[32,4,128]{2,1,0:T(4,128)}), f32[32,4,128]{2,1,0:T(4,128)S(1)}, u32[]{:S(2)}, u32[]{:S(2)}) async-start(f32[32,4,128]{2,1,0:T(4,128)} %get-tuple-element.18), calls=%async_computation.4 | async-start | bytes 131072 | tf_op jit(solution)/shard_map/all_to_all | solution.py:754

commit v5 on v4

--- a/solution.py
+++ b/solution.py
@@ -19,6 +19,7 @@
 HALF = 64
 BOTH = ("row", "col")
 COUNT, ROW, COL = 9, 10, 11
+SENT = 6
 MIB = 1024 * 1024
 SMALL, LARGE = 24 * MIB, 62 * MIB
 F32 = jnp.float32
@@ -254,7 +255,7 @@
 
 def start_kernel(
     sizes, codes, counts, damping, readings, depth, inclinations, declinations, turns, hats, resid,
-    source, out, side, meta, codes_in, depth_in, angles, read, map_rows, tiles, values, sems, more,
+    source, out, kept, side, meta, codes_in, depth_in, angles, read, map_rows, tiles, values, sems, more,
 ):
     rows, cols, own, bands = sizes
     row, col = lax.axis_index("row"), lax.axis_index("col")
@@ -279,7 +280,7 @@
     for i in range(rows):
         for g in range(width // 4):
             at = i * width + 4 * g
-            out[i, FOOTPRINT + g] = map_rows[at : at + 4]
+            out[i, SENT + g] = map_rows[at : at + 4]
     ints = [codes_in[0, k] for k in range(FOOTPRINT)] + [None, row, col]
     meta[0:1, :] = jnp.broadcast_to(counts[...].astype(F32), (1, LANES))
     for k in range(FOOTPRINT):
@@ -300,8 +301,25 @@
     put_weights(sizes, row, col, [depth_in[l] for l in range(LAYERS)], trig, side)
     for k in range(FOOTPRINT):
         copies[k].wait()
-        block = apply_adjoint(tiles.at[k], values)
-        out[:, ints[k]] = jnp.broadcast_to(block[None], (rows,) + block.shape)
+        kept[ints[k]] = apply_adjoint(tiles.at[k], values)
+    fill_pieces(out, kept, row)
+
+
+def fill_pieces(out, kept, here):
+    for peer in range(out.shape[0]):
+        low = jnp.maximum(peer - here - 1, -1)
+        for slot in range(2):
+            at = 3 * (jnp.clip(low + slot, -1, 1) + 1)
+            out[peer, 3 * slot : 3 * slot + 3] = kept[pl.ds(at, 3)]
+
+
+def arrived_part(arrived, kept, here, offset, which, other):
+    if offset == 0:
+        return kept[3 * (which + 1) + other]
+    peer, count = here - offset, arrived.shape[0]
+    slot = which - max(offset - 1, -1)
+    part = arrived[jnp.clip(peer, 0, count - 1), 3 * slot + other]
+    return jnp.where((peer >= 0) & (peer < count), part, 0.0)
 
 
 def place_rows(out, get):
@@ -310,20 +328,17 @@
             out[d, 1 + g] = get(d, g)
 
 
-def column_kernel(rows, cols, arrived, out):
+def column_kernel(rows, cols, arrived, kept, out, sums):
     row, col = lax.axis_index("row"), lax.axis_index("col")
-    for code in range(FOOTPRINT):
-        target, step = row + code // 3 - 1, code % 3 - 1
-        block = None
-        for a in range(3):
-            source = target - (a - 1)
-            here = (source >= 0) & (source < rows)
-            part = arrived[jnp.clip(source, 0, rows - 1), 3 * a + step + 1]
-            part = jnp.where(here, part, 0.0)
-            block = part if block is None else block + part
-        inside = (target >= 0) & (target < rows) & (col + step >= 0) & (col + step < cols)
-        block = jnp.where(inside, block, 0.0)
-        out[:, code] = jnp.broadcast_to(block[None], (cols,) + block.shape)
+    for north in (-1, 0, 1):
+        for east in (-1, 0, 1):
+            parts = [
+                arrived_part(arrived, kept, row, a - north, a, east + 1) for a in (-1, 0, 1)
+            ]
+            target, column = row + north, col + east
+            inside = (target >= 0) & (target < rows) & (column >= 0) & (column < cols)
+            sums[3 * (east + 1) + north + 1] = jnp.where(inside, parts[0] + parts[1] + parts[2], 0.0)
+    fill_pieces(out, sums, col)
 
 
 def share_kernel(arrived, own, everywhere):
@@ -333,20 +348,16 @@
 
 
 def normal_kernel(
-    rows, cols, meta, source, summed, arrived, turns, packed, plain, out, own, *refs
+    rows, cols, meta, source, summed, sums, arrived, turns, packed, plain, out, own, *refs
 ):
     (*apart, near, values, work, planes) = refs
     tiles, copies = source.at[0, 0], None
     row, col = lax.axis_index("row"), lax.axis_index("col")
     ints = [meta[2 + k, 0].astype(jnp.int32) for k in range(FOOTPRINT)] + [None, row, col]
     for code in range(FOOTPRINT):
-        block = None
-        for j in range(cols):
-            step = col + code % 3 - 1 - j
-            part = summed[j, 3 * (code // 3) + jnp.clip(step, -1, 1) + 1]
-            part = jnp.where((step >= -1) & (step <= 1), part, 0.0)
-            block = part if block is None else block + part
-        near[code] = block
+        north, east = code // 3 - 1, code % 3 - 1
+        parts = [arrived_part(summed, sums, col, b - east, b, north + 1) for b in (-1, 0, 1)]
+        near[code] = parts[0] + parts[1] + parts[2]
     blocks = [near[ints[k]] for k in range(FOOTPRINT)]
     me = row * cols + col
     out[...] = jnp.zeros(out.shape, F32)
@@ -375,7 +386,7 @@
     near, count = rows // 2, planes.shape[1]
     for i in range(rows):
         for g in range(count // 4):
-            planes[i, 4 * g : 4 * g + 4, :] = arrived[i, FOOTPRINT + g]
+            planes[i, 4 * g : 4 * g + 4, :] = arrived[i, SENT + g]
     for i in range(near):
         one, other = planes[i], planes[i + near]
         planes[i] = one + other
@@ -786,10 +797,12 @@
     tile_sems = pltpu.SemaphoreType.DMA((FOOTPRINT,))
     codes_scratch = pltpu.SMEM((1, FOOTPRINT), jnp.int32)
 
-    sums, side, meta = call(
+    nine = shape(FOOTPRINT, parts, LANES)
+    sums, kept, side, meta = call(
         functools.partial(start_kernel, sizes),
         (
-            shape(rows, FOOTPRINT + width // 4, parts, LANES),
+            shape(rows, SENT + width // 4, parts, LANES),
+            nine,
             shape(side_rows(own, bands, rows)[-1], LANES),
             shape(2 + FOOTPRINT, LANES),
         ),
@@ -814,10 +827,10 @@
         ],
     )
     arrived = lax.all_to_all(sums, "row", 0, 0, tiled=True)
-    summed = call(
+    summed, column_sums = call(
         functools.partial(column_kernel, rows, cols),
-        shape(cols, FOOTPRINT, parts, LANES),
-        [(VMEM, arrived)],
+        (shape(cols, SENT, parts, LANES), nine),
+        [(VMEM, arrived), (VMEM, kept)],
     )
     summed = lax.all_to_all(summed, "col", 0, 0, tiled=True)
 
@@ -828,6 +841,7 @@
             (VMEM, meta),
             (VMEM, kernel_tiles),
             (VMEM, summed),
+            (VMEM, column_sums),
             (VMEM, arrived),
             (VMEM, turns),
             (VMEM, forward_tables[0]),

time: 81.3 us -> 80.7 us (level)
  no operation moved by 1% of the time
where the time goes in v5:
time: 80.7 us; the launch traced here: 80.4 us
  blocking collectives  59.4 us (74%)
  Pallas kernels  11.9 us (15%)
  waiting for transfers between devices  3.93 us (5%)
  between operations  2.6 us (3%)
  starting transfers between devices  2.57 us (3%)
    all_to_all x3, blocking collectives, exchange(): return lax.all_to_all(pieces, BOTH, 0, 0, tiled=True)  36.1 us
    all_to_all x1, blocking collectives, on_device(): arrived = lax.all_to_all(sums, 'row', 0, 0, tiled=True)  12.9 us
    pallas_call x8, Pallas kernels, call(): pl.pallas_call(kernel, out_shape=outs, in_specs=[spec for spec, _ in ins]...  11.9 us
    all_to_all x1, blocking collectives, on_device(): summed = lax.all_to_all(summed, 'col', 0, 0, tiled=True)  10.4 us
    all_to_all x1, waiting for transfers between devices, exchange(): return lax.all_to_all(pieces, BOTH, 0, 0, tiled=True)  3.93 us
    all_to_all x1, starting transfers between devices, exchange(): return lax.all_to_all(pieces, BOTH, 0, 0, tiled=True)  2.57 us
  transfers between devices with their start and end apart: 1, of which 1 were waited for; matrix products, arithmetic and copies ran while one was open for 0% of the time, Pallas kernels for 4%

profile of v5, /device:TPU:0, one launch (start us, length us, event | category | flops | bytes accessed | tf_op | source)
XLA Modules:
  0.0 80.4 jit_solution(9911206232045244903)
XLA Ops:
  0.6 0.0 copy-start.4
  0.6 0.0 copy-start.5
  0.7 0.0 copy-start.2
  0.7 0.0 copy-start
  2.5 3.2 %shard_map.176 = (f32[8,22,4,128]{3,2,1,0:T(4,128)S(1)}, f32[9,4,128]{2,1,0:T(4,128)S(1)}, f32[1680,128]{1,0:T(8,128)S(1)}, f32[11,128]{1,0:T(8,128)S(1)}) custom-call(s32[1,1,9]{2,1,0:T(1,128)} %codes.1, s32[1,1]{1,0:T(1,128)S(6)} %copy.19.counts, f32[1,1]{1,0:T(1,128)} %bitcast.2.damping, f32[1,1,256]{2,1,0:T(1,128)} %readings.1, f32[2]{0:T(128)} %depth.1, ...), custom_call_target="tpu_custom_call" | custom-call | tf_op jit(solution)/shard_map/pallas_call | solution.py:754
  5.8 12.9 %all_to_all.30.arrived = f32[8,22,4,128]{3,2,1,0:T(4,128)S(1)} all-to-all(f32[8,22,4,128]{3,2,1,0:T(4,128)S(1)} %get-tuple-element.18), channel_id=1, replica_groups=mesh['row'=8,'col'=4] {'row'}, dimensions={0} | all-to-all | bytes 720896 | tf_op jit(solution)/shard_map/all_to_all | solution.py:829
  18.7 10.4 %all_to_all.31.summed = f32[4,6,4,128]{3,2,1,0:T(4,128)S(1)} all-to-all(f32[4,6,4,128]{3,2,1,0:T(4,128)S(1)} %get-tuple-element.20), channel_id=1, replica_groups=mesh['row'=8,'col'=4] {'col'}, dimensions={0} | all-to-all | bytes 98304 | tf_op jit(solution)/shard_map/all_to_all | solution.py:835
  29.1 0.0 copy-done.4
  29.1 0.0 copy-done.5
  29.1 0.0 copy-done.2
  29.1 0.0 copy-done
  29.1 0.0 copy-start.1
  29.1 1.9 %shard_map.178 = (f32[32,5,4,128]{3,2,1,0:T(4,128)S(1)}, f32[4,128]{1,0:T(4,128)S(1)}) custom-call(f32[11,128]{1,0:T(8,128)S(1)} %get-tuple-element.17.meta, f32[1,1,9,256,512]{4,3,2,1,0:T(8,128)S(1)} %copy-done, f32[4,6,4,128]{3,2,1,0:T(4,128)S(1)} %all_to_all.31.summed, f32[9,4,128]{2,1,0:T(4,128)S(1)} %get-tuple-element.21.sums, ...), custom_call_target="tpu_custom_call" | custom-call | tf_op jit(solution)/shard_map/pallas_call | solution.py:754
  31.0 12.7 %all_to_all.32.arrived = f32[32,5,4,128]{3,2,1,0:T(4,128)S(1)} all-to-all(f32[32,5,4,128]{3,2,1,0:T(4,128)S(1)} %get-tuple-element.22), channel_id=1, replica_groups=mesh['row'=8,'col'=4] {'row','col'}, dimensions={0} | all-to-all | bytes 655360 | tf_op jit(solution)/shard_map/all_to_all | solution.py:765
  43.7 0.0 copy-start.3
  43.7 0.0 copy-start.6
  43.7 11.5 %all_to_all.33.shared = f32[32,2,4,128]{3,2,1,0:T(4,128)S(1)} all-to-all(f32[32,2,4,128]{3,2,1,0:T(4,128)S(1)} %shard_map.179), channel_id=1, replica_groups=mesh['row'=8,'col'=4] {'row','col'}, dimensions={0} | all-to-all | bytes 262144 | tf_op jit(solution)/shard_map/all_to_all | solution.py:765
  55.2 1.9 %shard_map.180 = (f32[32,4,128]{2,1,0:T(4,128)S(1)}, f32[32,4,128]{2,1,0:T(4,128)}, f32[5,4,128]{2,1,0:T(4,128)S(1)}) custom-call(f32[11,128]{1,0:T(8,128)S(1)} %get-tuple-element.17.meta, f32[1,1,9,256,512]{4,3,2,1,0:T(8,128)S(1)} %copy-done, f32[32,2,4,128]{3,2,1,0:T(4,128)S(1)} %all_to_all.33.shared), custom_call_target="tpu_custom_call" | custom-call | tf_op jit(solution)/shard_map/pallas_call | solution.py:754
  57.1 2.6 %all-to-all-start.4 = ((f32[32,4,128]{2,1,0:T(4,128)}), f32[32,4,128]{2,1,0:T(4,128)S(1)}, u32[]{:S(2)}, u32[]{:S(2)}) async-start(f32[32,4,128]{2,1,0:T(4,128)} %get-tuple-element.24), calls=%async_computation.4 | async-start | bytes 131072 | tf_op jit(solution)/shard_map/all_to_all | solution.py:765
  59.7 0.0 copy-done.1
  59.7 3.5 %shard_map.181 = (f32[32,16,128]{2,1,0:T(8,128)S(1)}, f32[32,16,128]{2,1,0:T(8,128)S(1)}) custom-call(f32[32,5,4,128]{3,2,1,0:T(4,128)S(1)} %all_to_all.32.arrived, f32[32,2,4,128]{3,2,1,0:T(4,128)S(1)} %all_to_all.33.shared, f32[32,4,128]{2,1,0:T(4,128)S(1)} %get-tuple-element.26.second, f32[5,4,128]{2,1,0:T(4,128)S(1)} %get-tuple-element.25.carry, ...), custom_call_target="tpu_custom_call" | custom-call | tf_op jit(solution)/shard_map/pallas_call | solution.py:754
  63.2 3.9 %all-to-all-done.4.measured = f32[32,4,128]{2,1,0:T(4,128)S(1)} async-done(((f32[32,4,128]{2,1,0:T(4,128)}), f32[32,4,128]{2,1,0:T(4,128)S(1)}, u32[]{:S(2)}, u32[]{:S(2)}) %all-to-all-start.4) | async-done | bytes 65568 | tf_op jit(solution)/shard_map/all_to_all | solution.py:765
  67.2 0.1 shard_map.182
  67.3 11.9 %all_to_all.34.arrived = f32[32,16,128]{2,1,0:T(8,128)S(1)} all-to-all(f32[32,16,128]{2,1,0:T(8,128)S(1)} %shard_map.182), channel_id=1, replica_groups=mesh['row'=8,'col'=4] {'row','col'}, dimensions={0} | all-to-all | bytes 524288 | tf_op jit(solution)/shard_map/all_to_all | solution.py:765
  79.2 0.0 copy-done.3
  79.2 0.0 copy-done.6
  79.2 1.2 %shard_map.183 = (f32[1,512]{1,0:T(1,128)}, f32[64,1024]{1,0:T(8,128)}) custom-call(f32[32,16,128]{2,1,0:T(8,128)S(1)} %all_to_all.34.arrived, f32[32,4,128]{2,1,0:T(4,128)S(1)} %all-to-all-done.4.measured, f32[5,4,128]{2,1,0:T(4,128)S(1)} %get-tuple-element.25.carry, f32[2,5,4,128]{3,2,1,0:T(4,128)S(1)} %copy-done.4, bf16[2,64,256]{2,1,0:T(8,128)(2,1)S(1)} %copy-done.6, ...), custom_call_target="tpu_custom_call" | custom-call | tf_op jit(solution)/shard_map/pallas_call | solution.py:754
  (2 shorter events, 0.1 us)
Async XLA Ops:
  0.6 28.4 %copy-start.4 = (f32[2,5,4,128]{3,2,1,0:T(4,128)S(1)}, f32[2,5,4,128]{3,2,1,0:T(4,128)}, u32[]{:S(2)}) copy-start(f32[2,5,4,128]{3,2,1,0:T(4,128)} %constant.18.clone.turns) | copy-start | bytes 61444
  0.6 28.4 %copy-start.5 = (bf16[2,128,128]{2,1,0:T(8,128)(2,1)S(1)}, bf16[2,128,128]{2,1,0:T(8,128)(2,1)}, u32[]{:S(2)}) copy-start(bf16[2,128,128]{2,1,0:T(8,128)(2,1)} %constant.19.clone.packed) | copy-start | bytes 196612
  0.7 28.4 %copy-start.2 = (bf16[2,256,256]{2,1,0:T(8,128)(2,1)S(1)}, bf16[2,256,256]{2,1,0:T(8,128)(2,1)}, u32[]{:S(2)}) copy-start(bf16[2,256,256]{2,1,0:T(8,128)(2,1)} %constant.20.clone.plain) | copy-start | bytes 786436
  0.7 28.4 %copy-start = (f32[1,1,9,256,512]{4,3,2,1,0:T(8,128)S(1)}, f32[1,1,9,256,512]{4,3,2,1,0:T(8,128)}, u32[]{:S(2)}) copy-start(f32[1,1,9,256,512]{4,3,2,1,0:T(8,128)} %source.5) | copy-start | bytes 14155780
  29.1 30.6 %copy-start.1 = (bf16[2048,256]{1,0:T(8,128)(2,1)S(1)}, bf16[2048,256]{1,0:T(8,128)(2,1)}, u32[]{:S(2)}) copy-start(bf16[2048,256]{1,0:T(8,128)(2,1)} %constant.21.clone.tables) | copy-start | bytes 3145732
  43.7 35.5 %copy-start.3 = (bf16[2,128,256]{2,1,0:T(8,128)(2,1)S(1)}, bf16[2,128,256]{2,1,0:T(8,128)(2,1)}, u32[]{:S(2)}) copy-start(bf16[2,128,256]{2,1,0:T(8,128)(2,1)} %constant.23.clone.plain) | copy-start | bytes 393220
  43.7 35.5 %copy-start.6 = (bf16[2,64,256]{2,1,0:T(8,128)(2,1)S(1)}, bf16[2,64,256]{2,1,0:T(8,128)(2,1)}, u32[]{:S(2)}) copy-start(bf16[2,64,256]{2,1,0:T(8,128)(2,1)} %constant.22.clone.packed) | copy-start | bytes 196612
  57.1 10.1 %all-to-all-start.4 = ((f32[32,4,128]{2,1,0:T(4,128)}), f32[32,4,128]{2,1,0:T(4,128)S(1)}, u32[]{:S(2)}, u32[]{:S(2)}) async-start(f32[32,4,128]{2,1,0:T(4,128)} %get-tuple-element.24), calls=%async_computation.4 | async-start | bytes 131072 | tf_op jit(solution)/shard_map/all_to_all | solution.py:765

commit v6 on v5

--- a/solution.py
+++ b/solution.py
@@ -186,39 +186,30 @@
     return blocks
 
 
-def apply_forward(tiles, copies, blocks, count, out, work):
+def apply_forward(tiles, blocks, count, out):
     slots, width = tiles.shape[1:]
     parts = width // LANES
-    squares = jnp.zeros((SUB, LANES), F32)
-    for group, end in ((0, 4), (4, 8), (8, FOOTPRINT)):
-        for k in range(group, end if copies else group):
-            copies[k].wait()
-        spread = [
-            [jnp.broadcast_to(blocks[k][p : p + 1], (SUB, LANES)) for p in range(parts)]
-            for k in range(group, end)
-        ]
-
-        def step(t, squares, group=group, spread=spread):
-            at = pl.multiple_of(t * SUB, SUB)
-            sums = [None] * parts
-            for k in range(len(spread)):
-                for p in range(parts):
-                    tile = tiles[group + k, pl.ds(at, SUB), p * LANES : (p + 1) * LANES]
-                    term = tile * spread[k][p]
-                    sums[p] = term if sums[p] is None else sums[p] + term
-            acc = functools.reduce(jnp.add, sums)
-            if group > 0:
-                acc = acc + work[pl.ds(at, SUB), :]
-            if group + len(spread) < FOOTPRINT:
-                work[pl.ds(at, SUB), :] = acc
-                return squares
-            slot = at + lax.broadcasted_iota(jnp.int32, (SUB, LANES), 0)
-            value = jnp.where(slot.astype(F32) < count, jnp.sum(acc, axis=1, keepdims=True), 0.0)
-            if out is not None:
-                out[pl.ds(at, SUB), :] = value
-            return squares + value * value
-
-        squares = lax.fori_loop(0, slots // SUB, step, squares, unroll=8)
+    spread = [
+        [jnp.broadcast_to(block[p : p + 1], (SUB, LANES)) for p in range(parts)] for block in blocks
+    ]
+
+    def step(t, squares):
+        at = pl.multiple_of(t * SUB, SUB)
+        sums = [None] * parts
+        for k in range(FOOTPRINT):
+            for p in range(parts):
+                tile = tiles[k, pl.ds(at, SUB), p * LANES : (p + 1) * LANES]
+                term = tile * spread[k][p]
+                sums[p] = term if sums[p] is None else sums[p] + term
+        acc = functools.reduce(jnp.add, sums)
+        slot = at + lax.broadcasted_iota(jnp.int32, (SUB, LANES), 0)
+        value = jnp.where(slot.astype(F32) < count, jnp.sum(acc, axis=1, keepdims=True), 0.0)
+        if out is not None:
+            out[pl.ds(at, SUB), :] = value
+        return squares + value * value
+
+    zero = jnp.zeros((SUB, LANES), F32)
+    squares = lax.fori_loop(0, slots // SUB, step, zero, unroll=8)
     return jnp.sum(squares, axis=0, keepdims=True)
 
 
@@ -233,15 +224,6 @@
             term = tile[rows, p * LANES : (p + 1) * LANES] * weight
             sums[p][t % 2] = term if t < 2 else sums[p][t % 2] + term
     return jnp.concatenate([jnp.sum(a + b, axis=0, keepdims=True) for a, b in sums], axis=0)
-
-
-def send_adjoint(tile, values, k, ints, out, rows, cols):
-    device, inside = neighbour(k, ints, rows, cols)
-    block = jnp.where(inside, apply_adjoint(tile, values), 0.0)
-    if len(out.shape) == 4:
-        out[device, 0] = out[device, 0] + block
-    else:
-        out[device] = out[device] + block
 
 
 def tile_copies(source, tiles, sems):
@@ -341,17 +323,35 @@
     fill_pieces(out, sums, col)
 
 
-def share_kernel(arrived, own, everywhere):
-    block = jnp.sum(arrived[:, 0] if len(arrived.shape) == 4 else arrived[...], axis=0)
-    both = jnp.stack([own[...], block])
-    everywhere[...] = jnp.broadcast_to(both[None], everywhere.shape)
+def around(rows, cols):
+    row, col = lax.axis_index("row"), lax.axis_index("col")
+    for code in range(FOOTPRINT):
+        north, east = row + code // 3 - 1, col + code % 3 - 1
+        inside = (north >= 0) & (north < rows) & (east >= 0) & (east < cols)
+        yield code, jnp.clip(north * cols + east, 0, rows * cols - 1), inside
+
+
+def share_kernel(rows, cols, arrived, near, everywhere, right):
+    get = (lambda d: arrived[d, 0]) if len(arrived.shape) == 4 else (lambda d: arrived[d])
+    for device in range(rows * cols):
+        right[device] = get(device)
+    block = None
+    for code, device, inside in around(rows, cols):
+        part = jnp.where(inside, get(device), 0.0)
+        block = part if block is None else block + part
+
+        @pl.when(inside)
+        def _():
+            right[device] = near[code]
+
+    everywhere[...] = jnp.broadcast_to(block[None], everywhere.shape)
 
 
 def normal_kernel(
-    rows, cols, meta, source, summed, sums, arrived, turns, packed, plain, out, own, *refs
+    rows, cols, meta, source, summed, sums, arrived, turns, packed, plain, out, near, *refs
 ):
-    (*apart, near, values, work, planes) = refs
-    tiles, copies = source.at[0, 0], None
+    (*apart, values, planes) = refs
+    tiles = source.at[0, 0]
     row, col = lax.axis_index("row"), lax.axis_index("col")
     ints = [meta[2 + k, 0].astype(jnp.int32) for k in range(FOOTPRINT)] + [None, row, col]
     for code in range(FOOTPRINT):
@@ -360,13 +360,12 @@
         near[code] = parts[0] + parts[1] + parts[2]
     blocks = [near[ints[k]] for k in range(FOOTPRINT)]
     me = row * cols + col
-    out[...] = jnp.zeros(out.shape, F32)
-    own[...] = near[FOOTPRINT // 2]
-    ridge = meta[1:2, :] * own[...]
-    if apart:
-        out[me] = ridge
-    else:
-        out[me, 0] = ridge
+    own = near[FOOTPRINT // 2]
+    for device in range(rows * cols):
+        if apart:
+            out[device] = own
+        else:
+            out[device, 0] = own
 
     def store(device, piece):
         if apart:
@@ -376,9 +375,18 @@
                 out[device, 1 + g] = piece[4 * g : 4 * g + 4]
 
     north_transform(rows, cols, arrived, turns, (packed, plain), planes, store)
-    apply_forward(tiles, copies, blocks, meta[0:1, :], values, work)
+    apply_forward(tiles, blocks, meta[0:1, :], values)
     for k in range(FOOTPRINT):
-        send_adjoint(tiles.at[k], values, k, ints, out, rows, cols)
+        device, inside = neighbour(k, ints, rows, cols)
+        block = apply_adjoint(tiles.at[k], values)
+        block = block + jnp.where(device == me, meta[1:2, :], 0.0) * own
+
+        @pl.when(inside)
+        def _():
+            if apart:
+                out[device] = block
+            else:
+                out[device, 0] = block
 
 
 def north_transform(rows, cols, arrived, turns, tables, planes, store):
@@ -644,7 +652,7 @@
 
 
 def map_kernel(
-    sizes, width, arrived, shared, second, carry, tables, side, known, response,
+    sizes, width, arrived, first, second, carry, tables, side, known, response,
     coarse, fine, work, mixed, back, *spec,
 ):
     rows, cols, own, bands = sizes
@@ -660,19 +668,15 @@
 
     spectrum = east_forward(get, sizes, side, tables, work)
     weigh(spectrum, 0, sizes, side, mixed, True)
-    model_mix(shared.at[:, 0], carry[4, 0:1, 0:1], sizes, side, tables, coarse, fine, work, mixed, False)
+    model_mix(first, carry[4, 0:1, 0:1], sizes, side, tables, coarse, fine, work, mixed, False)
     east_inverse(mixed, sizes, side, tables, back, store_pieces(known, width))
     model_mix(second, None, sizes, side, tables, coarse, fine, work, mixed, True)
     east_inverse(mixed, sizes, side, tables, back, store_pieces(response, width))
 
 
-def direction_kernel(
-    rows, cols, meta, source, shared, second, measured, carry,
-    work,
-):
-    tiles, copies = source.at[0, 0], None
+def direction_kernel(rows, cols, meta, source, first, applied, second, measured, carry):
+    tiles = source.at[0, 0]
     row, col = lax.axis_index("row"), lax.axis_index("col")
-    first, applied = shared.at[:, 0], shared.at[:, 1]
     norm = total(first[...] * first[...])
     step = norm / total(first[...] * applied[...])
     residual = first[...] - step[None] * applied[...]
@@ -686,7 +690,7 @@
         carry[at] = jnp.broadcast_to(value, carry.shape[1:])
     ints = [meta[2 + k, 0].astype(jnp.int32) for k in range(FOOTPRINT)] + [None, row, col]
     blocks = near_blocks(ints, second, rows, cols)
-    squares = apply_forward(tiles, copies, blocks, meta[0:1, :], None, work)
+    squares = apply_forward(tiles, blocks, meta[0:1, :], None)
     measured[...] = jnp.broadcast_to(squares[None], measured.shape)
 
 
@@ -834,9 +838,9 @@
     )
     summed = lax.all_to_all(summed, "col", 0, 0, tiled=True)
 
-    sums, right_own, *spectrum = call(
+    sums, near, *spectrum = call(
         functools.partial(normal_kernel, rows, cols),
-        (beside, shape(parts, LANES)) if joined else (everywhere, shape(parts, LANES), pieces),
+        (beside, nine) if joined else (everywhere, nine, pieces),
         [
             (VMEM, meta),
             (VMEM, kernel_tiles),
@@ -847,15 +851,15 @@
             (VMEM, forward_tables[0]),
             (VMEM, forward_tables[1]),
         ],
-        [scratch(FOOTPRINT, parts, LANES)]
-        + [scratch(slots, LANES), scratch(slots, LANES)]
-        + [scratch(rows, width, LANES)],
+        [scratch(slots, LANES), scratch(rows, width, LANES)],
     )
     sums = exchange(sums)
-    shared = call(
-        share_kernel, shape(devices, 2, parts, LANES), [(VMEM, sums), (VMEM, right_own)]
-    )
-    shared = exchange(shared)
+    applied_all, right_side = call(
+        functools.partial(share_kernel, rows, cols),
+        (everywhere, everywhere),
+        [(VMEM, sums), (VMEM, near)],
+    )
+    applied = exchange(applied_all)
     if joined:
         spectrum, sorted_work = sums, [scratch(cols, 2 * own, tile_east)]
     else:
@@ -866,8 +870,7 @@
     second, measured, carry = call(
         functools.partial(direction_kernel, rows, cols),
         (everywhere, everywhere, shape(5, parts, LANES)),
-        [(VMEM, meta), (VMEM, kernel_tiles), (VMEM, shared)],
-        [scratch(slots, LANES)],
+        [(VMEM, meta), (VMEM, kernel_tiles), (VMEM, right_side), (VMEM, applied)],
     )
     work = [
         scratch(LAYERS, 2 * rows, cols * LANES),
@@ -881,7 +884,7 @@
         (pieces, pieces),
         [
             (VMEM, spectrum),
-            (VMEM, shared),
+            (VMEM, right_side),
             (VMEM, second),
             (VMEM, carry),
             (VMEM, tables),

time: 80.7 us -> 79.8 us (0.989)
  blocking collectives: 59.4 us -> 58.5 us
    all_to_all x3, blocking collectives: 36.1 us -> 35.2 us  [exchange(): return lax.all_to_all(pieces, BOTH, 0, 0, tiled=True)]
where the time goes in v6:
time: 79.8 us; the launch traced here: 79.5 us
  blocking collectives  58.5 us (73%)
  Pallas kernels  11.9 us (15%)
  waiting for transfers between devices  3.93 us (5%)
  between operations  2.61 us (3%)
  starting transfers between devices  2.57 us (3%)
    all_to_all x3, blocking collectives, exchange(): return lax.all_to_all(pieces, BOTH, 0, 0, tiled=True)  35.2 us
    all_to_all x1, blocking collectives, on_device(): arrived = lax.all_to_all(sums, 'row', 0, 0, tiled=True)  12.9 us
    pallas_call x8, Pallas kernels, call(): pl.pallas_call(kernel, out_shape=outs, in_specs=[spec for spec, _ in ins]...  11.9 us
    all_to_all x1, blocking collectives, on_device(): summed = lax.all_to_all(summed, 'col', 0, 0, tiled=True)  10.4 us
    all_to_all x1, waiting for transfers between devices, exchange(): return lax.all_to_all(pieces, BOTH, 0, 0, tiled=True)  3.93 us
    all_to_all x1, starting transfers between devices, exchange(): return lax.all_to_all(pieces, BOTH, 0, 0, tiled=True)  2.57 us
  transfers between devices with their start and end apart: 1, of which 1 were waited for; matrix products, arithmetic and copies ran while one was open for 0% of the time, Pallas kernels for 4%

profile of v6, /device:TPU:0, one launch (start us, length us, event | category | flops | bytes accessed | tf_op | source)
XLA Modules:
  0.0 79.5 jit_solution(7911136113912939077)
XLA Ops:
  0.6 0.0 copy-start.4
  0.6 0.0 copy-start.5
  0.7 0.0 copy-start.2
  0.7 0.0 copy-start
  2.5 3.2 %shard_map.176 = (f32[8,22,4,128]{3,2,1,0:T(4,128)S(1)}, f32[9,4,128]{2,1,0:T(4,128)S(1)}, f32[1680,128]{1,0:T(8,128)S(1)}, f32[11,128]{1,0:T(8,128)S(1)}) custom-call(s32[1,1,9]{2,1,0:T(1,128)} %codes.1, s32[1,1]{1,0:T(1,128)S(6)} %copy.19.counts, f32[1,1]{1,0:T(1,128)} %bitcast.2.damping, f32[1,1,256]{2,1,0:T(1,128)} %readings.1, f32[2]{0:T(128)} %depth.1, ...), custom_call_target="tpu_custom_call" | custom-call | tf_op jit(solution)/shard_map/pallas_call | solution.py:758
  5.8 12.9 %all_to_all.30.arrived = f32[8,22,4,128]{3,2,1,0:T(4,128)S(1)} all-to-all(f32[8,22,4,128]{3,2,1,0:T(4,128)S(1)} %get-tuple-element.20), channel_id=1, replica_groups=mesh['row'=8,'col'=4] {'row'}, dimensions={0} | all-to-all | bytes 720896 | tf_op jit(solution)/shard_map/all_to_all | solution.py:833
  18.7 10.4 %all_to_all.31.summed = f32[4,6,4,128]{3,2,1,0:T(4,128)S(1)} all-to-all(f32[4,6,4,128]{3,2,1,0:T(4,128)S(1)} %get-tuple-element.22), channel_id=1, replica_groups=mesh['row'=8,'col'=4] {'col'}, dimensions={0} | all-to-all | bytes 98304 | tf_op jit(solution)/shard_map/all_to_all | solution.py:839
  29.1 0.0 copy-done.4
  29.1 0.0 copy-done.5
  29.1 0.0 copy-done.2
  29.1 0.0 copy-done
  29.1 0.0 copy-start.1
  29.1 1.9 %shard_map.178 = (f32[32,5,4,128]{3,2,1,0:T(4,128)S(1)}, f32[9,4,128]{2,1,0:T(4,128)S(1)}) custom-call(f32[11,128]{1,0:T(8,128)S(1)} %get-tuple-element.19.meta, f32[1,1,9,256,512]{4,3,2,1,0:T(8,128)S(1)} %copy-done, f32[4,6,4,128]{3,2,1,0:T(4,128)S(1)} %all_to_all.31.summed, f32[9,4,128]{2,1,0:T(4,128)S(1)} %get-tuple-element.23.sums, ...), custom_call_target="tpu_custom_call" | custom-call | tf_op jit(solution)/shard_map/pallas_call | solution.py:758
  31.0 12.7 %all_to_all.32.arrived = f32[32,5,4,128]{3,2,1,0:T(4,128)S(1)} all-to-all(f32[32,5,4,128]{3,2,1,0:T(4,128)S(1)} %get-tuple-element.24), channel_id=1, replica_groups=mesh['row'=8,'col'=4] {'row','col'}, dimensions={0} | all-to-all | bytes 655360 | tf_op jit(solution)/shard_map/all_to_all | solution.py:769
  43.7 0.0 copy-start.3
  43.7 0.0 copy-start.6
  43.7 0.1 shard_map.179
  43.8 10.6 %all_to_all.33.applied = f32[32,4,128]{2,1,0:T(4,128)S(1)} all-to-all(f32[32,4,128]{2,1,0:T(4,128)S(1)} %get-tuple-element.27), channel_id=1, replica_groups=mesh['row'=8,'col'=4] {'row','col'}, dimensions={0} | all-to-all | bytes 131072 | tf_op jit(solution)/shard_map/all_to_all | solution.py:769
  54.4 1.8 %shard_map.180 = (f32[32,4,128]{2,1,0:T(4,128)S(1)}, f32[32,4,128]{2,1,0:T(4,128)}, f32[5,4,128]{2,1,0:T(4,128)S(1)}) custom-call(f32[11,128]{1,0:T(8,128)S(1)} %get-tuple-element.19.meta, f32[1,1,9,256,512]{4,3,2,1,0:T(8,128)S(1)} %copy-done, f32[32,4,128]{2,1,0:T(4,128)S(1)} %get-tuple-element.26.first, f32[32,4,128]{2,1,0:T(4,128)S(1)} %all_to_all.33.applied), custom_call_target="tpu_custom_call" | custom-call | tf_op jit(solution)/shard_map/pallas_call | solution.py:758
  56.2 2.6 %all-to-all-start.4 = ((f32[32,4,128]{2,1,0:T(4,128)}), f32[32,4,128]{2,1,0:T(4,128)S(1)}, u32[]{:S(2)}, u32[]{:S(2)}) async-start(f32[32,4,128]{2,1,0:T(4,128)} %get-tuple-element.28), calls=%async_computation.4 | async-start | bytes 131072 | tf_op jit(solution)/shard_map/all_to_all | solution.py:769
  58.8 0.0 copy-done.1
  58.8 3.5 %shard_map.181 = (f32[32,16,128]{2,1,0:T(8,128)S(1)}, f32[32,16,128]{2,1,0:T(8,128)S(1)}) custom-call(f32[32,5,4,128]{3,2,1,0:T(4,128)S(1)} %all_to_all.32.arrived, f32[32,4,128]{2,1,0:T(4,128)S(1)} %get-tuple-element.26.first, f32[32,4,128]{2,1,0:T(4,128)S(1)} %get-tuple-element.30.second, f32[5,4,128]{2,1,0:T(4,128)S(1)} %get-tuple-element.29.carry, ...), custom_call_target="tpu_custom_call" | custom-call | tf_op jit(solution)/shard_map/pallas_call | solution.py:758
  62.3 3.9 %all-to-all-done.4.measured = f32[32,4,128]{2,1,0:T(4,128)S(1)} async-done(((f32[32,4,128]{2,1,0:T(4,128)}), f32[32,4,128]{2,1,0:T(4,128)S(1)}, u32[]{:S(2)}, u32[]{:S(2)}) %all-to-all-start.4) | async-done | bytes 65568 | tf_op jit(solution)/shard_map/all_to_all | solution.py:769
  66.2 0.1 shard_map.182
  66.4 11.9 %all_to_all.34.arrived = f32[32,16,128]{2,1,0:T(8,128)S(1)} all-to-all(f32[32,16,128]{2,1,0:T(8,128)S(1)} %shard_map.182), channel_id=1, replica_groups=mesh['row'=8,'col'=4] {'row','col'}, dimensions={0} | all-to-all | bytes 524288 | tf_op jit(solution)/shard_map/all_to_all | solution.py:769
  78.3 0.0 copy-done.3
  78.3 0.0 copy-done.6
  78.3 1.2 %shard_map.183 = (f32[1,512]{1,0:T(1,128)}, f32[64,1024]{1,0:T(8,128)}) custom-call(f32[32,16,128]{2,1,0:T(8,128)S(1)} %all_to_all.34.arrived, f32[32,4,128]{2,1,0:T(4,128)S(1)} %all-to-all-done.4.measured, f32[5,4,128]{2,1,0:T(4,128)S(1)} %get-tuple-element.29.carry, f32[2,5,4,128]{3,2,1,0:T(4,128)S(1)} %copy-done.4, bf16[2,64,256]{2,1,0:T(8,128)(2,1)S(1)} %copy-done.6, ...), custom_call_target="tpu_custom_call" | custom-call | tf_op jit(solution)/shard_map/pallas_call | solution.py:758
  (1 shorter events, 0.0 us)
Async XLA Ops:
  0.6 28.5 %copy-start.4 = (f32[2,5,4,128]{3,2,1,0:T(4,128)S(1)}, f32[2,5,4,128]{3,2,1,0:T(4,128)}, u32[]{:S(2)}) copy-start(f32[2,5,4,128]{3,2,1,0:T(4,128)} %constant.18.clone.turns) | copy-start | bytes 61444
  0.6 28.4 %copy-start.5 = (bf16[2,128,128]{2,1,0:T(8,128)(2,1)S(1)}, bf16[2,128,128]{2,1,0:T(8,128)(2,1)}, u32[]{:S(2)}) copy-start(bf16[2,128,128]{2,1,0:T(8,128)(2,1)} %constant.19.clone.packed) | copy-start | bytes 196612
  0.7 28.4 %copy-start.2 = (bf16[2,256,256]{2,1,0:T(8,128)(2,1)S(1)}, bf16[2,256,256]{2,1,0:T(8,128)(2,1)}, u32[]{:S(2)}) copy-start(bf16[2,256,256]{2,1,0:T(8,128)(2,1)} %constant.20.clone.plain) | copy-start | bytes 786436
  0.7 28.4 %copy-start = (f32[1,1,9,256,512]{4,3,2,1,0:T(8,128)S(1)}, f32[1,1,9,256,512]{4,3,2,1,0:T(8,128)}, u32[]{:S(2)}) copy-start(f32[1,1,9,256,512]{4,3,2,1,0:T(8,128)} %source.5) | copy-start | bytes 14155780
  29.1 29.7 %copy-start.1 = (bf16[2048,256]{1,0:T(8,128)(2,1)S(1)}, bf16[2048,256]{1,0:T(8,128)(2,1)}, u32[]{:S(2)}) copy-start(bf16[2048,256]{1,0:T(8,128)(2,1)} %constant.21.clone.tables) | copy-start | bytes 3145732
  43.7 34.6 %copy-start.3 = (bf16[2,128,256]{2,1,0:T(8,128)(2,1)S(1)}, bf16[2,128,256]{2,1,0:T(8,128)(2,1)}, u32[]{:S(2)}) copy-start(bf16[2,128,256]{2,1,0:T(8,128)(2,1)} %constant.23.clone.plain) | copy-start | bytes 393220
  43.7 34.6 %copy-start.6 = (bf16[2,64,256]{2,1,0:T(8,128)(2,1)S(1)}, bf16[2,64,256]{2,1,0:T(8,128)(2,1)}, u32[]{:S(2)}) copy-start(bf16[2,64,256]{2,1,0:T(8,128)(2,1)} %constant.22.clone.packed) | copy-start | bytes 196612
  56.2 10.1 %all-to-all-start.4 = ((f32[32,4,128]{2,1,0:T(4,128)}), f32[32,4,128]{2,1,0:T(4,128)S(1)}, u32[]{:S(2)}, u32[]{:S(2)}) async-start(f32[32,4,128]{2,1,0:T(4,128)} %get-tuple-element.28), calls=%async_computation.4 | async-start | bytes 131072 | tf_op jit(solution)/shard_map/all_to_all | solution.py:769

commit v7 on v6

--- a/solution.py
+++ b/solution.py
@@ -652,10 +652,17 @@
 
 
 def map_kernel(
-    sizes, width, arrived, first, second, carry, tables, side, known, response,
+    sizes, width, arrived, first, second, meta, scalars, tables, side, known, response, carry,
     coarse, fine, work, mixed, back, *spec,
 ):
     rows, cols, own, bands = sizes
+    step = scalars[1:2, 0:1]
+    me = lax.axis_index("row") * cols + lax.axis_index("col")
+    carry[0] = step * first[me]
+    carry[1] = second[me]
+    carry[2] = jnp.broadcast_to(scalars[0:1], carry.shape[1:])
+    ridge = meta[1:2, 0:1] * total(second[...] * second[...])
+    carry[3] = jnp.broadcast_to(ridge, carry.shape[1:])
     if spec:
         sort_east(arrived, sizes, spec[0])
     spec = spec[0] if spec else arrived
@@ -668,13 +675,13 @@
 
     spectrum = east_forward(get, sizes, side, tables, work)
     weigh(spectrum, 0, sizes, side, mixed, True)
-    model_mix(first, carry[4, 0:1, 0:1], sizes, side, tables, coarse, fine, work, mixed, False)
+    model_mix(first, step, sizes, side, tables, coarse, fine, work, mixed, False)
     east_inverse(mixed, sizes, side, tables, back, store_pieces(known, width))
     model_mix(second, None, sizes, side, tables, coarse, fine, work, mixed, True)
     east_inverse(mixed, sizes, side, tables, back, store_pieces(response, width))
 
 
-def direction_kernel(rows, cols, meta, source, first, applied, second, measured, carry):
+def direction_kernel(rows, cols, meta, source, first, applied, second, measured, scalars):
     tiles = source.at[0, 0]
     row, col = lax.axis_index("row"), lax.axis_index("col")
     norm = total(first[...] * first[...])
@@ -682,12 +689,8 @@
     residual = first[...] - step[None] * applied[...]
     norm_next = total(residual * residual)
     second[...] = residual + (norm_next / norm)[None] * first[...]
-    ridge = meta[1:2, 0:1] * total(second[...] * second[...])
-    me = row * cols + col
-    carry[0] = step * first[me]
-    carry[1] = second[me]
-    for at, value in ((2, norm_next), (3, ridge), (4, step)):
-        carry[at] = jnp.broadcast_to(value, carry.shape[1:])
+    scalars[0:1] = jnp.broadcast_to(norm_next, (1, LANES))
+    scalars[1:2] = jnp.broadcast_to(step, (1, LANES))
     ints = [meta[2 + k, 0].astype(jnp.int32) for k in range(FOOTPRINT)] + [None, row, col]
     blocks = near_blocks(ints, second, rows, cols)
     squares = apply_forward(tiles, blocks, meta[0:1, :], None)
@@ -867,9 +870,9 @@
         spectrum = spectrum.reshape(rows, cols, own, 2, width).transpose(1, 3, 2, 0, 4)
         spectrum = spectrum.reshape(cols, 2 * own, tile_east)
 
-    second, measured, carry = call(
+    second, measured, scalars = call(
         functools.partial(direction_kernel, rows, cols),
-        (everywhere, everywhere, shape(5, parts, LANES)),
+        (everywhere, everywhere, shape(2, LANES)),
         [(VMEM, meta), (VMEM, kernel_tiles), (VMEM, right_side), (VMEM, applied)],
     )
     work = [
@@ -879,14 +882,15 @@
         scratch(own * bands, 2 * LANES),
         scratch(own * bands, 2 * LANES),
     ]
-    known, response = call(
+    known, response, carry = call(
         functools.partial(map_kernel, sizes, width),
-        (pieces, pieces),
+        (pieces, pieces, shape(4, parts, LANES)),
         [
             (VMEM, spectrum),
             (VMEM, right_side),
             (VMEM, second),
-            (VMEM, carry),
+            (VMEM, meta),
+            (VMEM, scalars),
             (VMEM, tables),
             (VMEM, side),
         ],

time: 79.8 us -> 79.6 us (level)
  no operation moved by 1% of the time
where the time goes in v7:
time: 79.6 us; the launch traced here: 79.3 us
  blocking collectives  58.5 us (73%)
  Pallas kernels  11.6 us (15%)
  waiting for transfers between devices  3.92 us (5%)
  between operations  2.61 us (3%)
  starting transfers between devices  2.57 us (3%)
    all_to_all x3, blocking collectives, exchange(): return lax.all_to_all(pieces, BOTH, 0, 0, tiled=True)  35.2 us
    all_to_all x1, blocking collectives, on_device(): arrived = lax.all_to_all(sums, 'row', 0, 0, tiled=True)  12.9 us
    pallas_call x8, Pallas kernels, call(): pl.pallas_call(kernel, out_shape=outs, in_specs=[spec for spec, _ in ins]...  11.6 us
    all_to_all x1, blocking collectives, on_device(): summed = lax.all_to_all(summed, 'col', 0, 0, tiled=True)  10.4 us
    all_to_all x1, waiting for transfers between devices, exchange(): return lax.all_to_all(pieces, BOTH, 0, 0, tiled=True)  3.92 us
    all_to_all x1, starting transfers between devices, exchange(): return lax.all_to_all(pieces, BOTH, 0, 0, tiled=True)  2.57 us
  transfers between devices with their start and end apart: 1, of which 1 were waited for; matrix products, arithmetic and copies ran while one was open for 0% of the time, Pallas kernels for 4%

profile of v7, /device:TPU:0, one launch (start us, length us, event | category | flops | bytes accessed | tf_op | source)
XLA Modules:
  0.0 79.3 jit_solution(9253824542911265953)
XLA Ops:
  0.6 0.0 copy-start.4
  0.6 0.0 copy-start.5
  0.7 0.0 copy-start.2
  0.7 0.0 copy-start
  2.5 3.2 %shard_map.176 = (f32[8,22,4,128]{3,2,1,0:T(4,128)S(1)}, f32[9,4,128]{2,1,0:T(4,128)S(1)}, f32[1680,128]{1,0:T(8,128)S(1)}, f32[11,128]{1,0:T(8,128)S(1)}) custom-call(s32[1,1,9]{2,1,0:T(1,128)} %codes.1, s32[1,1]{1,0:T(1,128)S(6)} %copy.19.counts, f32[1,1]{1,0:T(1,128)} %bitcast.2.damping, f32[1,1,256]{2,1,0:T(1,128)} %readings.1, f32[2]{0:T(128)} %depth.1, ...), custom_call_target="tpu_custom_call" | custom-call | tf_op jit(solution)/shard_map/pallas_call | solution.py:761
  5.8 12.9 %all_to_all.30.arrived = f32[8,22,4,128]{3,2,1,0:T(4,128)S(1)} all-to-all(f32[8,22,4,128]{3,2,1,0:T(4,128)S(1)} %get-tuple-element.21), channel_id=1, replica_groups=mesh['row'=8,'col'=4] {'row'}, dimensions={0} | all-to-all | bytes 720896 | tf_op jit(solution)/shard_map/all_to_all | solution.py:836
  18.7 10.4 %all_to_all.31.summed = f32[4,6,4,128]{3,2,1,0:T(4,128)S(1)} all-to-all(f32[4,6,4,128]{3,2,1,0:T(4,128)S(1)} %get-tuple-element.23), channel_id=1, replica_groups=mesh['row'=8,'col'=4] {'col'}, dimensions={0} | all-to-all | bytes 98304 | tf_op jit(solution)/shard_map/all_to_all | solution.py:842
  29.1 0.0 copy-done.4
  29.1 0.0 copy-done.5
  29.1 0.0 copy-done.2
  29.1 0.0 copy-done
  29.1 0.0 copy-start.1
  29.1 1.9 %shard_map.178 = (f32[32,5,4,128]{3,2,1,0:T(4,128)S(1)}, f32[9,4,128]{2,1,0:T(4,128)S(1)}) custom-call(f32[11,128]{1,0:T(8,128)S(1)} %get-tuple-element.20.meta, f32[1,1,9,256,512]{4,3,2,1,0:T(8,128)S(1)} %copy-done, f32[4,6,4,128]{3,2,1,0:T(4,128)S(1)} %all_to_all.31.summed, f32[9,4,128]{2,1,0:T(4,128)S(1)} %get-tuple-element.24.sums, ...), custom_call_target="tpu_custom_call" | custom-call | tf_op jit(solution)/shard_map/pallas_call | solution.py:761
  31.0 12.7 %all_to_all.32.arrived = f32[32,5,4,128]{3,2,1,0:T(4,128)S(1)} all-to-all(f32[32,5,4,128]{3,2,1,0:T(4,128)S(1)} %get-tuple-element.25), channel_id=1, replica_groups=mesh['row'=8,'col'=4] {'row','col'}, dimensions={0} | all-to-all | bytes 655360 | tf_op jit(solution)/shard_map/all_to_all | solution.py:772
  43.7 0.0 copy-start.3
  43.7 0.0 copy-start.6
  43.7 0.1 shard_map.179
  43.8 10.6 %all_to_all.33.applied = f32[32,4,128]{2,1,0:T(4,128)S(1)} all-to-all(f32[32,4,128]{2,1,0:T(4,128)S(1)} %get-tuple-element.28), channel_id=1, replica_groups=mesh['row'=8,'col'=4] {'row','col'}, dimensions={0} | all-to-all | bytes 131072 | tf_op jit(solution)/shard_map/all_to_all | solution.py:772
  54.4 1.6 %shard_map.180 = (f32[32,4,128]{2,1,0:T(4,128)S(1)}, f32[32,4,128]{2,1,0:T(4,128)}, f32[2,128]{1,0:T(2,128)S(1)}) custom-call(f32[11,128]{1,0:T(8,128)S(1)} %get-tuple-element.20.meta, f32[1,1,9,256,512]{4,3,2,1,0:T(8,128)S(1)} %copy-done, f32[32,4,128]{2,1,0:T(4,128)S(1)} %get-tuple-element.27.first, f32[32,4,128]{2,1,0:T(4,128)S(1)} %all_to_all.33.applied), custom_call_target="tpu_custom_call" | custom-call | tf_op jit(solution)/shard_map/pallas_call | solution.py:761
  55.9 2.6 %all-to-all-start.4 = ((f32[32,4,128]{2,1,0:T(4,128)}), f32[32,4,128]{2,1,0:T(4,128)S(1)}, u32[]{:S(2)}, u32[]{:S(2)}) async-start(f32[32,4,128]{2,1,0:T(4,128)} %get-tuple-element.29), calls=%async_computation.4 | async-start | bytes 131072 | tf_op jit(solution)/shard_map/all_to_all | solution.py:772
  58.5 0.0 copy-done.1
  58.5 3.6 %shard_map.181 = (f32[32,16,128]{2,1,0:T(8,128)S(1)}, f32[32,16,128]{2,1,0:T(8,128)S(1)}, f32[4,4,128]{2,1,0:T(4,128)S(1)}) custom-call(f32[32,5,4,128]{3,2,1,0:T(4,128)S(1)} %all_to_all.32.arrived, f32[32,4,128]{2,1,0:T(4,128)S(1)} %get-tuple-element.27.first, f32[32,4,128]{2,1,0:T(4,128)S(1)} %get-tuple-element.30.second, ...), custom_call_target="tpu_custom_call" | custom-call | tf_op jit(solution)/shard_map/pallas_call | solution.py:761
  62.1 3.9 %all-to-all-done.4.measured = f32[32,4,128]{2,1,0:T(4,128)S(1)} async-done(((f32[32,4,128]{2,1,0:T(4,128)}), f32[32,4,128]{2,1,0:T(4,128)S(1)}, u32[]{:S(2)}, u32[]{:S(2)}) %all-to-all-start.4) | async-done | bytes 65568 | tf_op jit(solution)/shard_map/all_to_all | solution.py:772
  66.0 0.1 shard_map.182
  66.1 11.9 %all_to_all.34.arrived = f32[32,16,128]{2,1,0:T(8,128)S(1)} all-to-all(f32[32,16,128]{2,1,0:T(8,128)S(1)} %shard_map.182), channel_id=1, replica_groups=mesh['row'=8,'col'=4] {'row','col'}, dimensions={0} | all-to-all | bytes 524288 | tf_op jit(solution)/shard_map/all_to_all | solution.py:772
  78.1 0.0 copy-done.3
  78.1 0.0 copy-done.6
  78.1 1.2 %shard_map.183 = (f32[1,512]{1,0:T(1,128)}, f32[64,1024]{1,0:T(8,128)}) custom-call(f32[32,16,128]{2,1,0:T(8,128)S(1)} %all_to_all.34.arrived, f32[32,4,128]{2,1,0:T(4,128)S(1)} %all-to-all-done.4.measured, f32[4,4,128]{2,1,0:T(4,128)S(1)} %get-tuple-element.33.carry, f32[2,5,4,128]{3,2,1,0:T(4,128)S(1)} %copy-done.4, bf16[2,64,256]{2,1,0:T(8,128)(2,1)S(1)} %copy-done.6, ...), custom_call_target="tpu_custom_call" | custom-call | tf_op jit(solution)/shard_map/pallas_call | solution.py:761
  (1 shorter events, 0.0 us)
Async XLA Ops:
  0.6 28.5 %copy-start.4 = (f32[2,5,4,128]{3,2,1,0:T(4,128)S(1)}, f32[2,5,4,128]{3,2,1,0:T(4,128)}, u32[]{:S(2)}) copy-start(f32[2,5,4,128]{3,2,1,0:T(4,128)} %constant.18.clone.turns) | copy-start | bytes 61444
  0.6 28.4 %copy-start.5 = (bf16[2,128,128]{2,1,0:T(8,128)(2,1)S(1)}, bf16[2,128,128]{2,1,0:T(8,128)(2,1)}, u32[]{:S(2)}) copy-start(bf16[2,128,128]{2,1,0:T(8,128)(2,1)} %constant.19.clone.packed) | copy-start | bytes 196612
  0.7 28.4 %copy-start.2 = (bf16[2,256,256]{2,1,0:T(8,128)(2,1)S(1)}, bf16[2,256,256]{2,1,0:T(8,128)(2,1)}, u32[]{:S(2)}) copy-start(bf16[2,256,256]{2,1,0:T(8,128)(2,1)} %constant.20.clone.plain) | copy-start | bytes 786436
  0.7 28.4 %copy-start = (f32[1,1,9,256,512]{4,3,2,1,0:T(8,128)S(1)}, f32[1,1,9,256,512]{4,3,2,1,0:T(8,128)}, u32[]{:S(2)}) copy-start(f32[1,1,9,256,512]{4,3,2,1,0:T(8,128)} %source.5) | copy-start | bytes 14155780
  29.1 29.4 %copy-start.1 = (bf16[2048,256]{1,0:T(8,128)(2,1)S(1)}, bf16[2048,256]{1,0:T(8,128)(2,1)}, u32[]{:S(2)}) copy-start(bf16[2048,256]{1,0:T(8,128)(2,1)} %constant.21.clone.tables) | copy-start | bytes 3145732
  43.7 34.4 %copy-start.3 = (bf16[2,128,256]{2,1,0:T(8,128)(2,1)S(1)}, bf16[2,128,256]{2,1,0:T(8,128)(2,1)}, u32[]{:S(2)}) copy-start(bf16[2,128,256]{2,1,0:T(8,128)(2,1)} %constant.23.clone.plain) | copy-start | bytes 393220
  43.7 34.4 %copy-start.6 = (bf16[2,64,256]{2,1,0:T(8,128)(2,1)S(1)}, bf16[2,64,256]{2,1,0:T(8,128)(2,1)}, u32[]{:S(2)}) copy-start(bf16[2,64,256]{2,1,0:T(8,128)(2,1)} %constant.22.clone.packed) | copy-start | bytes 196612
  55.9 10.1 %all-to-all-start.4 = ((f32[32,4,128]{2,1,0:T(4,128)}), f32[32,4,128]{2,1,0:T(4,128)S(1)}, u32[]{:S(2)}, u32[]{:S(2)}) async-start(f32[32,4,128]{2,1,0:T(4,128)} %get-tuple-element.29), calls=%async_computation.4 | async-start | bytes 131072 | tf_op jit(solution)/shard_map/all_to_all | solution.py:772

commit v8 on v7

--- a/solution.py
+++ b/solution.py
@@ -20,6 +20,7 @@
 BOTH = ("row", "col")
 COUNT, ROW, COL = 9, 10, 11
 SENT = 6
+SMALL_AT = 2 + FOOTPRINT
 MIB = 1024 * 1024
 SMALL, LARGE = 24 * MIB, 62 * MIB
 F32 = jnp.float32
@@ -280,7 +281,9 @@
         turn = jnp.full((1, LANES), angles[1, m], F32)
         flat = jnp.cos(up)
         trig += [jnp.sin(up), flat * jnp.cos(turn), flat * jnp.sin(turn)]
-    put_weights(sizes, row, col, [depth_in[l] for l in range(LAYERS)], trig, side)
+    small = trig + [jnp.full((1, LANES), depth_in[l], F32) for l in range(LAYERS)]
+    for n, value in enumerate(small):
+        meta[SMALL_AT + n : SMALL_AT + n + 1, :] = value
     for k in range(FOOTPRINT):
         copies[k].wait()
         kept[ints[k]] = apply_adjoint(tiles.at[k], values)
@@ -613,7 +616,7 @@
     return out
 
 
-def model_mix(vector, scale, sizes, side, tables, coarse, fine, work, mixed, first):
+def model_mix(vector, scale, sizes, side, weights, tables, coarse, fine, work, mixed, first):
     rows, cols, own, bands = sizes
     depth = cols * SRC_COLS
     planes = jnp.concatenate(model_rows(vector, sizes, side, coarse), axis=0)
@@ -630,7 +633,7 @@
             return fine[at : at + SUB, cut], fine[at + own : at + own + SUB, cut]
 
         spectrum = east_forward(get, sizes, side, tables, work)
-        weigh(spectrum, 1 + layer, sizes, side, mixed, first and layer == 0)
+        weigh(spectrum, 1 + layer, sizes, weights, mixed, first and layer == 0)
 
 
 def sort_east(arrived, sizes, spec):
@@ -653,9 +656,11 @@
 
 def map_kernel(
     sizes, width, arrived, first, second, meta, scalars, tables, side, known, response, carry,
-    coarse, fine, work, mixed, back, *spec,
+    weights, coarse, fine, work, mixed, back, *spec,
 ):
     rows, cols, own, bands = sizes
+    small = [meta[SMALL_AT + n : SMALL_AT + n + 1, :] for n in range(6 + LAYERS)]
+    put_weights(sizes, lax.axis_index("row"), lax.axis_index("col"), small[6:], small[:6], weights)
     step = scalars[1:2, 0:1]
     me = lax.axis_index("row") * cols + lax.axis_index("col")
     carry[0] = step * first[me]
@@ -674,10 +679,10 @@
         return spec[m // per, at : at + SUB, cut], spec[m // per, own + at : own + at + SUB, cut]
 
     spectrum = east_forward(get, sizes, side, tables, work)
-    weigh(spectrum, 0, sizes, side, mixed, True)
-    model_mix(first, step, sizes, side, tables, coarse, fine, work, mixed, False)
+    weigh(spectrum, 0, sizes, weights, mixed, True)
+    model_mix(first, step, sizes, side, weights, tables, coarse, fine, work, mixed, False)
     east_inverse(mixed, sizes, side, tables, back, store_pieces(known, width))
-    model_mix(second, None, sizes, side, tables, coarse, fine, work, mixed, True)
+    model_mix(second, None, sizes, side, weights, tables, coarse, fine, work, mixed, True)
     east_inverse(mixed, sizes, side, tables, back, store_pieces(response, width))
 
 
@@ -811,7 +816,7 @@
             shape(rows, SENT + width // 4, parts, LANES),
             nine,
             shape(side_rows(own, bands, rows)[-1], LANES),
-            shape(2 + FOOTPRINT, LANES),
+            shape(SMALL_AT + 6 + LAYERS, LANES),
         ),
         [apart(footprints), (VMEM, counts), (VMEM, damping.reshape(1, 1))]
         + [
@@ -876,6 +881,7 @@
         [(VMEM, meta), (VMEM, kernel_tiles), (VMEM, right_side), (VMEM, applied)],
     )
     work = [
+        scratch(side_rows(own, bands, rows)[1], LANES),
         scratch(LAYERS, 2 * rows, cols * LANES),
         scratch(LAYERS * 2 * own, east),
         scratch((own + 1) * bands, 2 * LANES),

time: 79.6 us -> 79.6 us (level)
  transfers between devices with their start and end apart: 1 -> 1, of which waited for: 1 -> 1; matrix products, arithmetic and copies ran while one was open for 0% -> 0% of each run, Pallas kernels for 4% -> 5%
where the time goes in v8:
time: 79.6 us; the launch traced here: 79.3 us
  blocking collectives  58.7 us (74%)
  Pallas kernels  11.7 us (15%)
  waiting for transfers between devices  3.66 us (5%)
  between operations  2.61 us (3%)
  starting transfers between devices  2.57 us (3%)
    all_to_all x3, blocking collectives, exchange(): return lax.all_to_all(pieces, BOTH, 0, 0, tiled=True)  35.4 us
    all_to_all x1, blocking collectives, on_device(): arrived = lax.all_to_all(sums, 'row', 0, 0, tiled=True)  13 us
    pallas_call x8, Pallas kernels, call(): pl.pallas_call(kernel, out_shape=outs, in_specs=[spec for spec, _ in ins]...  11.7 us
    all_to_all x1, blocking collectives, on_device(): summed = lax.all_to_all(summed, 'col', 0, 0, tiled=True)  10.4 us
    all_to_all x1, waiting for transfers between devices, exchange(): return lax.all_to_all(pieces, BOTH, 0, 0, tiled=True)  3.66 us
    all_to_all x1, starting transfers between devices, exchange(): return lax.all_to_all(pieces, BOTH, 0, 0, tiled=True)  2.57 us
  transfers between devices with their start and end apart: 1, of which 1 were waited for; matrix products, arithmetic and copies ran while one was open for 0% of the time, Pallas kernels for 5%

profile of v8, /device:TPU:0, one launch (start us, length us, event | category | flops | bytes accessed | tf_op | source)
XLA Modules:
  0.0 79.3 jit_solution(13199272290840744197)
XLA Ops:
  0.6 0.0 copy-start.4
  0.6 0.0 copy-start.5
  0.7 0.0 copy-start.2
  0.7 0.0 copy-start
  2.5 3.0 %shard_map.176 = (f32[8,22,4,128]{3,2,1,0:T(4,128)S(1)}, f32[9,4,128]{2,1,0:T(4,128)S(1)}, f32[1680,128]{1,0:T(8,128)S(1)}, f32[19,128]{1,0:T(8,128)S(1)}) custom-call(s32[1,1,9]{2,1,0:T(1,128)} %codes.1, s32[1,1]{1,0:T(1,128)S(6)} %copy.19.counts, f32[1,1]{1,0:T(1,128)} %bitcast.2.damping, f32[1,1,256]{2,1,0:T(1,128)} %readings.1, f32[2]{0:T(128)} %depth.1, ...), custom_call_target="tpu_custom_call" | custom-call | tf_op jit(solution)/shard_map/pallas_call | solution.py:766
  5.6 13.0 %all_to_all.30.arrived = f32[8,22,4,128]{3,2,1,0:T(4,128)S(1)} all-to-all(f32[8,22,4,128]{3,2,1,0:T(4,128)S(1)} %get-tuple-element.21), channel_id=1, replica_groups=mesh['row'=8,'col'=4] {'row'}, dimensions={0} | all-to-all | bytes 720896 | tf_op jit(solution)/shard_map/all_to_all | solution.py:841
  18.6 10.4 %all_to_all.31.summed = f32[4,6,4,128]{3,2,1,0:T(4,128)S(1)} all-to-all(f32[4,6,4,128]{3,2,1,0:T(4,128)S(1)} %get-tuple-element.23), channel_id=1, replica_groups=mesh['row'=8,'col'=4] {'col'}, dimensions={0} | all-to-all | bytes 98304 | tf_op jit(solution)/shard_map/all_to_all | solution.py:847
  28.9 0.0 copy-done.4
  28.9 0.0 copy-done.5
  28.9 0.0 copy-done.2
  28.9 0.0 copy-done
  28.9 0.0 copy-start.1
  29.0 1.9 %shard_map.178 = (f32[32,5,4,128]{3,2,1,0:T(4,128)S(1)}, f32[9,4,128]{2,1,0:T(4,128)S(1)}) custom-call(f32[19,128]{1,0:T(8,128)S(1)} %get-tuple-element.20.meta, f32[1,1,9,256,512]{4,3,2,1,0:T(8,128)S(1)} %copy-done, f32[4,6,4,128]{3,2,1,0:T(4,128)S(1)} %all_to_all.31.summed, f32[9,4,128]{2,1,0:T(4,128)S(1)} %get-tuple-element.24.sums, ...), custom_call_target="tpu_custom_call" | custom-call | tf_op jit(solution)/shard_map/pallas_call | solution.py:766
  30.8 12.7 %all_to_all.32.arrived = f32[32,5,4,128]{3,2,1,0:T(4,128)S(1)} all-to-all(f32[32,5,4,128]{3,2,1,0:T(4,128)S(1)} %get-tuple-element.25), channel_id=1, replica_groups=mesh['row'=8,'col'=4] {'row','col'}, dimensions={0} | all-to-all | bytes 655360 | tf_op jit(solution)/shard_map/all_to_all | solution.py:777
  43.5 0.0 copy-start.3
  43.5 0.0 copy-start.6
  43.5 0.1 shard_map.179
  43.6 10.6 %all_to_all.33.applied = f32[32,4,128]{2,1,0:T(4,128)S(1)} all-to-all(f32[32,4,128]{2,1,0:T(4,128)S(1)} %get-tuple-element.28), channel_id=1, replica_groups=mesh['row'=8,'col'=4] {'row','col'}, dimensions={0} | all-to-all | bytes 131072 | tf_op jit(solution)/shard_map/all_to_all | solution.py:777
  54.2 1.6 %shard_map.180 = (f32[32,4,128]{2,1,0:T(4,128)S(1)}, f32[32,4,128]{2,1,0:T(4,128)}, f32[2,128]{1,0:T(2,128)S(1)}) custom-call(f32[19,128]{1,0:T(8,128)S(1)} %get-tuple-element.20.meta, f32[1,1,9,256,512]{4,3,2,1,0:T(8,128)S(1)} %copy-done, f32[32,4,128]{2,1,0:T(4,128)S(1)} %get-tuple-element.27.first, f32[32,4,128]{2,1,0:T(4,128)S(1)} %all_to_all.33.applied), custom_call_target="tpu_custom_call" | custom-call | tf_op jit(solution)/shard_map/pallas_call | solution.py:766
  55.8 2.6 %all-to-all-start.4 = ((f32[32,4,128]{2,1,0:T(4,128)}), f32[32,4,128]{2,1,0:T(4,128)S(1)}, u32[]{:S(2)}, u32[]{:S(2)}) async-start(f32[32,4,128]{2,1,0:T(4,128)} %get-tuple-element.29), calls=%async_computation.4 | async-start | bytes 131072 | tf_op jit(solution)/shard_map/all_to_all | solution.py:777
  58.4 0.0 copy-done.1
  58.4 3.8 %shard_map.181 = (f32[32,16,128]{2,1,0:T(8,128)S(1)}, f32[32,16,128]{2,1,0:T(8,128)S(1)}, f32[4,4,128]{2,1,0:T(4,128)S(1)}) custom-call(f32[32,5,4,128]{3,2,1,0:T(4,128)S(1)} %all_to_all.32.arrived, f32[32,4,128]{2,1,0:T(4,128)S(1)} %get-tuple-element.27.first, f32[32,4,128]{2,1,0:T(4,128)S(1)} %get-tuple-element.30.second, ...), custom_call_target="tpu_custom_call" | custom-call | tf_op jit(solution)/shard_map/pallas_call | solution.py:766
  62.2 3.7 %all-to-all-done.4.measured = f32[32,4,128]{2,1,0:T(4,128)S(1)} async-done(((f32[32,4,128]{2,1,0:T(4,128)}), f32[32,4,128]{2,1,0:T(4,128)S(1)}, u32[]{:S(2)}, u32[]{:S(2)}) %all-to-all-start.4) | async-done | bytes 65568 | tf_op jit(solution)/shard_map/all_to_all | solution.py:777
  65.9 0.1 shard_map.182
  66.0 12.1 %all_to_all.34.arrived = f32[32,16,128]{2,1,0:T(8,128)S(1)} all-to-all(f32[32,16,128]{2,1,0:T(8,128)S(1)} %shard_map.182), channel_id=1, replica_groups=mesh['row'=8,'col'=4] {'row','col'}, dimensions={0} | all-to-all | bytes 524288 | tf_op jit(solution)/shard_map/all_to_all | solution.py:777
  78.1 0.0 copy-done.3
  78.1 0.0 copy-done.6
  78.1 1.2 %shard_map.183 = (f32[1,512]{1,0:T(1,128)}, f32[64,1024]{1,0:T(8,128)}) custom-call(f32[32,16,128]{2,1,0:T(8,128)S(1)} %all_to_all.34.arrived, f32[32,4,128]{2,1,0:T(4,128)S(1)} %all-to-all-done.4.measured, f32[4,4,128]{2,1,0:T(4,128)S(1)} %get-tuple-element.33.carry, f32[2,5,4,128]{3,2,1,0:T(4,128)S(1)} %copy-done.4, bf16[2,64,256]{2,1,0:T(8,128)(2,1)S(1)} %copy-done.6, ...), custom_call_target="tpu_custom_call" | custom-call | tf_op jit(solution)/shard_map/pallas_call | solution.py:766
  (1 shorter events, 0.0 us)
Async XLA Ops:
  0.6 28.3 %copy-start.4 = (f32[2,5,4,128]{3,2,1,0:T(4,128)S(1)}, f32[2,5,4,128]{3,2,1,0:T(4,128)}, u32[]{:S(2)}) copy-start(f32[2,5,4,128]{3,2,1,0:T(4,128)} %constant.18.clone.turns) | copy-start | bytes 61444
  0.6 28.3 %copy-start.5 = (bf16[2,128,128]{2,1,0:T(8,128)(2,1)S(1)}, bf16[2,128,128]{2,1,0:T(8,128)(2,1)}, u32[]{:S(2)}) copy-start(bf16[2,128,128]{2,1,0:T(8,128)(2,1)} %constant.19.clone.packed) | copy-start | bytes 196612
  0.7 28.3 %copy-start.2 = (bf16[2,256,256]{2,1,0:T(8,128)(2,1)S(1)}, bf16[2,256,256]{2,1,0:T(8,128)(2,1)}, u32[]{:S(2)}) copy-start(bf16[2,256,256]{2,1,0:T(8,128)(2,1)} %constant.20.clone.plain) | copy-start | bytes 786436
  0.7 28.3 %copy-start = (f32[1,1,9,256,512]{4,3,2,1,0:T(8,128)S(1)}, f32[1,1,9,256,512]{4,3,2,1,0:T(8,128)}, u32[]{:S(2)}) copy-start(f32[1,1,9,256,512]{4,3,2,1,0:T(8,128)} %source.5) | copy-start | bytes 14155780
  28.9 29.4 %copy-start.1 = (bf16[2048,256]{1,0:T(8,128)(2,1)S(1)}, bf16[2048,256]{1,0:T(8,128)(2,1)}, u32[]{:S(2)}) copy-start(bf16[2048,256]{1,0:T(8,128)(2,1)} %constant.21.clone.tables) | copy-start | bytes 3145732
  43.5 34.6 %copy-start.3 = (bf16[2,128,256]{2,1,0:T(8,128)(2,1)S(1)}, bf16[2,128,256]{2,1,0:T(8,128)(2,1)}, u32[]{:S(2)}) copy-start(bf16[2,128,256]{2,1,0:T(8,128)(2,1)} %constant.23.clone.plain) | copy-start | bytes 393220
  43.5 34.6 %copy-start.6 = (bf16[2,64,256]{2,1,0:T(8,128)(2,1)S(1)}, bf16[2,64,256]{2,1,0:T(8,128)(2,1)}, u32[]{:S(2)}) copy-start(bf16[2,64,256]{2,1,0:T(8,128)(2,1)} %constant.22.clone.packed) | copy-start | bytes 196612
  55.8 10.1 %all-to-all-start.4 = ((f32[32,4,128]{2,1,0:T(4,128)}), f32[32,4,128]{2,1,0:T(4,128)S(1)}, u32[]{:S(2)}, u32[]{:S(2)}) async-start(f32[32,4,128]{2,1,0:T(4,128)} %get-tuple-element.29), calls=%async_computation.4 | async-start | bytes 131072 | tf_op jit(solution)/shard_map/all_to_all | solution.py:777
